TPU v7x, 32 devices: a whole 2x2x4 slice. The times are simulated.
32 devices in a mesh: dp: 8 (over z, x), mp: 4 (over y, core).
Axes of the slice: x: 2, y: 2, z: 4, core: 2. Of those that a mesh axis runs over, the one named last changes fastest.
Arguments:
- hidden: bfloat16 [1024, 12288], P('dp', 'mp'), may hold values from -6 to 6
- w_out: bfloat16 [6144, 12288], P('dp', 'mp'), may hold values from -0.0546875 to 0.0546875
- direction: bfloat16 [6144, 12288], P('dp', 'mp'), may hold values from -6 to 6
- targets: bfloat16 [1024, 6144], P('mp', 'dp'), may hold values from -6 to 6
- codes: int32 [4], replicated, may hold values from 0 to 3
- code_weights: float32 [4], replicated, may hold values from 0.5 to 2
Outputs:
- inverse_product: float32 [6144, 12288], P('dp', 'mp')
All inputs are finite; a program needn't handle non-finite values.
Results may differ from a plain program's by a relative error of at most 0.006.
Values may be sent and summed in bfloat16 or wider, within the bound.
No kernel may reach another device: no remote copies, remote signals or barrier semaphores. Data moves between devices by JAX's collectives and lax.ppermute only.
A program may use at most 128 MiB of HBM per device.

v0:
```python
import jax
import jax.numpy as jnp
from jax import lax
from jax.sharding import PartitionSpec as P

GRID = 16
PATCHES = 256


STEP = 0.5


def contract_rows(left, right):
    return lax.dot_general(
        left, right, (((0,), (0,)), ((), ())), preferred_element_type=jnp.float32
    )


def weigh_rows(sums, targets, codes, code_weights, first_row):
    row_count = targets.shape[0]
    width = targets.shape[1]
    image_count = row_count // PATCHES
    image_codes = lax.dynamic_slice_in_dim(codes, first_row // PATCHES, image_count, 0)
    patch_grid = targets.reshape(image_count, GRID, GRID, width)
    horizontal = (image_codes % 2 == 1)[:, None, None, None]
    vertical = (image_codes // 2 == 1)[:, None, None, None]
    patch_grid = jnp.where(horizontal, patch_grid[:, :, ::-1], patch_grid)
    patch_grid = jnp.where(vertical, patch_grid[:, ::-1], patch_grid)
    aligned = patch_grid.reshape(row_count, width).astype(jnp.float32)
    outputs = sums[:, :width]
    moved = sums[:, width:]
    slope = 1.0 - jnp.tanh(outputs - aligned) ** 2
    image_weight = jnp.sum(
        jnp.where(
            image_codes[:, None] == jnp.arange(code_weights.shape[0], dtype=jnp.int32)[None, :],
            code_weights[None, :],
            0.0,
        ),
        axis=1,
    )
    product = (slope * moved).reshape(image_count, PATCHES, width) * image_weight[:, None, None]
    return product.reshape(row_count, width).astype(jnp.bfloat16)


def project_rows(rows_here, stacked):
    return lax.dot_general(
        rows_here, stacked, (((1,), (1,)), ((), ())), preferred_element_type=jnp.float32
    )


def on_device(hidden, w_out, direction, targets, codes, code_weights):
    stacked = jnp.concatenate([w_out, direction], axis=0)
    whole = lax.all_gather(hidden, "dp", axis=0, tiled=True)
    tokens_all = whole.shape[0]
    rows_here = whole
    sums = lax.psum_scatter(
        project_rows(rows_here, stacked).astype(jnp.bfloat16), "mp", scatter_dimension=0, tiled=True
    ).astype(jnp.float32)
    first_row = lax.axis_index("mp") * targets.shape[0]
    scaled = weigh_rows(sums, targets, codes, code_weights, first_row)
    rows_here = whole
    curvature = contract_rows(lax.all_gather(scaled, "mp", axis=0, tiled=True), rows_here)
    return 2.0 * direction.astype(jnp.float32) - STEP * (curvature / tokens_all)


def solution(mesh):
    return jax.shard_map(
        on_device,
        mesh=mesh,
        in_specs=(P("dp", "mp"), P("dp", "mp"), P("dp", "mp"), P("mp", "dp"), P(), P()),
        out_specs=P("dp", "mp"),
        check_vma=False,
    )
```

profile of v0, /device:TPU:0, one launch (start us, length us, event | category | flops | bytes accessed | tf_op | source)
XLA Modules:
  0.0 203.4 jit_solution(5141698554499488278)
XLA Ops:
  6.5 0.0 all-gather.3.cloned.1.call-start
  6.5 0.7 all-gather.3.cloned.1.call-update
  7.3 0.0 copy-start.1
  7.3 0.0 copy-start
  7.3 0.0 reduce-scatter.2.cloned.1.call-start
  7.3 104.0 %all-gather.3.cloned.1.call-done = bf16[1024,3072]{1,0:T(8,128)(2,1)} async-done(((bf16[128,3072]{1,0:T(8,128)(2,1)}), bf16[1024,3072]{1,0:T(8,128)(2,1)}) %all-gather.3.cloned.1.call-update) | async-done | bytes 6291472 | tf_op jit(solution)/shard_map/all_gather | solution.py:53
  111.3 16.0 %fusion.7 = bf16[1024,1536]{0,1:T(8,128)(2,1)} fusion(bf16[1024,3072]{1,0:T(8,128)(2,1)} %all-gather.3.cloned.1.call-done, bf16[768,3072]{1,0:T(8,128)(2,1)} %param.8, bf16[768,3072]{1,0:T(8,128)(2,1)} %param.7), kind=kOutput, calls=%fused_computation.6 | convolution fusion | flops 9684123648 | bytes 18874368 | tf_op jit(solution)/shard_map/dot_general | solution.py:46
  127.3 0.0 copy-start.2
  127.3 0.0 reduce-scatter.2.cloned.1.call-update
  127.3 0.0 all-gather.5.cloned.1.call-start
  127.4 0.0 copy-done.1
  127.4 0.7 dynamic_slice.3
  130.8 0.0 copy-done
  130.8 0.3 rev.6
  131.2 0.1 reverse_select_fusion
  131.3 0.1 bitcast_convert_fusion
  131.4 0.3 copy.9
  131.7 0.0 copy-done.2
  131.7 1.2 fusion.15
  132.9 30.7 %reduce-scatter.2.cloned.1.call-done = bf16[256,1536]{0,1:T(8,128)(2,1)} async-done(((bf16[1024,1536]{0,1:T(8,128)(2,1)}), bf16[256,1536]{0,1:T(8,128)(2,1)}) %reduce-scatter.2.cloned.1.call-update) | async-done | bytes 786448 | tf_op jit(solution)/shard_map/reduce_scatter | solution.py:56
  163.6 1.2 convert_element_type.24
  164.9 1.5 fusion.11
  166.4 0.0 all-gather.5.cloned.1.call-update
  166.4 20.0 %all-gather.5.cloned.1.call-done = bf16[1024,768]{0,1:T(8,128)(2,1)} async-done(((bf16[256,768]{0,1:T(8,128)(2,1)}), bf16[1024,768]{0,1:T(8,128)(2,1)}) %all-gather.5.cloned.1.call-update) | async-done | bytes 1572880 | tf_op jit(solution)/shard_map/all_gather | solution.py:62
  186.4 10.5 %multiply_subtract_fusion = f32[768,3072]{1,0:T(8,128)} fusion(bf16[768,3072]{1,0:T(8,128)(2,1)} %param.8, bf16[1024,768]{0,1:T(8,128)(2,1)} %all-gather.5.cloned.1.call-done, bf16[1024,3072]{1,0:T(8,128)(2,1)} %all-gather.3.cloned.1.call-done), kind=kOutput, calls=%fused_computation.4 | convolution fusion | flops 4841275392 | bytes 22020096 | tf_op jit(solution)/shard_map/dot_general | solution.py:14
  (1 shorter events, 0.0 us)
Async XLA Ops:
  6.5 104.8 %all-gather.3.cloned.1.call-start = ((), (), s32[]{:S(2)}) async-start(), calls=%async_computation.1 | async-start | bytes 7077888 | tf_op jit(solution)/shard_map/all_gather | solution.py:53
  7.3 120.2 %copy-start.1 = (s32[4]{0:T(128)S(1)}, s32[4]{0:T(128)}, u32[]{:S(2)}) copy-start(s32[4]{0:T(128)} %param.10) | copy-start | bytes 52
  7.3 123.6 %copy-start = (bf16[256,768]{1,0:T(8,128)(2,1)S(1)}, bf16[256,768]{1,0:T(8,128)(2,1)}, u32[]{:S(2)}) copy-start(bf16[256,768]{1,0:T(8,128)(2,1)} %param.9) | copy-start | bytes 1179652
  7.3 156.3 %reduce-scatter.2.cloned.1.call-start = ((), (), s32[]{:S(2)}) async-start(), calls=%async_computation.2 | async-start | bytes 3932160 | tf_op jit(solution)/shard_map/reduce_scatter | solution.py:56
  127.3 4.3 %copy-start.2 = (f32[4]{0:T(128)S(1)}, f32[4]{0:T(128)}, u32[]{:S(2)}) copy-start(f32[4]{0:T(128)} %param.11) | copy-start | bytes 52
  127.3 59.0 %all-gather.5.cloned.1.call-start = ((), (), s32[]{:S(2)}) async-start(), calls=%async_computation.3 | async-start | bytes 1966080 | tf_op jit(solution)/shard_map/all_gather | solution.py:62
Sparse Core Ops, SparseCore 0:
  9.5 101.7 all-gather.2
  127.5 36.0 reduce-scatter.1
  166.5 19.8 all-gather.4
where the time goes:
time: 204 us; the launch traced here: 203 us
  waiting for transfers between devices  155 us (76%)
  matrix products  26.5 us (13%)
  between operations  16 us (8%)
  other arithmetic  4.17 us (2%)
    all_gather x1, waiting for transfers between devices, on_device(): whole = lax.all_gather(hidden, 'dp', axis=0, tiled=True)  104 us
    reduce_scatter x1, waiting for transfers between devices, on_device(): lax.psum_scatter(project_rows(rows_here, stacked).astype(jnp.bfloat16), '...  30.7 us
    all_gather x1, waiting for transfers between devices, on_device(): lax.all_gather(scaled, 'mp', axis=0, tiled=True)  20 us
    dot_general x1, matrix products, project_rows(): lax.dot_general(rows_here, stacked, (((1,), (1,)), ((), ())), preferred_e...  16 us
    dot_general x1, matrix products, contract_rows(): lax.dot_general(left, right, (((0,), (0,)), ((), ())), preferred_element_...  10.5 us
  transfers between devices with their start and end apart: 3, of which 3 were waited for; matrix products, arithmetic and copies ran while one was open for 1% of the time, Pallas kernels for 0%

commit v1 on v0

--- a/solution.py
+++ b/solution.py
@@ -48,24 +48,114 @@
     )
 
 
-def on_device(hidden, w_out, direction, targets, codes, code_weights):
+def on_device_any(hidden, w_out, direction, targets, codes, code_weights):
     stacked = jnp.concatenate([w_out, direction], axis=0)
     whole = lax.all_gather(hidden, "dp", axis=0, tiled=True)
-    tokens_all = whole.shape[0]
-    rows_here = whole
     sums = lax.psum_scatter(
-        project_rows(rows_here, stacked).astype(jnp.bfloat16), "mp", scatter_dimension=0, tiled=True
+        project_rows(whole, stacked).astype(jnp.bfloat16), "mp", scatter_dimension=0, tiled=True
     ).astype(jnp.float32)
     first_row = lax.axis_index("mp") * targets.shape[0]
     scaled = weigh_rows(sums, targets, codes, code_weights, first_row)
-    rows_here = whole
-    curvature = contract_rows(lax.all_gather(scaled, "mp", axis=0, tiled=True), rows_here)
+    curvature = contract_rows(lax.all_gather(scaled, "mp", axis=0, tiled=True), whole)
+    return 2.0 * direction.astype(jnp.float32) - STEP * (curvature / whole.shape[0])
+
+
+RING = (0, 2, 4, 6, 7, 5, 3, 1)
+COUNT = len(RING)
+UP = [(RING[i], RING[(i + 1) % COUNT]) for i in range(COUNT)]
+DOWN = [(RING[i], RING[(i - 1) % COUNT]) for i in range(COUNT)]
+CORE = [(i, i ^ 1) for i in range(4)]
+ROW = [(i, i ^ 2) for i in range(4)]
+
+
+def order_of(dp):
+    at = RING.index(dp)
+    seq = [(0, 0), (0, 1)]
+    for k in range(1, COUNT // 2):
+        seq += [(-k, 0), (k, 0), (-k, 1), (k, 1)]
+    seq += [(COUNT // 2, 0), (COUNT // 2, 1)]
+    return [2 * RING[(at + k) % COUNT] + h for k, h in seq]
+
+
+ORDER = [order_of(d) for d in range(COUNT)]
+
+
+def on_device(hidden, w_out, direction, targets, codes, code_weights):
+    dp = lax.axis_index("dp")
+    mp = lax.axis_index("mp")
+    core = mp % 2
+    rows, width = hidden.shape[0], w_out.shape[0]
+    half, part = rows // 2, width // 2
+    tokens_all = rows * COUNT
+
+    def swap(value, pairs):
+        return lax.ppermute(value, "mp", pairs)
+
+    up, down = [(hidden[:half], hidden[half:])], [(hidden[:half], hidden[half:])]
+    for k in range(1, COUNT // 2):
+        up.append(tuple(lax.ppermute(v, "dp", UP) for v in up[-1]))
+        down.append(tuple(lax.ppermute(v, "dp", DOWN) for v in down[-1]))
+    last = (lax.ppermute(up[-1][0], "dp", UP), lax.ppermute(down[-1][1], "dp", DOWN))
+
+    def cols(value, which):
+        return lax.dynamic_slice_in_dim(value, which * part, part, 1)
+
+    two = jnp.concatenate([cols(targets, core), swap(cols(targets, 1 - core), CORE)], axis=0)
+    four = jnp.concatenate([two, swap(two, ROW)], axis=0)
+    base = jnp.asarray(ORDER, jnp.int32)[dp] * half
+    token = (base[:, None] + jnp.arange(half, dtype=jnp.int32)[None, :]).reshape(1, tokens_all)
+    image, patch = token // PATCHES, token % PATCHES
+
+    def look_up(table, index):
+        at = jnp.arange(table.shape[0], dtype=jnp.int32)[:, None]
+        return jnp.sum(jnp.where(index == at, table[:, None], 0), axis=0, keepdims=True)
+
+    code = look_up(codes, image)
+    weight = look_up(code_weights, code)
+    row, col = patch // GRID, patch % GRID
+    col = jnp.where(code % 2 == 1, GRID - 1 - col, col)
+    row = jnp.where(code // 2 == 1, GRID - 1 - row, row)
+    source = (image ^ mp) * PATCHES + row * GRID + col
+    one_hot = (jnp.arange(tokens_all, dtype=jnp.int32)[:, None] == source).astype(jnp.bfloat16)
+    aligned = contract_rows(four, one_hot)
+
+    def pair_rows(which):
+        return jnp.concatenate(
+            [lax.dynamic_slice_in_dim(w_out, which * part, part, 0),
+             lax.dynamic_slice_in_dim(direction, which * part, part, 0)], axis=0)
+
+    stack_mine, stack_theirs = pair_rows(core), pair_rows(1 - core)
+
+    def round_of(block, start):
+        theirs = swap(project_rows(stack_theirs, block).astype(jnp.bfloat16), CORE)
+        kept = project_rows(stack_mine, block).astype(jnp.bfloat16).astype(jnp.float32)
+        chip = kept + theirs.astype(jnp.float32)
+        sums = chip + swap(chip.astype(jnp.bfloat16), ROW).astype(jnp.float32)
+        at = slice(start, start + block.shape[0])
+        slope = 1.0 - jnp.tanh(sums[:part] - aligned[:, at]) ** 2
+        mine = (weight[:, at] * slope * sums[part:]).astype(jnp.bfloat16)
+        theirs = swap(mine, CORE)
+        low, high = lax.select(core == 0, mine, theirs), lax.select(core == 0, theirs, mine)
+        return jnp.concatenate([low, high], axis=0)
+
+    blocks = [hidden]
+    for k in range(1, COUNT // 2):
+        blocks.append(jnp.concatenate([up[k][0], down[k][0], up[k][1], down[k][1]], axis=0))
+    blocks.append(jnp.concatenate(last, axis=0))
+    start, scaled = 0, []
+    for block in blocks:
+        scaled.append(round_of(block, start))
+        start += block.shape[0]
+    curvature = jnp.dot(
+        jnp.concatenate(scaled, axis=1), jnp.concatenate(blocks, axis=0), preferred_element_type=jnp.float32
+    )
     return 2.0 * direction.astype(jnp.float32) - STEP * (curvature / tokens_all)
 
 
 def solution(mesh):
+    planned = mesh.shape["dp"] == COUNT and mesh.shape["mp"] == 4
     return jax.shard_map(
-        on_device,
+        on_device if planned else on_device_any,
         mesh=mesh,
         in_specs=(P("dp", "mp"), P("dp", "mp"), P("dp", "mp"), P("mp", "dp"), P(), P()),
         out_specs=P("dp", "mp"),

time: 204 us -> 131 us (0.64)
  waiting for transfers between devices: 155 us -> 59.6 us
  starting transfers between devices: 0.08 us -> 24 us
  between operations: 16 us -> 0.58 us
  local copies, waits for them, and re-layouts: 1.26 us -> 15.8 us
    all_gather x2 -> x0, waiting for transfers between devices: 124 us -> none  [the longest x1 104 us: on_device(): whole = lax.all_gather(hidden, 'dp', axis=0, tiled=True)]
    ppermute x0 -> x31, waiting for transfers between devices: none -> 59.6 us  [the longest x6 37.1 us: on_device(): up.append(tuple((lax.ppermute(v, 'dp', UP) for v in up[-1])))]
    reduce_scatter x1 -> x0, waiting for transfers between devices: 30.7 us -> none  [on_device(): lax.psum_scatter(project_rows(rows_here, stacked).astype(jnp.bfloat16), '...]
    ppermute x0 -> x31, starting transfers between devices: none -> 24 us  [the longest x6 11.3 us: on_device(): down.append(tuple((lax.ppermute(v, 'dp', DOWN) for v in down[-1])))]
    dot_general x1, matrix products: 10.5 us -> 1.99 us  [contract_rows(): lax.dot_general(left, right, (((0,), (0,)), ((), ())), preferred_element_...]
    dot_general x0 -> x1, matrix products: none -> 7.51 us  [on_device(): jnp.dot(jnp.concatenate(scaled, axis=1), jnp.concatenate(blocks, axis=0),...]
    dynamic_slice x1 -> x2, local copies, waits for them, and re-layouts: 0.65 us -> 8.04 us  [the longest x1 6.3 us: pair_rows(): lax.dynamic_slice_in_dim(direction, which * part, part, 0)]
    unnamed x6 -> x40, local copies, waits for them, and re-layouts: 0.01 us -> 4.91 us
  transfers between devices with their start and end apart: 3 -> 31, of which waited for: 3 -> 9; matrix products, arithmetic and copies ran while one was open for 1% -> 28% of each run, Pallas kernels for 0% -> 0%
where the time goes in v1:
time: 131 us; the launch traced here: 130 us
  waiting for transfers between devices  59.6 us (45%)
  matrix products  26.2 us (20%)
  starting transfers between devices  24 us (18%)
  local copies, waits for them, and re-layouts  15.8 us (12%)
  other arithmetic  4.03 us (3%)
    ppermute x6, waiting for transfers between devices, on_device(): up.append(tuple((lax.ppermute(v, 'dp', UP) for v in up[-1])))  37.1 us
    dot_general x10, matrix products, project_rows(): lax.dot_general(rows_here, stacked, (((1,), (1,)), ((), ())), preferred_e...  16.7 us
    ppermute x17, waiting for transfers between devices, swap(): return lax.ppermute(value, 'mp', pairs)  13.4 us
    ppermute x6, starting transfers between devices, on_device(): down.append(tuple((lax.ppermute(v, 'dp', DOWN) for v in down[-1])))  11.3 us
    ppermute x17, starting transfers between devices, swap(): return lax.ppermute(value, 'mp', pairs)  8.29 us
    dot_general x1, matrix products, on_device(): jnp.dot(jnp.concatenate(scaled, axis=1), jnp.concatenate(blocks, axis=0),...  7.51 us
    ppermute x1, waiting for transfers between devices, on_device(): lax.ppermute(up[-1][0], 'dp', UP)  7.35 us
    dynamic_slice x1, local copies, waits for them, and re-layouts, pair_rows(): lax.dynamic_slice_in_dim(direction, which * part, part, 0)  6.3 us
  transfers between devices with their start and end apart: 31, of which 9 were waited for; matrix products, arithmetic and copies ran while one was open for 28% of the time, Pallas kernels for 0%

profile of v1, /device:TPU:0, one launch (start us, length us, event | category | flops | bytes accessed | tf_op | source)
XLA Modules:
  0.0 130.3 jit_solution(16531924019708003053)
XLA Ops:
  0.0 2.1 %fusion.58 = (bf16[64,3072]{1,0:T(8,128)(2,1)}, bf16[64,3072]{1,0:T(8,128)(2,1)}) fusion(bf16[128,3072]{1,0:T(8,128)(2,1)} %param.7), kind=kLoop, calls=%fused_computation.167 | loop fusion | bytes 1572864 | tf_op jit(solution)/shard_map/slice | solution.py:94
  2.1 2.9 %collective-permute-start.8 = (bf16[64,3072]{1,0:T(8,128)(2,1)}, bf16[64,3072]{1,0:T(8,128)(2,1)}, u32[]{:S(2)}, u32[]{:S(2)}) collective-permute-start(bf16[64,3072]{1,0:T(8,128)(2,1)} %get-tuple-element.14), channel_id=1, source_target_pairs={{0,4},{8,0},{16,8},{24,16},{28,24},{20,28},{12,20},{4,12},{1,5},{9... | collective-permute-start | bytes 1179656 | tf_op jit(solution)/shard_map/ppermute | solution.py:97
  5.1 1.7 %constant_dynamic-slice_fusion = (bf16[256,384]{1,0:T(8,128)(2,1)S(1)}, bf16[256,384]{1,0:T(8,128)(2,1)}) fusion(bf16[256,768]{1,0:T(8,128)(2,1)} %param.10, s32[]{:T(128)S(6)} %select_n.152, s32[]{:T(128)S(6)} %select_n.153), kind=kLoop, calls=%fused_computation.155 | loop fusion | bytes 786440 | tf_op jit(solution)/shard_map/dynamic_slice | solution.py:101
  6.9 1.9 %collective-permute-start.6 = (bf16[64,3072]{1,0:T(8,128)(2,1)}, bf16[64,3072]{1,0:T(8,128)(2,1)}, u32[]{:S(2)}, u32[]{:S(2)}) collective-permute-start(bf16[64,3072]{1,0:T(8,128)(2,1)} %get-tuple-element.15), channel_id=1, source_target_pairs={{0,4},{8,0},{16,8},{24,16},{28,24},{20,28},{12,20},{4,12},{1,5},{9... | collective-permute-start | bytes 1179656 | tf_op jit(solution)/shard_map/ppermute | solution.py:97
  8.8 6.3 %constant_dynamic-slice_fusion.1 = (bf16[384,3072]{1,0:T(8,128)(2,1)S(1)}, bf16[384,3072]{1,0:T(8,128)(2,1)S(1)}, bf16[384,3072]{1,0:T(8,128)(2,1)}, bf16[384,3072]{1,0:T(8,128)(2,1)S(1)}) fusion(bf16[768,3072]{1,0:T(8,128)(2,1)} %param.9, s32[]{:T(128)S(6)} %select_n.153, s32[]{:T(128)S(6)} %select_n.152, bf16[768,3072]{1,0:T(8,128)(2,1)} %param.8), kind=kLoop, calls=%fused_computation.156 | loop fusion | bytes 18874376 | tf_op jit(solution)/shard_map/dynamic_slice | solution.py:125
  15.1 2.2 %convolution_convert_fusion.8 = bf16[768,128]{1,0:T(8,128)(2,1)} fusion(bf16[128,3072]{1,0:T(8,128)(2,1)S(1)} %copy-done, bf16[384,3072]{1,0:T(8,128)(2,1)S(1)} %get-tuple-element.7, bf16[384,3072]{1,0:T(8,128)(2,1)S(1)} %get-tuple-element.72), kind=kOutput, calls=%fused_computation.22 | convolution fusion | flops 613515264 | bytes 5701632 | tf_op jit(solution)/shard_map/dot_general | solution.py:46
  17.6 0.9 constant_dynamic-update-slice_fusion.28
  18.5 0.7 fusion.56
  19.5 0.7 select_reduce_fusion
  20.2 0.6 slice_bitcast_fusion
  21.3 1.1 pad_maximum_fusion.2
  22.4 1.7 %collective-permute-start.3 = (bf16[512,384]{1,0:T(8,128)(2,1)S(1)}, bf16[512,384]{1,0:T(8,128)(2,1)S(1)}, u32[]{:S(2)}, u32[]{:S(2)}) collective-permute-start(bf16[512,384]{1,0:T(8,128)(2,1)S(1)} %pad_maximum_fusion.2), channel_id=1, source_target_pairs={{0,2},{1,3},{2,0},{3,1},{4,6},{5,7},{6,4},{7,5},{8,10},{9,11},{10,... | collective-permute-start | bytes 1179656 | tf_op jit(solution)/shard_map/ppermute | solution.py:92
  24.1 3.2 %fusion.31 = (bf16[768,128]{1,0:T(8,128)(2,1)S(1)}, f32[768,128]{1,0:T(8,128)S(1)}) fusion(bf16[768,128]{1,0:T(8,128)(2,1)S(1)} %collective-permute-done, bf16[128,3072]{1,0:T(8,128)(2,1)S(1)} %copy-done, bf16[384,3072]{1,0:T(8,128)(2,1)S(1)} %get-tuple-element.8, bf16[384,3072]{1,0:T(8,128)(2,1)} %get-tuple-element.71), kind=kOutput, calls=%fused_computation.61 | convolution fusion | flops 613908480 | bytes 6291456 | tf_op jit(solution)/shard_map/dot_general | solution.py:46
  27.3 5.0 %collective-permute-done.5 = bf16[64,3072]{1,0:T(8,128)(2,1)S(1)} collective-permute-done((bf16[64,3072]{1,0:T(8,128)(2,1)}, bf16[64,3072]{1,0:T(8,128)(2,1)S(1)}, u32[]{:S(2)}, u32[]{:S(2)}) %collective-permute-start.5) | collective-permute-done | bytes 393248 | tf_op jit(solution)/shard_map/ppermute | solution.py:96
  32.3 1.5 %collective-permute-start.1 = (bf16[768,128]{1,0:T(8,128)(2,1)S(1)}, bf16[768,128]{1,0:T(8,128)(2,1)S(1)}, u32[]{:S(2)}, u32[]{:S(2)}) collective-permute-start(bf16[768,128]{1,0:T(8,128)(2,1)S(1)} %get-tuple-element.63), channel_id=1, source_target_pairs={{0,2},{1,3},{2,0},{3,1},{4,6},{5,7},{6,4},{7,5},{8,10},{9,11},{10,... | collective-permute-start | bytes 589832 | tf_op jit(solution)/shard_map/ppermute | solution.py:92
  33.9 1.1 constant_dynamic-update-slice_fusion.26
  35.0 1.1 constant_dynamic-update-slice_fusion.25
  36.1 1.1 constant_dynamic-update-slice_fusion.24
  37.2 1.4 %convolution_convert_fusion.4 = bf16[768,256]{1,0:T(8,128)(2,1)S(1)} fusion(bf16[256,3072]{1,0:T(8,128)(2,1)S(1)} %get-tuple-element.37, bf16[384,3072]{1,0:T(8,128)(2,1)S(1)} %copy-done.3, bf16[384,3072]{1,0:T(8,128)(2,1)S(1)} %copy-done.5), kind=kOutput, calls=%fused_computation.14 | convolution fusion | flops 1217593344 | bytes 6684672 | tf_op jit(solution)/shard_map/dot_general | solution.py:46
  38.7 1.6 %collective-permute-start.15 = (bf16[64,3072]{1,0:T(8,128)(2,1)}, bf16[64,3072]{1,0:T(8,128)(2,1)S(1)}, u32[]{:S(2)}, u32[]{:S(2)}) collective-permute-start(bf16[64,3072]{1,0:T(8,128)(2,1)} %collective-permute-done.8), channel_id=1, source_target_pairs={{0,4},{8,0},{16,8},{24,16},{28,24},{20,28},{12,20},{4,12},{1,5},{9... | collective-permute-start | bytes 1179656 | tf_op jit(solution)/shard_map/ppermute | solution.py:97
  40.8 0.5 collective-permute-start.12
  41.4 1.5 %collective-permute-start.13 = (bf16[64,3072]{1,0:T(8,128)(2,1)}, bf16[64,3072]{1,0:T(8,128)(2,1)S(1)}, u32[]{:S(2)}, u32[]{:S(2)}) collective-permute-start(bf16[64,3072]{1,0:T(8,128)(2,1)} %collective-permute-done.6), channel_id=1, source_target_pairs={{0,4},{8,0},{16,8},{24,16},{28,24},{20,28},{12,20},{4,12},{1,5},{9... | collective-permute-start | bytes 1179656 | tf_op jit(solution)/shard_map/ppermute | solution.py:97
  43.0 2.0 %fusion = f32[384,1024]{1,0:T(8,128)S(1)} fusion(s32[1024]{0:T(1024)S(1)} %fusion.45, bf16[512,384]{1,0:T(8,128)(2,1)S(1)} %collective-permute-done.3, bf16[256,384]{1,0:T(8,128)(2,1)} %collective-permute-done.2, bf16[256,384]{1,0:T(8,128)(2,1)S(1)} %get-tuple-element.50), kind=kOutput, calls=%fused_computation.4 | convolution fusion | flops 808714240 | bytes 2363392 | tf_op jit(solution)/shard_map/dot_general | solution.py:14
  45.0 15.2 %collective-permute-done.12 = bf16[64,3072]{1,0:T(8,128)(2,1)S(1)} collective-permute-done((bf16[64,3072]{1,0:T(8,128)(2,1)S(1)}, bf16[64,3072]{1,0:T(8,128)(2,1)S(1)}, u32[]{:S(2)}, u32[]{:S(2)}) %collective-permute-start.12) | collective-permute-done | bytes 393248 | tf_op jit(solution)/shard_map/ppermute | solution.py:96
  60.5 1.4 %convolution_convert_fusion.2 = bf16[768,256]{1,0:T(8,128)(2,1)S(1)} fusion(bf16[256,3072]{1,0:T(8,128)(2,1)S(1)} %get-tuple-element.29, bf16[384,3072]{1,0:T(8,128)(2,1)S(1)} %copy-done.3, bf16[384,3072]{1,0:T(8,128)(2,1)S(1)} %copy-done.5), kind=kOutput, calls=%fused_computation.10 | convolution fusion | flops 1217593344 | bytes 6684672 | tf_op jit(solution)/shard_map/dot_general | solution.py:46
  62.0 1.6 %collective-permute-start.20 = (bf16[64,3072]{1,0:T(8,128)(2,1)S(1)}, bf16[64,3072]{1,0:T(8,128)(2,1)S(1)}, u32[]{:S(2)}, u32[]{:S(2)}) collective-permute-start(bf16[64,3072]{1,0:T(8,128)(2,1)S(1)} %collective-permute-done.13), channel_id=1, source_target_pairs={{0,4},{8,0},{16,8},{24,16},{28,24},{20,28},{12,20},{4,12},{1,5},{9... | collective-permute-start | bytes 1179656 | tf_op jit(solution)/shard_map/ppermute | solution.py:97
  64.1 1.4 %fusion.63 = (bf16[768,256]{1,0:T(8,128)(2,1)S(1)}, f32[768,256]{1,0:T(8,128)S(1)}) fusion(bf16[768,256]{1,0:T(8,128)(2,1)S(1)} %collective-permute-done.9, bf16[256,3072]{1,0:T(8,128)(2,1)S(1)} %get-tuple-element.37, bf16[384,3072]{1,0:T(8,128)(2,1)S(1)} %get-tuple-element.8, bf16[384,3072]{1,0:T(8,128)(2,1)S(1)} %copy-done.1), kind=kOutput, calls=%fused_computation.172 | convolution fusion | flops 1218379776 | bytes 7864320 | tf_op jit(solution)/shard_map/dot_general | solution.py:46
  65.6 0.6 collective-permute-start.10
  66.1 1.6 %collective-permute-start.22 = (bf16[64,3072]{1,0:T(8,128)(2,1)S(1)}, bf16[64,3072]{1,0:T(8,128)(2,1)S(1)}, u32[]{:S(2)}, u32[]{:S(2)}) collective-permute-start(bf16[64,3072]{1,0:T(8,128)(2,1)S(1)} %collective-permute-done.15), channel_id=1, source_target_pairs={{0,4},{8,0},{16,8},{24,16},{28,24},{20,28},{12,20},{4,12},{1,5},{9... | collective-permute-start | bytes 1179656 | tf_op jit(solution)/shard_map/ppermute | solution.py:97
  67.7 7.2 %collective-permute-done.19 = bf16[64,3072]{1,0:T(8,128)(2,1)S(1)} collective-permute-done((bf16[64,3072]{1,0:T(8,128)(2,1)S(1)}, bf16[64,3072]{1,0:T(8,128)(2,1)S(1)}, u32[]{:S(2)}, u32[]{:S(2)}) %collective-permute-start.19) | collective-permute-done | bytes 393248 | tf_op jit(solution)/shard_map/ppermute | solution.py:96
  74.9 0.5 collective-permute-start.21
  75.5 9.7 %collective-permute-done.21 = bf16[64,3072]{1,0:T(8,128)(2,1)S(1)} collective-permute-done((bf16[64,3072]{1,0:T(8,128)(2,1)S(1)}, bf16[64,3072]{1,0:T(8,128)(2,1)S(1)}, u32[]{:S(2)}, u32[]{:S(2)}) %collective-permute-start.21) | collective-permute-done | bytes 393248 | tf_op jit(solution)/shard_map/ppermute | solution.py:96
  85.4 1.4 %convolution_convert_fusion = bf16[768,256]{1,0:T(8,128)(2,1)S(1)} fusion(bf16[256,3072]{1,0:T(8,128)(2,1)S(1)} %get-tuple-element.21, bf16[384,3072]{1,0:T(8,128)(2,1)S(1)} %copy-done.3, bf16[384,3072]{1,0:T(8,128)(2,1)S(1)} %copy-done.5), kind=kOutput, calls=%fused_computation.6 | convolution fusion | flops 1217593344 | bytes 6684672 | tf_op jit(solution)/shard_map/dot_general | solution.py:46
  86.9 0.5 collective-permute-start.26
  87.4 1.4 %fusion.62 = (bf16[768,256]{1,0:T(8,128)(2,1)S(1)}, f32[768,256]{1,0:T(8,128)S(1)}) fusion(bf16[768,256]{1,0:T(8,128)(2,1)S(1)} %collective-permute-done.16, bf16[256,3072]{1,0:T(8,128)(2,1)S(1)} %get-tuple-element.29, bf16[384,3072]{1,0:T(8,128)(2,1)S(1)} %get-tuple-element.8, bf16[384,3072]{1,0:T(8,128)(2,1)S(1)} %copy-done.1), kind=kOutput, calls=%fused_computation.171 | convolution fusion | flops 1218379776 | bytes 7864320 | tf_op jit(solution)/shard_map/dot_general | solution.py:46
  88.8 0.6 collective-permute-start.17
  89.4 1.6 %collective-permute-start.27 = (bf16[64,3072]{1,0:T(8,128)(2,1)S(1)}, bf16[64,3072]{1,0:T(8,128)(2,1)S(1)}, u32[]{:S(2)}, u32[]{:S(2)}) collective-permute-start(bf16[64,3072]{1,0:T(8,128)(2,1)S(1)} %collective-permute-done.22), channel_id=1, source_target_pairs={{0,4},{8,0},{16,8},{24,16},{28,24},{20,28},{12,20},{4,12},{1,5},{9... | collective-permute-start | bytes 1179656 | tf_op jit(solution)/shard_map/ppermute | solution.py:98
  91.1 7.3 %collective-permute-done.26 = bf16[64,3072]{1,0:T(8,128)(2,1)S(1)} collective-permute-done((bf16[64,3072]{1,0:T(8,128)(2,1)S(1)}, bf16[64,3072]{1,0:T(8,128)(2,1)S(1)}, u32[]{:S(2)}, u32[]{:S(2)}) %collective-permute-start.26) | collective-permute-done | bytes 393248 | tf_op jit(solution)/shard_map/ppermute | solution.py:98
  98.5 1.8 %collective-permute-done.27 = bf16[64,3072]{1,0:T(8,128)(2,1)S(1)} collective-permute-done((bf16[64,3072]{1,0:T(8,128)(2,1)S(1)}, bf16[64,3072]{1,0:T(8,128)(2,1)S(1)}, u32[]{:S(2)}, u32[]{:S(2)}) %collective-permute-start.27) | collective-permute-done | bytes 393248 | tf_op jit(solution)/shard_map/ppermute | solution.py:98
  100.4 1.4 %convolution_convert_fusion.6 = bf16[768,128]{1,0:T(8,128)(2,1)S(1)} fusion(bf16[128,3072]{1,0:T(8,128)(2,1)S(1)} %get-tuple-element.17, bf16[384,3072]{1,0:T(8,128)(2,1)S(1)} %copy-done.3, bf16[384,3072]{1,0:T(8,128)(2,1)S(1)} %copy-done.5), kind=kOutput, calls=%fused_computation.18 | convolution fusion | flops 613515264 | bytes 5701632 | tf_op jit(solution)/shard_map/dot_general | solution.py:46
  101.9 1.4 %fusion.61 = (bf16[768,256]{1,0:T(8,128)(2,1)S(1)}, f32[768,256]{1,0:T(8,128)S(1)}) fusion(bf16[768,256]{1,0:T(8,128)(2,1)S(1)} %collective-permute-done.23, bf16[256,3072]{1,0:T(8,128)(2,1)S(1)} %get-tuple-element.21, bf16[384,3072]{1,0:T(8,128)(2,1)S(1)} %get-tuple-element.8, bf16[384,3072]{1,0:T(8,128)(2,1)S(1)} %copy-done.1), kind=kOutput, calls=%fused_computation.170 | convolution fusion | flops 1218379776 | bytes 7864320 | tf_op jit(solution)/shard_map/dot_general | solution.py:46
  103.3 1.6 %collective-permute-start.24 = (bf16[768,256]{1,0:T(8,128)(2,1)S(1)}, bf16[768,256]{1,0:T(8,128)(2,1)S(1)}, u32[]{:S(2)}, u32[]{:S(2)}) collective-permute-start(bf16[768,256]{1,0:T(8,128)(2,1)S(1)} %get-tuple-element.65), channel_id=1, source_target_pairs={{0,2},{1,3},{2,0},{3,1},{4,6},{5,7},{6,4},{7,5},{8,10},{9,11},{10,... | collective-permute-start | bytes 1179656 | tf_op jit(solution)/shard_map/ppermute | solution.py:92
  104.9 1.4 %fusion.60 = (bf16[768,128]{1,0:T(8,128)(2,1)S(1)}, f32[768,128]{1,0:T(8,128)S(1)}) fusion(bf16[768,128]{1,0:T(8,128)(2,1)S(1)} %collective-permute-done.28, bf16[128,3072]{1,0:T(8,128)(2,1)S(1)} %get-tuple-element.17, bf16[384,3072]{1,0:T(8,128)(2,1)S(1)} %get-tuple-element.8, bf16[384,3072]{1,0:T(8,128)(2,1)S(1)} %copy-done.1), kind=kOutput, calls=%fused_computation.169 | convolution fusion | flops 613908480 | bytes 6291456 | tf_op jit(solution)/shard_map/dot_general | solution.py:46
  106.3 0.6 collective-permute-start.29
  107.0 12.1 %collective-permute-done.29 = bf16[768,128]{1,0:T(8,128)(2,1)S(1)} collective-permute-done((bf16[768,128]{1,0:T(8,128)(2,1)S(1)}, bf16[768,128]{1,0:T(8,128)(2,1)S(1)}, u32[]{:S(2)}, u32[]{:S(2)}) %collective-permute-start.29) | collective-permute-done | bytes 196640 | tf_op jit(solution)/shard_map/ppermute | solution.py:92
  119.4 0.5 collective-permute-start.4
  121.1 1.0 collective-permute-done.18
  122.8 7.5 %multiply_subtract_fusion = f32[768,3072]{1,0:T(8,128)} fusion(bf16[768,3072]{1,0:T(8,128)(2,1)S(1)} %bitcast.23, bf16[768,1024]{1,0:T(8,128)(2,1)S(1)} %maximum_dynamic-update-slice_fusion.3, bf16[1024,3072]{1,0:T(8,128)(2,1)S(1)} %get-tuple-element.16), kind=kOutput, calls=%fused_computation | convolution fusion | flops 4841275392 | bytes 22020096 | tf_op jit(solution)/shard_map/dot_general | solution.py:149
  (99 shorter events, 5.4 us)
Async XLA Ops:
  2.1 34.0 %collective-permute-start.8 = (bf16[64,3072]{1,0:T(8,128)(2,1)}, bf16[64,3072]{1,0:T(8,128)(2,1)}, u32[]{:S(2)}, u32[]{:S(2)}) collective-permute-start(bf16[64,3072]{1,0:T(8,128)(2,1)} %get-tuple-element.14), channel_id=1, source_target_pairs={{0,4},{8,0},{16,8},{24,16},{28,24},{20,28},{12,20},{4,12},{1,5},{9... | collective-permute-start | bytes 1179656 | tf_op jit(solution)/shard_map/ppermute | solution.py:97
  5.0 30.0 %collective-permute-start.7 = (bf16[64,3072]{1,0:T(8,128)(2,1)}, bf16[64,3072]{1,0:T(8,128)(2,1)}, u32[]{:S(2)}, u32[]{:S(2)}) collective-permute-start(bf16[64,3072]{1,0:T(8,128)(2,1)} %get-tuple-element.14), channel_id=1, source_target_pairs={{0,8},{8,16},{16,24},{24,28},{28,20},{20,12},{12,4},{4,0},{1,9},{9... | collective-permute-start | bytes 1179656 | tf_op jit(solution)/shard_map/ppermute | solution.py:96
  6.9 13.9 %collective-permute-start.2 = (bf16[256,384]{1,0:T(8,128)(2,1)}, bf16[256,384]{1,0:T(8,128)(2,1)}, u32[]{:S(2)}, u32[]{:S(2)}) collective-permute-start(bf16[256,384]{1,0:T(8,128)(2,1)} %get-tuple-element.51), channel_id=1, source_target_pairs={{0,1},{1,0},{2,3},{3,2},{4,5},{5,4},{6,7},{7,6},{8,9},{9,8},{10,11... | collective-permute-start | bytes 589832 | tf_op jit(solution)/shard_map/ppermute | solution.py:92
  6.9 8.2 %copy-start = (bf16[128,3072]{1,0:T(8,128)(2,1)S(1)}, bf16[128,3072]{1,0:T(8,128)(2,1)}, u32[]{:S(2)}) copy-start(bf16[128,3072]{1,0:T(8,128)(2,1)} %param.7) | copy-start | bytes 2359300
  6.9 27.1 %collective-permute-start.6 = (bf16[64,3072]{1,0:T(8,128)(2,1)}, bf16[64,3072]{1,0:T(8,128)(2,1)}, u32[]{:S(2)}, u32[]{:S(2)}) collective-permute-start(bf16[64,3072]{1,0:T(8,128)(2,1)} %get-tuple-element.15), channel_id=1, source_target_pairs={{0,4},{8,0},{16,8},{24,16},{28,24},{20,28},{12,20},{4,12},{1,5},{9... | collective-permute-start | bytes 1179656 | tf_op jit(solution)/shard_map/ppermute | solution.py:97
  15.1 2.2 %copy-start.2 = (bf16[384,3072]{1,0:T(8,128)(2,1)}, bf16[384,3072]{1,0:T(8,128)(2,1)S(1)}, u32[]{:S(2)}) copy-start(bf16[384,3072]{1,0:T(8,128)(2,1)S(1)} %get-tuple-element.7) | copy-start | bytes 7077892
  15.1 2.2 %copy-start.4 = (bf16[384,3072]{1,0:T(8,128)(2,1)}, bf16[384,3072]{1,0:T(8,128)(2,1)S(1)}, u32[]{:S(2)}) copy-start(bf16[384,3072]{1,0:T(8,128)(2,1)S(1)} %get-tuple-element.72) | copy-start | bytes 7077892
  15.1 4.2 %copy-start.8 = (s32[4]{0:T(128)S(1)}, s32[4]{0:T(128)}, u32[]{:S(2)}) copy-start(s32[4]{0:T(128)} %param.11) | copy-start | bytes 52
  17.3 5.0 %collective-permute-start = (bf16[768,128]{1,0:T(8,128)(2,1)}, bf16[768,128]{1,0:T(8,128)(2,1)S(1)}, u32[]{:S(2)}, u32[]{:S(2)}) collective-permute-start(bf16[768,128]{1,0:T(8,128)(2,1)} %convolution_convert_fusion.8), channel_id=1, source_target_pairs={{0,1},{1,0},{2,3},{3,2},{4,5},{5,4},{6,7},{7,6},{8,9},{9,8},{10,11... | collective-permute-start | bytes 589832 | tf_op jit(solution)/shard_map/ppermute | solution.py:92
  20.8 11.5 %collective-permute-start.5 = (bf16[64,3072]{1,0:T(8,128)(2,1)}, bf16[64,3072]{1,0:T(8,128)(2,1)S(1)}, u32[]{:S(2)}, u32[]{:S(2)}) collective-permute-start(bf16[64,3072]{1,0:T(8,128)(2,1)} %get-tuple-element.15), channel_id=1, source_target_pairs={{0,8},{8,16},{16,24},{24,28},{28,20},{20,12},{12,4},{4,0},{1,9},{9... | collective-permute-start | bytes 1179656 | tf_op jit(solution)/shard_map/ppermute | solution.py:96
  21.2 12.6 %slice-start.2 = ((s8[6291456]{0:T(1024)(128)(4,1)}), s8[4194304]{0:T(1024)(128)(4,1)S(1)}, s32[]{:S(2)}) async-start(s8[6291456]{0:T(1024)(128)(4,1)} %bitcast.24), calls=%async_computation.2 | async-start | bytes 8388608
  22.4 19.0 %collective-permute-start.3 = (bf16[512,384]{1,0:T(8,128)(2,1)S(1)}, bf16[512,384]{1,0:T(8,128)(2,1)S(1)}, u32[]{:S(2)}, u32[]{:S(2)}) collective-permute-start(bf16[512,384]{1,0:T(8,128)(2,1)S(1)} %pad_maximum_fusion.2), channel_id=1, source_target_pairs={{0,2},{1,3},{2,0},{3,1},{4,6},{5,7},{6,4},{7,5},{8,10},{9,11},{10,... | collective-permute-start | bytes 1179656 | tf_op jit(solution)/shard_map/ppermute | solution.py:92
  24.1 9.7 %slice-start.3 = ((s8[6291456]{0:T(1024)(128)(4,1)}), s8[2097152]{0:T(1024)(128)(4,1)S(1)}, s32[]{:S(2)}) async-start(s8[6291456]{0:T(1024)(128)(4,1)} %bitcast.24), calls=%async_computation.3 | async-start | bytes 4194304
  27.3 9.9 %copy-start.3 = (bf16[384,3072]{1,0:T(8,128)(2,1)S(1)}, bf16[384,3072]{1,0:T(8,128)(2,1)}, u32[]{:S(2)}) copy-start(bf16[384,3072]{1,0:T(8,128)(2,1)} %copy-done.2) | copy-start | bytes 7077892
  27.3 9.9 %copy-start.5 = (bf16[384,3072]{1,0:T(8,128)(2,1)S(1)}, bf16[384,3072]{1,0:T(8,128)(2,1)}, u32[]{:S(2)}) copy-start(bf16[384,3072]{1,0:T(8,128)(2,1)} %copy-done.4) | copy-start | bytes 7077892
  32.3 8.5 %collective-permute-start.1 = (bf16[768,128]{1,0:T(8,128)(2,1)S(1)}, bf16[768,128]{1,0:T(8,128)(2,1)S(1)}, u32[]{:S(2)}, u32[]{:S(2)}) collective-permute-start(bf16[768,128]{1,0:T(8,128)(2,1)S(1)} %get-tuple-element.63), channel_id=1, source_target_pairs={{0,2},{1,3},{2,0},{3,1},{4,6},{5,7},{6,4},{7,5},{8,10},{9,11},{10,... | collective-permute-start | bytes 589832 | tf_op jit(solution)/shard_map/ppermute | solution.py:92
  38.6 25.5 %collective-permute-start.9 = (bf16[768,256]{1,0:T(8,128)(2,1)S(1)}, bf16[768,256]{1,0:T(8,128)(2,1)S(1)}, u32[]{:S(2)}, u32[]{:S(2)}) collective-permute-start(bf16[768,256]{1,0:T(8,128)(2,1)S(1)} %convolution_convert_fusion.4), channel_id=1, source_target_pairs={{0,1},{1,0},{2,3},{3,2},{4,5},{5,4},{6,7},{7,6},{8,9},{9,8},{10,11... | collective-permute-start | bytes 1179656 | tf_op jit(solution)/shard_map/ppermute | solution.py:92
  38.7 21.7 %collective-permute-start.15 = (bf16[64,3072]{1,0:T(8,128)(2,1)}, bf16[64,3072]{1,0:T(8,128)(2,1)S(1)}, u32[]{:S(2)}, u32[]{:S(2)}) collective-permute-start(bf16[64,3072]{1,0:T(8,128)(2,1)} %collective-permute-done.8), channel_id=1, source_target_pairs={{0,4},{8,0},{16,8},{24,16},{28,24},{20,28},{12,20},{4,12},{1,5},{9... | collective-permute-start | bytes 1179656 | tf_op jit(solution)/shard_map/ppermute | solution.py:97
  40.4 20.0 %collective-permute-start.14 = (bf16[64,3072]{1,0:T(8,128)(2,1)}, bf16[64,3072]{1,0:T(8,128)(2,1)S(1)}, u32[]{:S(2)}, u32[]{:S(2)}) collective-permute-start(bf16[64,3072]{1,0:T(8,128)(2,1)} %collective-permute-done.7), channel_id=1, source_target_pairs={{0,8},{8,16},{16,24},{24,28},{28,20},{20,12},{12,4},{4,0},{1,9},{9... | collective-permute-start | bytes 1179656 | tf_op jit(solution)/shard_map/ppermute | solution.py:96
  40.8 19.4 %collective-permute-start.12 = (bf16[64,3072]{1,0:T(8,128)(2,1)S(1)}, bf16[64,3072]{1,0:T(8,128)(2,1)S(1)}, u32[]{:S(2)}, u32[]{:S(2)}) collective-permute-start(bf16[64,3072]{1,0:T(8,128)(2,1)S(1)} %collective-permute-done.5), channel_id=1, source_target_pairs={{0,8},{8,16},{16,24},{24,28},{28,20},{20,12},{12,4},{4,0},{1,9},{9... | collective-permute-start | bytes 1179656 | tf_op jit(solution)/shard_map/ppermute | solution.py:96
  41.4 18.8 %collective-permute-start.13 = (bf16[64,3072]{1,0:T(8,128)(2,1)}, bf16[64,3072]{1,0:T(8,128)(2,1)S(1)}, u32[]{:S(2)}, u32[]{:S(2)}) collective-permute-start(bf16[64,3072]{1,0:T(8,128)(2,1)} %collective-permute-done.6), channel_id=1, source_target_pairs={{0,4},{8,0},{16,8},{24,16},{28,24},{20,28},{12,20},{4,12},{1,5},{9... | collective-permute-start | bytes 1179656 | tf_op jit(solution)/shard_map/ppermute | solution.py:97
  60.5 3.6 %copy-start.1 = (bf16[384,3072]{1,0:T(8,128)(2,1)S(1)}, bf16[384,3072]{1,0:T(8,128)(2,1)}, u32[]{:S(2)}) copy-start(bf16[384,3072]{1,0:T(8,128)(2,1)} %get-tuple-element.71) | copy-start | bytes 7077892
  62.0 25.4 %collective-permute-start.16 = (bf16[768,256]{1,0:T(8,128)(2,1)S(1)}, bf16[768,256]{1,0:T(8,128)(2,1)S(1)}, u32[]{:S(2)}, u32[]{:S(2)}) collective-permute-start(bf16[768,256]{1,0:T(8,128)(2,1)S(1)} %convolution_convert_fusion.2), channel_id=1, source_target_pairs={{0,1},{1,0},{2,3},{3,2},{4,5},{5,4},{6,7},{7,6},{8,9},{9,8},{10,11... | collective-permute-start | bytes 1179656 | tf_op jit(solution)/shard_map/ppermute | solution.py:92
  62.0 13.3 %collective-permute-start.20 = (bf16[64,3072]{1,0:T(8,128)(2,1)S(1)}, bf16[64,3072]{1,0:T(8,128)(2,1)S(1)}, u32[]{:S(2)}, u32[]{:S(2)}) collective-permute-start(bf16[64,3072]{1,0:T(8,128)(2,1)S(1)} %collective-permute-done.13), channel_id=1, source_target_pairs={{0,4},{8,0},{16,8},{24,16},{28,24},{20,28},{12,20},{4,12},{1,5},{9... | collective-permute-start | bytes 1179656 | tf_op jit(solution)/shard_map/ppermute | solution.py:97
  63.7 11.2 %collective-permute-start.19 = (bf16[64,3072]{1,0:T(8,128)(2,1)S(1)}, bf16[64,3072]{1,0:T(8,128)(2,1)S(1)}, u32[]{:S(2)}, u32[]{:S(2)}) collective-permute-start(bf16[64,3072]{1,0:T(8,128)(2,1)S(1)} %collective-permute-done.12), channel_id=1, source_target_pairs={{0,8},{8,16},{16,24},{24,28},{28,20},{20,12},{12,4},{4,0},{1,9},{9... | collective-permute-start | bytes 1179656 | tf_op jit(solution)/shard_map/ppermute | solution.py:96
  65.6 25.4 %collective-permute-start.10 = (bf16[768,256]{1,0:T(8,128)(2,1)S(1)}, bf16[768,256]{1,0:T(8,128)(2,1)S(1)}, u32[]{:S(2)}, u32[]{:S(2)}) collective-permute-start(bf16[768,256]{1,0:T(8,128)(2,1)S(1)} %get-tuple-element.69), channel_id=1, source_target_pairs={{0,2},{1,3},{2,0},{3,1},{4,6},{5,7},{6,4},{7,5},{8,10},{9,11},{10,... | collective-permute-start | bytes 1179656 | tf_op jit(solution)/shard_map/ppermute | solution.py:92
  66.1 19.2 %collective-permute-start.22 = (bf16[64,3072]{1,0:T(8,128)(2,1)S(1)}, bf16[64,3072]{1,0:T(8,128)(2,1)S(1)}, u32[]{:S(2)}, u32[]{:S(2)}) collective-permute-start(bf16[64,3072]{1,0:T(8,128)(2,1)S(1)} %collective-permute-done.15), channel_id=1, source_target_pairs={{0,4},{8,0},{16,8},{24,16},{28,24},{20,28},{12,20},{4,12},{1,5},{9... | collective-permute-start | bytes 1179656 | tf_op jit(solution)/shard_map/ppermute | solution.py:97
  74.9 10.4 %collective-permute-start.21 = (bf16[64,3072]{1,0:T(8,128)(2,1)S(1)}, bf16[64,3072]{1,0:T(8,128)(2,1)S(1)}, u32[]{:S(2)}, u32[]{:S(2)}) collective-permute-start(bf16[64,3072]{1,0:T(8,128)(2,1)S(1)} %collective-permute-done.14), channel_id=1, source_target_pairs={{0,8},{8,16},{16,24},{24,28},{28,20},{20,12},{12,4},{4,0},{1,9},{9... | collective-permute-start | bytes 1179656 | tf_op jit(solution)/shard_map/ppermute | solution.py:96
  86.8 15.0 %collective-permute-start.23 = (bf16[768,256]{1,0:T(8,128)(2,1)S(1)}, bf16[768,256]{1,0:T(8,128)(2,1)S(1)}, u32[]{:S(2)}, u32[]{:S(2)}) collective-permute-start(bf16[768,256]{1,0:T(8,128)(2,1)S(1)} %convolution_convert_fusion), channel_id=1, source_target_pairs={{0,1},{1,0},{2,3},{3,2},{4,5},{5,4},{6,7},{7,6},{8,9},{9,8},{10,11... | collective-permute-start | bytes 1179656 | tf_op jit(solution)/shard_map/ppermute | solution.py:92
  86.9 11.5 %collective-permute-start.26 = (bf16[64,3072]{1,0:T(8,128)(2,1)S(1)}, bf16[64,3072]{1,0:T(8,128)(2,1)S(1)}, u32[]{:S(2)}, u32[]{:S(2)}) collective-permute-start(bf16[64,3072]{1,0:T(8,128)(2,1)S(1)} %collective-permute-done.19), channel_id=1, source_target_pairs={{0,8},{8,16},{16,24},{24,28},{28,20},{20,12},{12,4},{4,0},{1,9},{9... | collective-permute-start | bytes 1179656 | tf_op jit(solution)/shard_map/ppermute | solution.py:98
  88.8 18.1 %collective-permute-start.17 = (bf16[768,256]{1,0:T(8,128)(2,1)S(1)}, bf16[768,256]{1,0:T(8,128)(2,1)S(1)}, u32[]{:S(2)}, u32[]{:S(2)}) collective-permute-start(bf16[768,256]{1,0:T(8,128)(2,1)S(1)} %get-tuple-element.67), channel_id=1, source_target_pairs={{0,2},{1,3},{2,0},{3,1},{4,6},{5,7},{6,4},{7,5},{8,10},{9,11},{10,... | collective-permute-start | bytes 1179656 | tf_op jit(solution)/shard_map/ppermute | solution.py:92
  89.4 10.9 %collective-permute-start.27 = (bf16[64,3072]{1,0:T(8,128)(2,1)S(1)}, bf16[64,3072]{1,0:T(8,128)(2,1)S(1)}, u32[]{:S(2)}, u32[]{:S(2)}) collective-permute-start(bf16[64,3072]{1,0:T(8,128)(2,1)S(1)} %collective-permute-done.22), channel_id=1, source_target_pairs={{0,4},{8,0},{16,8},{24,16},{28,24},{20,28},{12,20},{4,12},{1,5},{9... | collective-permute-start | bytes 1179656 | tf_op jit(solution)/shard_map/ppermute | solution.py:98
  101.8 3.1 %collective-permute-start.28 = (bf16[768,128]{1,0:T(8,128)(2,1)S(1)}, bf16[768,128]{1,0:T(8,128)(2,1)S(1)}, u32[]{:S(2)}, u32[]{:S(2)}) collective-permute-start(bf16[768,128]{1,0:T(8,128)(2,1)S(1)} %convolution_convert_fusion.6), channel_id=1, source_target_pairs={{0,1},{1,0},{2,3},{3,2},{4,5},{5,4},{6,7},{7,6},{8,9},{9,8},{10,11... | collective-permute-start | bytes 589832 | tf_op jit(solution)/shard_map/ppermute | solution.py:92
  103.3 15.8 %copy-start.6 = (f32[128]{0:T(128)S(1)}, f32[128]{0:T(128)}, u32[]{:S(2)}) copy-start(f32[128]{0:T(128)} %get-tuple-element.56) | copy-start | bytes 1540
  103.3 15.8 %copy-start.7 = (f32[128]{0:T(128)S(1)}, f32[128]{0:T(128)}, u32[]{:S(2)}) copy-start(f32[128]{0:T(128)} %get-tuple-element.57) | copy-start | bytes 1540
  103.3 16.6 %collective-permute-start.24 = (bf16[768,256]{1,0:T(8,128)(2,1)S(1)}, bf16[768,256]{1,0:T(8,128)(2,1)S(1)}, u32[]{:S(2)}, u32[]{:S(2)}) collective-permute-start(bf16[768,256]{1,0:T(8,128)(2,1)S(1)} %get-tuple-element.65), channel_id=1, source_target_pairs={{0,2},{1,3},{2,0},{3,1},{4,6},{5,7},{6,4},{7,5},{8,10},{9,11},{10,... | collective-permute-start | bytes 1179656 | tf_op jit(solution)/shard_map/ppermute | solution.py:92
  106.3 12.8 %collective-permute-start.29 = (bf16[768,128]{1,0:T(8,128)(2,1)S(1)}, bf16[768,128]{1,0:T(8,128)(2,1)S(1)}, u32[]{:S(2)}, u32[]{:S(2)}) collective-permute-start(bf16[768,128]{1,0:T(8,128)(2,1)S(1)} %get-tuple-element.61), channel_id=1, source_target_pairs={{0,2},{1,3},{2,0},{3,1},{4,6},{5,7},{6,4},{7,5},{8,10},{9,11},{10,... | collective-permute-start | bytes 589832 | tf_op jit(solution)/shard_map/ppermute | solution.py:92
  119.2 3.6 %slice-start = ((s8[4718592]{0:T(1024)(128)(4,1)}), s8[4194304]{0:T(1024)(128)(4,1)S(1)}, s32[]{:S(2)}) async-start(s8[4718592]{0:T(1024)(128)(4,1)} %bitcast.22), calls=%async_computation | async-start | bytes 8388608
  119.3 1.8 %collective-permute-start.30 = (bf16[384,128]{1,0:T(8,128)(2,1)S(1)}, bf16[384,128]{1,0:T(8,128)(2,1)S(1)}, u32[]{:S(2)}, u32[]{:S(2)}) collective-permute-start(bf16[384,128]{1,0:T(8,128)(2,1)S(1)} %get-tuple-element.9), channel_id=1, source_target_pairs={{0,1},{1,0},{2,3},{3,2},{4,5},{5,4},{6,7},{7,6},{8,9},{9,8},{10,11... | collective-permute-start | bytes 294920 | tf_op jit(solution)/shard_map/ppermute | solution.py:92
  119.4 1.6 %collective-permute-start.4 = (bf16[384,128]{1,0:T(8,128)(2,1)S(1)}, bf16[384,128]{1,0:T(8,128)(2,1)S(1)}, u32[]{:S(2)}, u32[]{:S(2)}) collective-permute-start(bf16[384,128]{1,0:T(8,128)(2,1)S(1)} %get-tuple-element.10), channel_id=1, source_target_pairs={{0,1},{1,0},{2,3},{3,2},{4,5},{5,4},{6,7},{7,6},{8,9},{9,8},{10,11... | collective-permute-start | bytes 294920 | tf_op jit(solution)/shard_map/ppermute | solution.py:92
  120.0 2.8 %slice-start.1 = ((s8[4718592]{0:T(1024)(128)(4,1)}), s8[524288]{0:T(1024)(128)(4,1)S(1)}, s32[]{:S(2)}) async-start(s8[4718592]{0:T(1024)(128)(4,1)} %bitcast.22), calls=%async_computation.1 | async-start | bytes 1048576
  120.4 2.2 %collective-permute-start.25 = (bf16[384,256]{1,0:T(8,128)(2,1)S(1)}, bf16[384,256]{1,0:T(8,128)(2,1)S(1)}, u32[]{:S(2)}, u32[]{:S(2)}) collective-permute-start(bf16[384,256]{1,0:T(8,128)(2,1)S(1)} %get-tuple-element.11), channel_id=1, source_target_pairs={{0,1},{1,0},{2,3},{3,2},{4,5},{5,4},{6,7},{7,6},{8,9},{9,8},{10,11... | collective-permute-start | bytes 589832 | tf_op jit(solution)/shard_map/ppermute | solution.py:92
  120.5 1.6 %collective-permute-start.18 = (bf16[384,256]{1,0:T(8,128)(2,1)S(1)}, bf16[384,256]{1,0:T(8,128)(2,1)S(1)}, u32[]{:S(2)}, u32[]{:S(2)}) collective-permute-start(bf16[384,256]{1,0:T(8,128)(2,1)S(1)} %get-tuple-element.12), channel_id=1, source_target_pairs={{0,1},{1,0},{2,3},{3,2},{4,5},{5,4},{6,7},{7,6},{8,9},{9,8},{10,11... | collective-permute-start | bytes 589832 | tf_op jit(solution)/shard_map/ppermute | solution.py:92
  120.9 1.5 %collective-permute-start.11 = (bf16[384,256]{1,0:T(8,128)(2,1)S(1)}, bf16[384,256]{1,0:T(8,128)(2,1)S(1)}, u32[]{:S(2)}, u32[]{:S(2)}) collective-permute-start(bf16[384,256]{1,0:T(8,128)(2,1)S(1)} %get-tuple-element.13), channel_id=1, source_target_pairs={{0,1},{1,0},{2,3},{3,2},{4,5},{5,4},{6,7},{7,6},{8,9},{9,8},{10,11... | collective-permute-start | bytes 589832 | tf_op jit(solution)/shard_map/ppermute | solution.py:92

commit v2 on v1

--- a/solution.py
+++ b/solution.py
@@ -1,6 +1,10 @@
+import functools
+
 import jax
 import jax.numpy as jnp
 from jax import lax
+from jax.experimental import pallas as pl
+from jax.experimental.pallas import tpu as pltpu
 from jax.sharding import PartitionSpec as P
 
 GRID = 16
@@ -72,12 +76,104 @@
     at = RING.index(dp)
     seq = [(0, 0), (0, 1)]
     for k in range(1, COUNT // 2):
-        seq += [(-k, 0), (k, 0), (-k, 1), (k, 1)]
+        seq += [(-k, 0), (-k, 1), (k, 0), (k, 1)]
     seq += [(COUNT // 2, 0), (COUNT // 2, 1)]
     return [2 * RING[(at + k) % COUNT] + h for k, h in seq]
 
 
 ORDER = [order_of(d) for d in range(COUNT)]
+
+
+WEIGHT = 0.15
+
+
+def cost(flops):
+    return pl.CostEstimate(flops=int(WEIGHT * flops), bytes_accessed=0, transcendentals=0)
+
+
+IN_VMEM = pl.BlockSpec(memory_space=pltpu.VMEM)
+
+
+def project_kernel(wanted, count, which_ref, w_ref, d_ref, *refs):
+    parts, outs, block = refs[:count], refs[count:-1], refs[-1]
+    part = w_ref.shape[0] // 2
+    row = 0
+    for ref in parts:
+        block[row : row + ref.shape[0], :] = ref[...]
+        row += ref.shape[0]
+    for flip, out in zip(wanted, outs):
+        which = which_ref[0] if flip == 0 else 1 - which_ref[0]
+        rows = pl.ds(pl.multiple_of(which * part, part), part)
+        for at, source in enumerate((w_ref, d_ref)):
+            out[at * part : (at + 1) * part, :] = project_rows(source[rows, :], block[...]).astype(out.dtype)
+
+
+def project(core, w_out, direction, parts, wanted):
+    count = sum(v.shape[0] for v in parts)
+    width, depth = w_out.shape
+    return pl.pallas_call(
+        functools.partial(project_kernel, wanted, len(parts)),
+        out_shape=[jax.ShapeDtypeStruct((width, count), jnp.bfloat16) for _ in wanted]
+        + [jax.ShapeDtypeStruct((count, depth), jnp.bfloat16)],
+        in_specs=[pl.BlockSpec(memory_space=pltpu.SMEM)] + [IN_VMEM] * (2 + len(parts)),
+        out_specs=[IN_VMEM] * (len(wanted) + 1),
+        compiler_params=pltpu.CompilerParams(vmem_limit_bytes=20 * 2**20),
+        cost_estimate=cost(2 * len(wanted) * width * max(count, 256) * depth),
+        name="project",
+    )(core, w_out, direction, *parts)
+
+
+def contract_kernel(count, step, tile, which_ref, base_ref, *refs):
+    terms, out = [refs[3 * i : 3 * i + 3] for i in range(count)], refs[3 * count]
+    width, depth = base_ref.shape
+    part = width // 2
+    first = base_ref.dtype == jnp.bfloat16
+    if not first:
+        buffer, sem = refs[3 * count + 1 :]
+
+    def copy_of(i):
+        columns = pl.ds(pl.multiple_of(i * tile, tile), tile)
+        return pltpu.make_async_copy(buffer.at[i % 2], out.at[:, columns], sem.at[i % 2])
+
+    for i in range(depth // tile):
+        columns = slice(i * tile, (i + 1) * tile)
+        if not first and i >= 2:
+            copy_of(i - 2).wait()
+        for flip in (0, 1):
+            which = which_ref[0] if flip == 0 else 1 - which_ref[0]
+            rows = pl.ds(pl.multiple_of(which * part, part), part)
+            total = sum(
+                jnp.dot(term[flip][...], term[2][:, columns], preferred_element_type=jnp.float32) for term in terms
+            )
+            if first:
+                out[rows, columns] = 2.0 * base_ref[rows, columns].astype(jnp.float32) - step * total
+            else:
+                buffer[i % 2, rows, :] = base_ref[rows, columns] - step * total
+        if not first:
+            copy_of(i).start()
+    if not first:
+        for i in range(max(0, depth // tile - 2), depth // tile):
+            copy_of(i).wait()
+
+
+def contract(core, base, terms, step):
+    width, depth = base.shape
+    first = base.dtype == jnp.bfloat16
+    tile = 512
+    while depth % tile:
+        tile //= 2
+    return pl.pallas_call(
+        functools.partial(contract_kernel, len(terms), step, tile),
+        out_shape=jax.ShapeDtypeStruct((width, depth), jnp.float32),
+        in_specs=[pl.BlockSpec(memory_space=pltpu.SMEM)] + [IN_VMEM] * (1 + 3 * len(terms)),
+        out_specs=IN_VMEM if first else pl.BlockSpec(memory_space=pl.ANY),
+        scratch_shapes=[]
+        if first
+        else [pltpu.VMEM((2, width, tile), jnp.float32), pltpu.SemaphoreType.DMA((2,))],
+        compiler_params=pltpu.CompilerParams(vmem_limit_bytes=20 * 2**20),
+        cost_estimate=cost(2 * width * depth * sum(term[2].shape[0] for term in terms)),
+        name="contract",
+    )(core, base, *[v for term in terms for v in term])
 
 
 def on_device(hidden, w_out, direction, targets, codes, code_weights):
@@ -91,17 +187,17 @@
     def swap(value, pairs):
         return lax.ppermute(value, "mp", pairs)
 
-    up, down = [(hidden[:half], hidden[half:])], [(hidden[:half], hidden[half:])]
-    for k in range(1, COUNT // 2):
-        up.append(tuple(lax.ppermute(v, "dp", UP) for v in up[-1]))
-        down.append(tuple(lax.ppermute(v, "dp", DOWN) for v in down[-1]))
-    last = (lax.ppermute(up[-1][0], "dp", UP), lax.ppermute(down[-1][1], "dp", DOWN))
+    def gate(*values):
+        return lax.optimization_barrier(values)
+
+    def step(pair):
+        return lax.ppermute(pair[0], "dp", UP), lax.ppermute(pair[1], "dp", DOWN)
 
     def cols(value, which):
         return lax.dynamic_slice_in_dim(value, which * part, part, 1)
 
     two = jnp.concatenate([cols(targets, core), swap(cols(targets, 1 - core), CORE)], axis=0)
-    four = jnp.concatenate([two, swap(two, ROW)], axis=0)
+    other = swap(two, ROW)
     base = jnp.asarray(ORDER, jnp.int32)[dp] * half
     token = (base[:, None] + jnp.arange(half, dtype=jnp.int32)[None, :]).reshape(1, tokens_all)
     image, patch = token // PATCHES, token % PATCHES
@@ -117,39 +213,55 @@
     row = jnp.where(code // 2 == 1, GRID - 1 - row, row)
     source = (image ^ mp) * PATCHES + row * GRID + col
     one_hot = (jnp.arange(tokens_all, dtype=jnp.int32)[:, None] == source).astype(jnp.bfloat16)
-    aligned = contract_rows(four, one_hot)
-
-    def pair_rows(which):
-        return jnp.concatenate(
-            [lax.dynamic_slice_in_dim(w_out, which * part, part, 0),
-             lax.dynamic_slice_in_dim(direction, which * part, part, 0)], axis=0)
-
-    stack_mine, stack_theirs = pair_rows(core), pair_rows(1 - core)
-
-    def round_of(block, start):
-        theirs = swap(project_rows(stack_theirs, block).astype(jnp.bfloat16), CORE)
-        kept = project_rows(stack_mine, block).astype(jnp.bfloat16).astype(jnp.float32)
-        chip = kept + theirs.astype(jnp.float32)
-        sums = chip + swap(chip.astype(jnp.bfloat16), ROW).astype(jnp.float32)
-        at = slice(start, start + block.shape[0])
+
+    aligned = contract_rows(jnp.concatenate([two, other], axis=0), one_hot)
+    one = core[None]
+
+    def add(kept, theirs):
+        return kept.astype(jnp.float32) + theirs.astype(jnp.float32)
+
+    def over_rows(chip):
+        return swap(chip.astype(jnp.bfloat16), ROW)
+
+    def weigh(chip, across, start):
+        sums = add(chip, across)
+        at = slice(start, start + sums.shape[1])
         slope = 1.0 - jnp.tanh(sums[:part] - aligned[:, at]) ** 2
         mine = (weight[:, at] * slope * sums[part:]).astype(jnp.bfloat16)
-        theirs = swap(mine, CORE)
-        low, high = lax.select(core == 0, mine, theirs), lax.select(core == 0, theirs, mine)
-        return jnp.concatenate([low, high], axis=0)
-
-    blocks = [hidden]
-    for k in range(1, COUNT // 2):
-        blocks.append(jnp.concatenate([up[k][0], down[k][0], up[k][1], down[k][1]], axis=0))
-    blocks.append(jnp.concatenate(last, axis=0))
-    start, scaled = 0, []
-    for block in blocks:
-        scaled.append(round_of(block, start))
-        start += block.shape[0]
-    curvature = jnp.dot(
-        jnp.concatenate(scaled, axis=1), jnp.concatenate(blocks, axis=0), preferred_element_type=jnp.float32
-    )
-    return 2.0 * direction.astype(jnp.float32) - STEP * (curvature / tokens_all)
+        return mine, swap(mine, CORE)
+
+    hop1 = step((hidden, hidden))
+    theirs0, kept0, _ = project(one, w_out, direction, [hidden], (1, 0))
+    chip0 = add(kept0, swap(theirs0, CORE))
+    across0 = over_rows(chip0)
+
+    hop2 = step(hop1)
+    theirs1, kept1, block1 = project(one, w_out, direction, hop1, (1, 0))
+    chip1 = add(kept1, swap(theirs1, CORE))
+    across1 = over_rows(chip1)
+    *hop2, kept1 = gate(*hop2, kept1)
+    hop3 = step(hop2)
+    theirs2, kept2, block2 = project(one, w_out, direction, hop2, (1, 0))
+    chip2 = add(kept2, swap(theirs2, CORE))
+    across2 = over_rows(chip2)
+    scaled0 = weigh(chip0, across0, 0)
+    *hop3, kept2 = gate(*hop3, kept2)
+    hop4 = step((hop3[0][:half], hop3[1][half:]))
+    theirs3, kept3, block3 = project(one, w_out, direction, hop3, (1, 0))
+    chip3 = add(kept3, swap(theirs3, CORE))
+    across3 = over_rows(chip3)
+    scaled1 = weigh(chip1, across1, rows)
+    *hop4, kept3 = gate(*hop4, kept3)
+    theirs4, block4 = project(one, w_out, direction, hop4, (1,))
+    theirs4 = swap(theirs4, CORE)
+    kept4, _ = project(one, w_out, direction, hop4, (0,))
+    chip4 = add(kept4, theirs4)
+    across4 = over_rows(chip4)
+    scaled2 = weigh(chip2, across2, 3 * rows)
+    total = contract(one, direction, [(*scaled0, hidden), (*scaled1, block1), (*scaled2, block2)], STEP / tokens_all)
+    scaled3 = weigh(chip3, across3, 5 * rows)
+    scaled4 = weigh(chip4, across4, 7 * rows)
+    return contract(one, total, [(*scaled3, block3), (*scaled4, block4)], STEP / tokens_all)
 
 
 def solution(mesh):

time: 131 us -> 101 us (0.77)
  matrix products: 26.2 us -> 1.08 us
  Pallas kernels: 0 us -> 23.4 us
  waiting for transfers between devices: 59.6 us -> 41.4 us
  starting transfers between devices: 24 us -> 19.8 us
  local copies, waits for them, and re-layouts: 15.8 us -> 11.7 us
  other arithmetic: 4.03 us -> 2.47 us
    dot_general x11 -> x0, matrix products: 24.2 us -> none  [the longest x10 16.7 us: project_rows(): lax.dot_general(rows_here, stacked, (((1,), (1,)), ((), ())), preferred_e...]
    pallas_call x0 -> x8, Pallas kernels: none -> 23.4 us  [the longest x6 13.9 us: project(): pl.pallas_call(functools.partial(project_kernel, wanted, len(parts)), out...]
    ppermute x14 -> x8, waiting for transfers between devices: 46.3 us -> 27.9 us  [step(): return (lax.ppermute(pair[0], 'dp', UP), lax.ppermute(pair[1], 'dp', DOWN))]
    ppermute x14 -> x8, starting transfers between devices: 15.7 us -> 9.16 us  [step(): return (lax.ppermute(pair[0], 'dp', UP), lax.ppermute(pair[1], 'dp', DOWN))]
    dynamic_slice x1 -> x0, local copies, waits for them, and re-layouts: 6.3 us -> none  [pair_rows(): lax.dynamic_slice_in_dim(direction, which * part, part, 0)]
    unnamed x40 -> x20, local copies, waits for them, and re-layouts: 4.91 us -> 10.5 us
    ppermute x17, starting transfers between devices: 8.29 us -> 10.6 us  [swap(): return lax.ppermute(value, 'mp', pairs)]
    slice x2 -> x3, local copies, waits for them, and re-layouts: 2.11 us -> 0.06 us  [the longest x2 0.05 us: on_device(): hop4 = step((hop3[0][:half], hop3[1][half:]))]
  transfers between devices with their start and end apart: 31 -> 25, of which waited for: 9 -> 11; matrix products, arithmetic and copies ran while one was open for 28% -> 5% of each run, Pallas kernels for 0% -> 18%
where the time goes in v2:
time: 101 us; the launch traced here: 100 us
  waiting for transfers between devices  41.4 us (41%)
  Pallas kernels  23.4 us (23%)
  starting transfers between devices  19.8 us (20%)
  local copies, waits for them, and re-layouts  11.7 us (12%)
  other arithmetic  2.47 us (2%)
  matrix products  1.08 us (1%)
    ppermute x8, waiting for transfers between devices, step(): return (lax.ppermute(pair[0], 'dp', UP), lax.ppermute(pair[1], 'dp', DOWN))  27.9 us
    pallas_call x6, Pallas kernels, project(): pl.pallas_call(functools.partial(project_kernel, wanted, len(parts)), out...  13.9 us
    ppermute x17, waiting for transfers between devices, swap(): return lax.ppermute(value, 'mp', pairs)  13.5 us
    ppermute x17, starting transfers between devices, swap(): return lax.ppermute(value, 'mp', pairs)  10.6 us
    unnamed x20, local copies, waits for them, and re-layouts  10.5 us
    pallas_call x2, Pallas kernels, contract(): pl.pallas_call(functools.partial(contract_kernel, len(terms), step, tile)...  9.51 us
    ppermute x8, starting transfers between devices, step(): return (lax.ppermute(pair[0], 'dp', UP), lax.ppermute(pair[1], 'dp', DOWN))  9.16 us
  transfers between devices with their start and end apart: 25, of which 11 were waited for; matrix products, arithmetic and copies ran while one was open for 5% of the time, Pallas kernels for 18%

profile of v2, /device:TPU:0, one launch (start us, length us, event | category | flops | bytes accessed | tf_op | source)
XLA Modules:
  0.0 100.3 jit_solution(5480684638263357176)
XLA Ops:
  0.0 3.0 %collective-permute-start.5 = (bf16[128,3072]{1,0:T(8,128)(2,1)}, bf16[128,3072]{1,0:T(8,128)(2,1)S(1)}, u32[]{:S(2)}, u32[]{:S(2)}) collective-permute-start(bf16[128,3072]{1,0:T(8,128)(2,1)} %refs_2_.1), channel_id=1, source_target_pairs={{0,8},{8,16},{16,24},{24,28},{28,20},{20,12},{12,4},{4,0},{1,9},{9... | collective-permute-start | bytes 2359304 | tf_op jit(solution)/shard_map/ppermute | solution.py:194
  3.0 1.1 %constant_dynamic-slice_fusion = (bf16[256,384]{1,0:T(8,128)(2,1)S(1)}, bf16[256,384]{1,0:T(8,128)(2,1)S(1)}) fusion(bf16[256,768]{1,0:T(8,128)(2,1)} %param.10, s32[]{:T(128)S(6)} %select_n.103, s32[]{:T(128)S(6)} %select_n.104), kind=kLoop, calls=%fused_computation.97 | loop fusion | bytes 786440 | tf_op jit(solution)/shard_map/dynamic_slice | solution.py:197
  4.2 2.3 %copy-done = bf16[768,3072]{1,0:T(8,128)(2,1)S(1)} copy-done((bf16[768,3072]{1,0:T(8,128)(2,1)S(1)}, bf16[768,3072]{1,0:T(8,128)(2,1)}, u32[]{:S(2)}) %copy-start) | copy-done | bytes 4718616
  6.5 2.3 %copy-done.2 = bf16[768,3072]{1,0:T(8,128)(2,1)S(1)} copy-done((bf16[768,3072]{1,0:T(8,128)(2,1)S(1)}, bf16[768,3072]{1,0:T(8,128)(2,1)}, u32[]{:S(2)}) %copy-start.2) | copy-done | bytes 4718616
  8.9 1.1 %copy-done.4 = bf16[128,3072]{1,0:T(8,128)(2,1)S(1)} copy-done((bf16[128,3072]{1,0:T(8,128)(2,1)S(1)}, bf16[128,3072]{1,0:T(8,128)(2,1)}, u32[]{:S(2)}) %copy-start.4) | copy-done | bytes 786456
  10.0 2.6 %project.6 = (bf16[768,128]{1,0:T(8,128)(2,1)S(1)}, bf16[768,128]{1,0:T(8,128)(2,1)S(1)}, bf16[128,3072]{1,0:T(8,128)(2,1)}) custom-call(s32[1]{0:T(128)} %bitcast.which_ref, bf16[768,3072]{1,0:T(8,128)(2,1)S(1)} %copy-done.2, bf16[768,3072]{1,0:T(8,128)(2,1)S(1)} %copy-done, bf16[128,3072]{1,0:T(8,128)(2,1)S(1)} %copy-done.4), custom_call_target="tpu_custom_call" | custom-call | flops 362387872 | tf_op jit(solution)/shard_map/project/pallas_call | solution.py:114
  12.6 0.6 collective-permute-start
  13.2 0.7 fusion.51
  14.2 6.5 %collective-permute-done.5.refs_0_ = bf16[128,3072]{1,0:T(8,128)(2,1)S(1)} collective-permute-done((bf16[128,3072]{1,0:T(8,128)(2,1)}, bf16[128,3072]{1,0:T(8,128)(2,1)S(1)}, u32[]{:S(2)}, u32[]{:S(2)}) %collective-permute-start.5) | collective-permute-done | bytes 786464 | tf_op jit(solution)/shard_map/ppermute | solution.py:194
  20.7 1.8 %collective-permute-start.10 = (bf16[128,3072]{1,0:T(8,128)(2,1)S(1)}, bf16[128,3072]{1,0:T(8,128)(2,1)S(1)}, u32[]{:S(2)}, u32[]{:S(2)}) collective-permute-start(bf16[128,3072]{1,0:T(8,128)(2,1)S(1)} %collective-permute-done.5.refs_0_), channel_id=1, source_target_pairs={{0,8},{8,16},{16,24},{24,28},{28,20},{20,12},{12,4},{4,0},{1,9},{9... | collective-permute-start | bytes 2359304 | tf_op jit(solution)/shard_map/ppermute | solution.py:194
  22.5 0.2 collective-permute-start.11
  22.8 1.8 %collective-permute-start.1 = (bf16[768,128]{1,0:T(8,128)(2,1)S(1)}, bf16[768,128]{1,0:T(8,128)(2,1)S(1)}, u32[]{:S(2)}, u32[]{:S(2)}) collective-permute-start(bf16[768,128]{1,0:T(8,128)(2,1)S(1)} %fusion.25), channel_id=1, source_target_pairs={{0,2},{1,3},{2,0},{3,1},{4,6},{5,7},{6,4},{7,5},{8,10},{9,11},{10,... | collective-permute-start | bytes 589832 | tf_op jit(solution)/shard_map/ppermute | solution.py:188
  24.6 2.3 %copy-done.1 = bf16[768,3072]{1,0:T(8,128)(2,1)S(1)} copy-done((bf16[768,3072]{1,0:T(8,128)(2,1)S(1)}, bf16[768,3072]{1,0:T(8,128)(2,1)}, u32[]{:S(2)}) %copy-start.1) | copy-done | bytes 4718616
  27.0 2.3 %copy-done.3 = bf16[768,3072]{1,0:T(8,128)(2,1)S(1)} copy-done((bf16[768,3072]{1,0:T(8,128)(2,1)S(1)}, bf16[768,3072]{1,0:T(8,128)(2,1)}, u32[]{:S(2)}) %copy-start.3) | copy-done | bytes 4718616
  29.3 2.6 %project.7 = (bf16[768,256]{1,0:T(8,128)(2,1)S(1)}, bf16[768,256]{1,0:T(8,128)(2,1)S(1)}, bf16[256,3072]{1,0:T(8,128)(2,1)S(1)}) custom-call(s32[1]{0:T(128)} %bitcast.which_ref, bf16[768,3072]{1,0:T(8,128)(2,1)S(1)} %copy-done.3, bf16[768,3072]{1,0:T(8,128)(2,1)S(1)} %copy-done.1, bf16[128,3072]{1,0:T(8,128)(2,1)S(1)} %collective-permute-done.5.refs_0_, ...), custom_call_target="tpu_custom_call" | custom-call | flops 362387872 | tf_op jit(solution)/shard_map/project/pallas_call | solution.py:114
  32.1 0.3 collective-permute-start.3
  32.4 7.0 %collective-permute-done.10.refs_0_ = bf16[128,3072]{1,0:T(8,128)(2,1)S(1)} collective-permute-done((bf16[128,3072]{1,0:T(8,128)(2,1)S(1)}, bf16[128,3072]{1,0:T(8,128)(2,1)S(1)}, u32[]{:S(2)}, u32[]{:S(2)}) %collective-permute-start.10) | collective-permute-done | bytes 786464 | tf_op jit(solution)/shard_map/ppermute | solution.py:194
  39.4 1.2 %collective-permute-done.11.refs_1_ = bf16[128,3072]{1,0:T(8,128)(2,1)S(1)} collective-permute-done((bf16[128,3072]{1,0:T(8,128)(2,1)S(1)}, bf16[128,3072]{1,0:T(8,128)(2,1)S(1)}, u32[]{:S(2)}, u32[]{:S(2)}) %collective-permute-start.11) | collective-permute-done | bytes 786464 | tf_op jit(solution)/shard_map/ppermute | solution.py:194
  40.7 1.6 %collective-permute-start.15 = (bf16[128,3072]{1,0:T(8,128)(2,1)S(1)}, bf16[128,3072]{1,0:T(8,128)(2,1)S(1)}, u32[]{:S(2)}, u32[]{:S(2)}) collective-permute-start(bf16[128,3072]{1,0:T(8,128)(2,1)S(1)} %collective-permute-done.10.refs_0_), channel_id=1, source_target_pairs={{0,8},{8,16},{16,24},{24,28},{28,20},{20,12},{12,4},{4,0},{1,9},{9... | collective-permute-start | bytes 2359304 | tf_op jit(solution)/shard_map/ppermute | solution.py:194
  42.2 0.4 collective-permute-start.16
  42.8 2.6 %project.8 = (bf16[768,256]{1,0:T(8,128)(2,1)S(1)}, bf16[768,256]{1,0:T(8,128)(2,1)S(1)}, bf16[256,3072]{1,0:T(8,128)(2,1)S(1)}) custom-call(s32[1]{0:T(128)} %bitcast.which_ref, bf16[768,3072]{1,0:T(8,128)(2,1)S(1)} %copy-done.3, bf16[768,3072]{1,0:T(8,128)(2,1)S(1)} %copy-done.1, bf16[128,3072]{1,0:T(8,128)(2,1)S(1)} %collective-permute-done.10.refs_0_, ...), custom_call_target="tpu_custom_call" | custom-call | flops 362387872 | tf_op jit(solution)/shard_map/project/pallas_call | solution.py:114
  45.6 1.6 %collective-permute-start.8 = (bf16[768,256]{1,0:T(8,128)(2,1)S(1)}, bf16[768,256]{1,0:T(8,128)(2,1)S(1)}, u32[]{:S(2)}, u32[]{:S(2)}) collective-permute-start(bf16[768,256]{1,0:T(8,128)(2,1)S(1)} %fusion.7), channel_id=1, source_target_pairs={{0,2},{1,3},{2,0},{3,1},{4,6},{5,7},{6,4},{7,5},{8,10},{9,11},{10,... | collective-permute-start | bytes 1179656 | tf_op jit(solution)/shard_map/ppermute | solution.py:188
  47.2 1.1 %fusion = f32[384,1024]{1,0:T(8,128)S(1)} fusion(s32[1024]{0:T(1024)S(1)} %fusion.40, bf16[512,384]{1,0:T(8,128)(2,1)S(1)} %collective-permute-done.3, bf16[256,384]{1,0:T(8,128)(2,1)S(1)} %collective-permute-done.2, bf16[256,384]{1,0:T(8,128)(2,1)S(1)} %get-tuple-element.50), kind=kOutput, calls=%fused_computation.1 | convolution fusion | flops 808714240 | bytes 2363392 | tf_op jit(solution)/shard_map/dot_general | solution.py:18
  48.3 9.6 %collective-permute-done.15.refs_0_ = bf16[128,3072]{1,0:T(8,128)(2,1)S(1)} collective-permute-done((bf16[128,3072]{1,0:T(8,128)(2,1)S(1)}, bf16[128,3072]{1,0:T(8,128)(2,1)S(1)}, u32[]{:S(2)}, u32[]{:S(2)}) %collective-permute-start.15) | collective-permute-done | bytes 786464 | tf_op jit(solution)/shard_map/ppermute | solution.py:194
  57.9 2.0 %collective-permute-done.16.refs_1_ = bf16[128,3072]{1,0:T(8,128)(2,1)S(1)} collective-permute-done((bf16[128,3072]{1,0:T(8,128)(2,1)S(1)}, bf16[128,3072]{1,0:T(8,128)(2,1)S(1)}, u32[]{:S(2)}, u32[]{:S(2)}) %collective-permute-start.16) | collective-permute-done | bytes 786464 | tf_op jit(solution)/shard_map/ppermute | solution.py:194
  59.9 0.5 collective-permute-start.21
  60.4 1.6 %collective-permute-start.20 = (bf16[64,3072]{1,0:T(8,128)(2,1)S(1)}, bf16[64,3072]{1,0:T(8,128)(2,1)S(1)}, u32[]{:S(2)}, u32[]{:S(2)}) collective-permute-start(bf16[64,3072]{1,0:T(8,128)(2,1)S(1)} %slice.83), channel_id=1, source_target_pairs={{0,8},{8,16},{16,24},{24,28},{28,20},{20,12},{12,4},{4,0},{1,9},{9... | collective-permute-start | bytes 1179656 | tf_op jit(solution)/shard_map/ppermute | solution.py:194
  62.0 2.6 %project.9 = (bf16[768,256]{1,0:T(8,128)(2,1)S(1)}, bf16[768,256]{1,0:T(8,128)(2,1)S(1)}, bf16[256,3072]{1,0:T(8,128)(2,1)S(1)}) custom-call(s32[1]{0:T(128)} %bitcast.which_ref, bf16[768,3072]{1,0:T(8,128)(2,1)S(1)} %copy-done.3, bf16[768,3072]{1,0:T(8,128)(2,1)S(1)} %copy-done.1, bf16[128,3072]{1,0:T(8,128)(2,1)S(1)} %collective-permute-done.15.refs_0_, ...), custom_call_target="tpu_custom_call" | custom-call | flops 362387872 | tf_op jit(solution)/shard_map/project/pallas_call | solution.py:114
  64.8 1.6 %collective-permute-start.13 = (bf16[768,256]{1,0:T(8,128)(2,1)S(1)}, bf16[768,256]{1,0:T(8,128)(2,1)S(1)}, u32[]{:S(2)}, u32[]{:S(2)}) collective-permute-start(bf16[768,256]{1,0:T(8,128)(2,1)S(1)} %fusion.8), channel_id=1, source_target_pairs={{0,2},{1,3},{2,0},{3,1},{4,6},{5,7},{6,4},{7,5},{8,10},{9,11},{10,... | collective-permute-start | bytes 1179656 | tf_op jit(solution)/shard_map/ppermute | solution.py:188
  66.4 0.1 convert_add_fusion.4
  66.5 1.2 %collective-permute-done.21.refs_1_ = bf16[64,3072]{1,0:T(8,128)(2,1)S(1)} collective-permute-done((bf16[64,3072]{1,0:T(8,128)(2,1)S(1)}, bf16[64,3072]{1,0:T(8,128)(2,1)S(1)}, u32[]{:S(2)}, u32[]{:S(2)}) %collective-permute-start.21) | collective-permute-done | bytes 393248 | tf_op jit(solution)/shard_map/ppermute | solution.py:194
  67.7 0.5 collective-permute-done.20.refs_0_
  68.3 1.6 %collective-permute-start.18 = (bf16[768,256]{1,0:T(8,128)(2,1)S(1)}, bf16[768,256]{1,0:T(8,128)(2,1)S(1)}, u32[]{:S(2)}, u32[]{:S(2)}) collective-permute-start(bf16[768,256]{1,0:T(8,128)(2,1)S(1)} %fusion.9), channel_id=1, source_target_pairs={{0,2},{1,3},{2,0},{3,1},{4,6},{5,7},{6,4},{7,5},{8,10},{9,11},{10,... | collective-permute-start | bytes 1179656 | tf_op jit(solution)/shard_map/ppermute | solution.py:188
  69.9 1.4 %project.11 = (bf16[768,128]{1,0:T(8,128)(2,1)S(1)}, bf16[128,3072]{1,0:T(8,128)(2,1)S(1)}) custom-call(s32[1]{0:T(128)} %bitcast.which_ref, bf16[768,3072]{1,0:T(8,128)(2,1)S(1)} %copy-done.3, bf16[768,3072]{1,0:T(8,128)(2,1)S(1)} %copy-done.1, bf16[64,3072]{1,0:T(8,128)(2,1)S(1)} %collective-permute-done.20.refs_0_, ...), custom_call_target="tpu_custom_call" | custom-call | flops 181193936 | tf_op jit(solution)/shard_map/project/pallas_call | solution.py:114
  71.3 5.5 %collective-permute-done.13 = bf16[768,256]{1,0:T(8,128)(2,1)S(1)} collective-permute-done((bf16[768,256]{1,0:T(8,128)(2,1)S(1)}, bf16[768,256]{1,0:T(8,128)(2,1)S(1)}, u32[]{:S(2)}, u32[]{:S(2)}) %collective-permute-start.13) | collective-permute-done | bytes 393248 | tf_op jit(solution)/shard_map/ppermute | solution.py:188
  76.8 0.1 convert_add_fusion.2
  76.9 2.0 %project.10 = (bf16[768,128]{1,0:T(8,128)(2,1)S(1)}, bf16[128,3072]{1,0:T(8,128)(2,1)}) custom-call(s32[1]{0:T(128)} %bitcast.which_ref, bf16[768,3072]{1,0:T(8,128)(2,1)S(1)} %copy-done.3, bf16[768,3072]{1,0:T(8,128)(2,1)S(1)} %copy-done.1, bf16[64,3072]{1,0:T(8,128)(2,1)S(1)} %collective-permute-done.20.refs_0_, ...), custom_call_target="tpu_custom_call" | custom-call | flops 181193936 | tf_op jit(solution)/shard_map/project/pallas_call | solution.py:114
  79.0 1.6 %collective-permute-start.23 = (bf16[768,128]{1,0:T(8,128)(2,1)S(1)}, bf16[768,128]{1,0:T(8,128)(2,1)S(1)}, u32[]{:S(2)}, u32[]{:S(2)}) collective-permute-start(bf16[768,128]{1,0:T(8,128)(2,1)S(1)} %fusion.26), channel_id=1, source_target_pairs={{0,2},{1,3},{2,0},{3,1},{4,6},{5,7},{6,4},{7,5},{8,10},{9,11},{10,... | collective-permute-start | bytes 589832 | tf_op jit(solution)/shard_map/ppermute | solution.py:188
  80.5 4.7 %collective-permute-done.18 = bf16[768,256]{1,0:T(8,128)(2,1)S(1)} collective-permute-done((bf16[768,256]{1,0:T(8,128)(2,1)S(1)}, bf16[768,256]{1,0:T(8,128)(2,1)S(1)}, u32[]{:S(2)}, u32[]{:S(2)}) %collective-permute-start.18) | collective-permute-done | bytes 393248 | tf_op jit(solution)/shard_map/ppermute | solution.py:188
  85.2 0.1 convert_add_fusion
  85.3 0.4 fusion.10
  85.8 0.5 collective-permute-start.14
  86.4 2.6 %collective-permute-done.23 = bf16[768,128]{1,0:T(8,128)(2,1)S(1)} collective-permute-done((bf16[768,128]{1,0:T(8,128)(2,1)S(1)}, bf16[768,128]{1,0:T(8,128)(2,1)S(1)}, u32[]{:S(2)}, u32[]{:S(2)}) %collective-permute-start.23) | collective-permute-done | bytes 196640 | tf_op jit(solution)/shard_map/ppermute | solution.py:188
  89.1 0.1 fusion.27
  89.3 0.5 collective-permute-start.24
  89.8 0.8 collective-permute-done.4.refs_1_
  90.6 3.8 %contract.2.base_ref = f32[768,3072]{1,0:T(8,128)S(1)} custom-call(s32[1]{0:T(128)} %bitcast.which_ref, bf16[768,3072]{1,0:T(8,128)(2,1)S(1)} %bitcast.12, bf16[384,128]{1,0:T(8,128)(2,1)S(1)} %get-tuple-element.46.refs_0_, bf16[384,128]{1,0:T(8,128)(2,1)S(1)} %collective-permute-done.4.refs_1_, bf16[128,3072]{1,0:T(8,128)(2,1)S(1)} %copy-done.5, ...), custom_call_target="tpu_custom_call" | custom-call | flops 452984832 | tf_op jit(solution)/shard_map/contract/pallas_call | solution.py:165
  94.5 5.7 %contract.3 = f32[768,3072]{1,0:T(8,128)} custom-call(s32[1]{0:T(128)} %bitcast.which_ref, f32[768,3072]{1,0:T(8,128)S(1)} %contract.2.base_ref, bf16[384,256]{1,0:T(8,128)(2,1)S(1)} %get-tuple-element.47.refs_0_, bf16[384,256]{1,0:T(8,128)(2,1)S(1)} %collective-permute-done.19.refs_1_, bf16[256,3072]{1,0:T(8,128)(2,1)S(1)} %get-tuple-element.39.refs_2_, ...), custom_call_target="tpu_custom_call" | custom-call | flops 271790912 | tf_op jit(solution)/shard_map/contract/pallas_call | solution.py:165
  (57 shorter events, 1.7 us)
Async XLA Ops:
  0.0 20.7 %collective-permute-start.5 = (bf16[128,3072]{1,0:T(8,128)(2,1)}, bf16[128,3072]{1,0:T(8,128)(2,1)S(1)}, u32[]{:S(2)}, u32[]{:S(2)}) collective-permute-start(bf16[128,3072]{1,0:T(8,128)(2,1)} %refs_2_.1), channel_id=1, source_target_pairs={{0,8},{8,16},{16,24},{24,28},{28,20},{20,12},{12,4},{4,0},{1,9},{9... | collective-permute-start | bytes 2359304 | tf_op jit(solution)/shard_map/ppermute | solution.py:194
  3.0 19.5 %collective-permute-start.6 = (bf16[128,3072]{1,0:T(8,128)(2,1)}, bf16[128,3072]{1,0:T(8,128)(2,1)S(1)}, u32[]{:S(2)}, u32[]{:S(2)}) collective-permute-start(bf16[128,3072]{1,0:T(8,128)(2,1)} %refs_2_.1), channel_id=1, source_target_pairs={{0,4},{8,0},{16,8},{24,16},{28,24},{20,28},{12,20},{4,12},{1,5},{9... | collective-permute-start | bytes 2359304 | tf_op jit(solution)/shard_map/ppermute | solution.py:194
  4.1 27.9 %collective-permute-start.2 = (bf16[256,384]{1,0:T(8,128)(2,1)S(1)}, bf16[256,384]{1,0:T(8,128)(2,1)S(1)}, u32[]{:S(2)}, u32[]{:S(2)}) collective-permute-start(bf16[256,384]{1,0:T(8,128)(2,1)S(1)} %get-tuple-element.51), channel_id=1, source_target_pairs={{0,1},{1,0},{2,3},{3,2},{4,5},{5,4},{6,7},{7,6},{8,9},{9,8},{10,11... | collective-permute-start | bytes 589832 | tf_op jit(solution)/shard_map/ppermute | solution.py:188
  4.2 2.3 %copy-start = (bf16[768,3072]{1,0:T(8,128)(2,1)S(1)}, bf16[768,3072]{1,0:T(8,128)(2,1)}, u32[]{:S(2)}) copy-start(bf16[768,3072]{1,0:T(8,128)(2,1)} %d_ref.11) | copy-start | bytes 14155780
  6.5 2.3 %copy-start.2 = (bf16[768,3072]{1,0:T(8,128)(2,1)S(1)}, bf16[768,3072]{1,0:T(8,128)(2,1)}, u32[]{:S(2)}) copy-start(bf16[768,3072]{1,0:T(8,128)(2,1)} %w_ref.11) | copy-start | bytes 14155780
  8.8 1.1 %copy-start.4 = (bf16[128,3072]{1,0:T(8,128)(2,1)S(1)}, bf16[128,3072]{1,0:T(8,128)(2,1)}, u32[]{:S(2)}) copy-start(bf16[128,3072]{1,0:T(8,128)(2,1)} %refs_2_.1) | copy-start | bytes 2359300
  10.0 4.0 %copy-start.6 = (s32[4]{0:T(128)S(1)}, s32[4]{0:T(128)}, u32[]{:S(2)}) copy-start(s32[4]{0:T(128)} %param.11) | copy-start | bytes 52
  10.0 4.1 %copy-start.7 = (f32[4]{0:T(128)S(1)}, f32[4]{0:T(128)}, u32[]{:S(2)}) copy-start(f32[4]{0:T(128)} %param.12) | copy-start | bytes 52
  12.6 10.1 %collective-permute-start = (bf16[768,128]{1,0:T(8,128)(2,1)S(1)}, bf16[768,128]{1,0:T(8,128)(2,1)S(1)}, u32[]{:S(2)}, u32[]{:S(2)}) collective-permute-start(bf16[768,128]{1,0:T(8,128)(2,1)S(1)} %get-tuple-element.26), channel_id=1, source_target_pairs={{0,1},{1,0},{2,3},{3,2},{4,5},{5,4},{6,7},{7,6},{8,9},{9,8},{10,11... | collective-permute-start | bytes 589832 | tf_op jit(solution)/shard_map/ppermute | solution.py:188
  20.7 18.7 %collective-permute-start.10 = (bf16[128,3072]{1,0:T(8,128)(2,1)S(1)}, bf16[128,3072]{1,0:T(8,128)(2,1)S(1)}, u32[]{:S(2)}, u32[]{:S(2)}) collective-permute-start(bf16[128,3072]{1,0:T(8,128)(2,1)S(1)} %collective-permute-done.5.refs_0_), channel_id=1, source_target_pairs={{0,8},{8,16},{16,24},{24,28},{28,20},{20,12},{12,4},{4,0},{1,9},{9... | collective-permute-start | bytes 2359304 | tf_op jit(solution)/shard_map/ppermute | solution.py:194
  22.5 18.1 %collective-permute-start.11 = (bf16[128,3072]{1,0:T(8,128)(2,1)S(1)}, bf16[128,3072]{1,0:T(8,128)(2,1)S(1)}, u32[]{:S(2)}, u32[]{:S(2)}) collective-permute-start(bf16[128,3072]{1,0:T(8,128)(2,1)S(1)} %collective-permute-done.6.refs_1_), channel_id=1, source_target_pairs={{0,4},{8,0},{16,8},{24,16},{28,24},{20,28},{12,20},{4,12},{1,5},{9... | collective-permute-start | bytes 2359304 | tf_op jit(solution)/shard_map/ppermute | solution.py:194
  22.8 19.9 %collective-permute-start.1 = (bf16[768,128]{1,0:T(8,128)(2,1)S(1)}, bf16[768,128]{1,0:T(8,128)(2,1)S(1)}, u32[]{:S(2)}, u32[]{:S(2)}) collective-permute-start(bf16[768,128]{1,0:T(8,128)(2,1)S(1)} %fusion.25), channel_id=1, source_target_pairs={{0,2},{1,3},{2,0},{3,1},{4,6},{5,7},{6,4},{7,5},{8,10},{9,11},{10,... | collective-permute-start | bytes 589832 | tf_op jit(solution)/shard_map/ppermute | solution.py:188
  24.6 2.3 %copy-start.1 = (bf16[768,3072]{1,0:T(8,128)(2,1)S(1)}, bf16[768,3072]{1,0:T(8,128)(2,1)}, u32[]{:S(2)}) copy-start(bf16[768,3072]{1,0:T(8,128)(2,1)} %d_ref.11) | copy-start | bytes 14155780
  27.0 2.3 %copy-start.3 = (bf16[768,3072]{1,0:T(8,128)(2,1)S(1)}, bf16[768,3072]{1,0:T(8,128)(2,1)}, u32[]{:S(2)}) copy-start(bf16[768,3072]{1,0:T(8,128)(2,1)} %w_ref.11) | copy-start | bytes 14155780
  31.9 13.6 %collective-permute-start.7 = (bf16[768,256]{1,0:T(8,128)(2,1)S(1)}, bf16[768,256]{1,0:T(8,128)(2,1)S(1)}, u32[]{:S(2)}, u32[]{:S(2)}) collective-permute-start(bf16[768,256]{1,0:T(8,128)(2,1)S(1)} %get-tuple-element.28), channel_id=1, source_target_pairs={{0,1},{1,0},{2,3},{3,2},{4,5},{5,4},{6,7},{7,6},{8,9},{9,8},{10,11... | collective-permute-start | bytes 1179656 | tf_op jit(solution)/shard_map/ppermute | solution.py:188
  32.1 15.1 %collective-permute-start.3 = (bf16[512,384]{1,0:T(8,128)(2,1)S(1)}, bf16[512,384]{1,0:T(8,128)(2,1)S(1)}, u32[]{:S(2)}, u32[]{:S(2)}) collective-permute-start(bf16[512,384]{1,0:T(8,128)(2,1)S(1)} %pad_maximum_fusion), channel_id=1, source_target_pairs={{0,2},{1,3},{2,0},{3,1},{4,6},{5,7},{6,4},{7,5},{8,10},{9,11},{10,... | collective-permute-start | bytes 1179656 | tf_op jit(solution)/shard_map/ppermute | solution.py:188
  40.7 17.2 %collective-permute-start.15 = (bf16[128,3072]{1,0:T(8,128)(2,1)S(1)}, bf16[128,3072]{1,0:T(8,128)(2,1)S(1)}, u32[]{:S(2)}, u32[]{:S(2)}) collective-permute-start(bf16[128,3072]{1,0:T(8,128)(2,1)S(1)} %collective-permute-done.10.refs_0_), channel_id=1, source_target_pairs={{0,8},{8,16},{16,24},{24,28},{28,20},{20,12},{12,4},{4,0},{1,9},{9... | collective-permute-start | bytes 2359304 | tf_op jit(solution)/shard_map/ppermute | solution.py:194
  42.2 17.6 %collective-permute-start.16 = (bf16[128,3072]{1,0:T(8,128)(2,1)S(1)}, bf16[128,3072]{1,0:T(8,128)(2,1)S(1)}, u32[]{:S(2)}, u32[]{:S(2)}) collective-permute-start(bf16[128,3072]{1,0:T(8,128)(2,1)S(1)} %collective-permute-done.11.refs_1_), channel_id=1, source_target_pairs={{0,4},{8,0},{16,8},{24,16},{28,24},{20,28},{12,20},{4,12},{1,5},{9... | collective-permute-start | bytes 2359304 | tf_op jit(solution)/shard_map/ppermute | solution.py:194
  45.4 19.3 %collective-permute-start.12 = (bf16[768,256]{1,0:T(8,128)(2,1)S(1)}, bf16[768,256]{1,0:T(8,128)(2,1)S(1)}, u32[]{:S(2)}, u32[]{:S(2)}) collective-permute-start(bf16[768,256]{1,0:T(8,128)(2,1)S(1)} %get-tuple-element.33), channel_id=1, source_target_pairs={{0,1},{1,0},{2,3},{3,2},{4,5},{5,4},{6,7},{7,6},{8,9},{9,8},{10,11... | collective-permute-start | bytes 1179656 | tf_op jit(solution)/shard_map/ppermute | solution.py:188
  45.6 20.8 %collective-permute-start.8 = (bf16[768,256]{1,0:T(8,128)(2,1)S(1)}, bf16[768,256]{1,0:T(8,128)(2,1)S(1)}, u32[]{:S(2)}, u32[]{:S(2)}) collective-permute-start(bf16[768,256]{1,0:T(8,128)(2,1)S(1)} %fusion.7), channel_id=1, source_target_pairs={{0,2},{1,3},{2,0},{3,1},{4,6},{5,7},{6,4},{7,5},{8,10},{9,11},{10,... | collective-permute-start | bytes 1179656 | tf_op jit(solution)/shard_map/ppermute | solution.py:188
  59.9 7.8 %collective-permute-start.21 = (bf16[64,3072]{1,0:T(8,128)(2,1)S(1)}, bf16[64,3072]{1,0:T(8,128)(2,1)S(1)}, u32[]{:S(2)}, u32[]{:S(2)}) collective-permute-start(bf16[64,3072]{1,0:T(8,128)(2,1)S(1)} %slice.84), channel_id=1, source_target_pairs={{0,4},{8,0},{16,8},{24,16},{28,24},{20,28},{12,20},{4,12},{1,5},{9... | collective-permute-start | bytes 1179656 | tf_op jit(solution)/shard_map/ppermute | solution.py:194
  60.4 7.8 %collective-permute-start.20 = (bf16[64,3072]{1,0:T(8,128)(2,1)S(1)}, bf16[64,3072]{1,0:T(8,128)(2,1)S(1)}, u32[]{:S(2)}, u32[]{:S(2)}) collective-permute-start(bf16[64,3072]{1,0:T(8,128)(2,1)S(1)} %slice.83), channel_id=1, source_target_pairs={{0,8},{8,16},{16,24},{24,28},{28,20},{20,12},{12,4},{4,0},{1,9},{9... | collective-permute-start | bytes 1179656 | tf_op jit(solution)/shard_map/ppermute | solution.py:194
  64.6 3.6 %collective-permute-start.17 = (bf16[768,256]{1,0:T(8,128)(2,1)S(1)}, bf16[768,256]{1,0:T(8,128)(2,1)S(1)}, u32[]{:S(2)}, u32[]{:S(2)}) collective-permute-start(bf16[768,256]{1,0:T(8,128)(2,1)S(1)} %get-tuple-element.38), channel_id=1, source_target_pairs={{0,1},{1,0},{2,3},{3,2},{4,5},{5,4},{6,7},{7,6},{8,9},{9,8},{10,11... | collective-permute-start | bytes 1179656 | tf_op jit(solution)/shard_map/ppermute | solution.py:188
  64.8 12.0 %collective-permute-start.13 = (bf16[768,256]{1,0:T(8,128)(2,1)S(1)}, bf16[768,256]{1,0:T(8,128)(2,1)S(1)}, u32[]{:S(2)}, u32[]{:S(2)}) collective-permute-start(bf16[768,256]{1,0:T(8,128)(2,1)S(1)} %fusion.8), channel_id=1, source_target_pairs={{0,2},{1,3},{2,0},{3,1},{4,6},{5,7},{6,4},{7,5},{8,10},{9,11},{10,... | collective-permute-start | bytes 1179656 | tf_op jit(solution)/shard_map/ppermute | solution.py:188
  68.3 16.9 %collective-permute-start.18 = (bf16[768,256]{1,0:T(8,128)(2,1)S(1)}, bf16[768,256]{1,0:T(8,128)(2,1)S(1)}, u32[]{:S(2)}, u32[]{:S(2)}) collective-permute-start(bf16[768,256]{1,0:T(8,128)(2,1)S(1)} %fusion.9), channel_id=1, source_target_pairs={{0,2},{1,3},{2,0},{3,1},{4,6},{5,7},{6,4},{7,5},{8,10},{9,11},{10,... | collective-permute-start | bytes 1179656 | tf_op jit(solution)/shard_map/ppermute | solution.py:188
  71.2 7.7 %collective-permute-start.22 = (bf16[768,128]{1,0:T(8,128)(2,1)S(1)}, bf16[768,128]{1,0:T(8,128)(2,1)S(1)}, u32[]{:S(2)}, u32[]{:S(2)}) collective-permute-start(bf16[768,128]{1,0:T(8,128)(2,1)S(1)} %get-tuple-element.43), channel_id=1, source_target_pairs={{0,1},{1,0},{2,3},{3,2},{4,5},{5,4},{6,7},{7,6},{8,9},{9,8},{10,11... | collective-permute-start | bytes 589832 | tf_op jit(solution)/shard_map/ppermute | solution.py:188
  76.8 13.8 %slice-start = ((s8[4718592]{0:T(1024)(128)(4,1)}), s8[4194304]{0:T(1024)(128)(4,1)S(1)}, s32[]{:S(2)}) async-start(s8[4718592]{0:T(1024)(128)(4,1)} %bitcast.11), calls=%async_computation | async-start | bytes 8388608
  76.9 13.7 %slice-start.1 = ((s8[4718592]{0:T(1024)(128)(4,1)}), s8[524288]{0:T(1024)(128)(4,1)S(1)}, s32[]{:S(2)}) async-start(s8[4718592]{0:T(1024)(128)(4,1)} %bitcast.11), calls=%async_computation.1 | async-start | bytes 1048576
  79.0 10.1 %collective-permute-start.23 = (bf16[768,128]{1,0:T(8,128)(2,1)S(1)}, bf16[768,128]{1,0:T(8,128)(2,1)S(1)}, u32[]{:S(2)}, u32[]{:S(2)}) collective-permute-start(bf16[768,128]{1,0:T(8,128)(2,1)S(1)} %fusion.26), channel_id=1, source_target_pairs={{0,2},{1,3},{2,0},{3,1},{4,6},{5,7},{6,4},{7,5},{8,10},{9,11},{10,... | collective-permute-start | bytes 589832 | tf_op jit(solution)/shard_map/ppermute | solution.py:188
  85.7 4.9 %copy-start.5 = (bf16[128,3072]{1,0:T(8,128)(2,1)S(1)}, bf16[128,3072]{1,0:T(8,128)(2,1)}, u32[]{:S(2)}) copy-start(bf16[128,3072]{1,0:T(8,128)(2,1)} %refs_2_.1) | copy-start | bytes 2359300
  85.7 8.7 %collective-permute-start.19 = (bf16[384,256]{1,0:T(8,128)(2,1)S(1)}, bf16[384,256]{1,0:T(8,128)(2,1)S(1)}, u32[]{:S(2)}, u32[]{:S(2)}) collective-permute-start(bf16[384,256]{1,0:T(8,128)(2,1)S(1)} %get-tuple-element.47.refs_0_), channel_id=1, source_target_pairs={{0,1},{1,0},{2,3},{3,2},{4,5},{5,4},{6,7},{7,6},{8,9},{9,8},{10,11... | collective-permute-start | bytes 589832 | tf_op jit(solution)/shard_map/ppermute | solution.py:188
  85.8 4.7 %collective-permute-start.14 = (bf16[384,256]{1,0:T(8,128)(2,1)S(1)}, bf16[384,256]{1,0:T(8,128)(2,1)S(1)}, u32[]{:S(2)}, u32[]{:S(2)}) collective-permute-start(bf16[384,256]{1,0:T(8,128)(2,1)S(1)} %get-tuple-element.48.refs_6_), channel_id=1, source_target_pairs={{0,1},{1,0},{2,3},{3,2},{4,5},{5,4},{6,7},{7,6},{8,9},{9,8},{10,11... | collective-permute-start | bytes 589832 | tf_op jit(solution)/shard_map/ppermute | solution.py:188
  86.3 4.2 %collective-permute-start.9 = (bf16[384,256]{1,0:T(8,128)(2,1)S(1)}, bf16[384,256]{1,0:T(8,128)(2,1)S(1)}, u32[]{:S(2)}, u32[]{:S(2)}) collective-permute-start(bf16[384,256]{1,0:T(8,128)(2,1)S(1)} %get-tuple-element.49.refs_3_), channel_id=1, source_target_pairs={{0,1},{1,0},{2,3},{3,2},{4,5},{5,4},{6,7},{7,6},{8,9},{9,8},{10,11... | collective-permute-start | bytes 589832 | tf_op jit(solution)/shard_map/ppermute | solution.py:188
  89.2 1.4 %collective-permute-start.4 = (bf16[384,128]{1,0:T(8,128)(2,1)S(1)}, bf16[384,128]{1,0:T(8,128)(2,1)S(1)}, u32[]{:S(2)}, u32[]{:S(2)}) collective-permute-start(bf16[384,128]{1,0:T(8,128)(2,1)S(1)} %get-tuple-element.46.refs_0_), channel_id=1, source_target_pairs={{0,1},{1,0},{2,3},{3,2},{4,5},{5,4},{6,7},{7,6},{8,9},{9,8},{10,11... | collective-permute-start | bytes 294920 | tf_op jit(solution)/shard_map/ppermute | solution.py:188
  89.3 5.2 %collective-permute-start.24 = (bf16[384,128]{1,0:T(8,128)(2,1)S(1)}, bf16[384,128]{1,0:T(8,128)(2,1)S(1)}, u32[]{:S(2)}, u32[]{:S(2)}) collective-permute-start(bf16[384,128]{1,0:T(8,128)(2,1)S(1)} %get-tuple-element.45.refs_3_), channel_id=1, source_target_pairs={{0,1},{1,0},{2,3},{3,2},{4,5},{5,4},{6,7},{7,6},{8,9},{9,8},{10,11... | collective-permute-start | bytes 294920 | tf_op jit(solution)/shard_map/ppermute | solution.py:188

commit v3 on v2

--- a/solution.py
+++ b/solution.py
@@ -123,53 +123,52 @@
     )(core, w_out, direction, *parts)
 
 
-def contract_kernel(count, step, tile, which_ref, base_ref, *refs):
+def contract_kernel(count, step, tile, last, which_ref, base_ref, *refs):
     terms, out = [refs[3 * i : 3 * i + 3] for i in range(count)], refs[3 * count]
     width, depth = base_ref.shape
     part = width // 2
-    first = base_ref.dtype == jnp.bfloat16
-    if not first:
+    tiles = depth // tile
+    if last:
         buffer, sem = refs[3 * count + 1 :]
 
     def copy_of(i):
-        columns = pl.ds(pl.multiple_of(i * tile, tile), tile)
-        return pltpu.make_async_copy(buffer.at[i % 2], out.at[:, columns], sem.at[i % 2])
-
-    for i in range(depth // tile):
+        return pltpu.make_async_copy(buffer.at[i], out.at[:, i * tile : (i + 1) * tile], sem.at[i])
+
+    for i in range(tiles):
         columns = slice(i * tile, (i + 1) * tile)
-        if not first and i >= 2:
-            copy_of(i - 2).wait()
         for flip in (0, 1):
             which = which_ref[0] if flip == 0 else 1 - which_ref[0]
             rows = pl.ds(pl.multiple_of(which * part, part), part)
             total = sum(
                 jnp.dot(term[flip][...], term[2][:, columns], preferred_element_type=jnp.float32) for term in terms
             )
-            if first:
-                out[rows, columns] = 2.0 * base_ref[rows, columns].astype(jnp.float32) - step * total
+            base = base_ref[rows, columns]
+            if base.dtype == jnp.bfloat16:
+                base = 2.0 * base.astype(jnp.float32)
+            if last:
+                buffer[i, rows, :] = base - step * total
             else:
-                buffer[i % 2, rows, :] = base_ref[rows, columns] - step * total
-        if not first:
+                out[rows, columns] = base - step * total
+        if last:
             copy_of(i).start()
-    if not first:
-        for i in range(max(0, depth // tile - 2), depth // tile):
+    if last:
+        for i in range(tiles):
             copy_of(i).wait()
 
 
-def contract(core, base, terms, step):
+def contract(core, base, terms, step, last):
     width, depth = base.shape
-    first = base.dtype == jnp.bfloat16
     tile = 512
     while depth % tile:
         tile //= 2
+    tiles = depth // tile
     return pl.pallas_call(
-        functools.partial(contract_kernel, len(terms), step, tile),
+        functools.partial(contract_kernel, len(terms), step, tile, last),
         out_shape=jax.ShapeDtypeStruct((width, depth), jnp.float32),
         in_specs=[pl.BlockSpec(memory_space=pltpu.SMEM)] + [IN_VMEM] * (1 + 3 * len(terms)),
-        out_specs=IN_VMEM if first else pl.BlockSpec(memory_space=pl.ANY),
-        scratch_shapes=[]
-        if first
-        else [pltpu.VMEM((2, width, tile), jnp.float32), pltpu.SemaphoreType.DMA((2,))],
+        out_specs=pl.BlockSpec(memory_space=pl.ANY) if last else IN_VMEM,
+        scratch_shapes=[pltpu.VMEM((tiles, width, tile), jnp.float32), pltpu.SemaphoreType.DMA((tiles,))] if last else [],
+        input_output_aliases={1: 0} if base.dtype == jnp.float32 and not last else {},
         compiler_params=pltpu.CompilerParams(vmem_limit_bytes=20 * 2**20),
         cost_estimate=cost(2 * width * depth * sum(term[2].shape[0] for term in terms)),
         name="contract",
@@ -214,8 +213,10 @@
     source = (image ^ mp) * PATCHES + row * GRID + col
     one_hot = (jnp.arange(tokens_all, dtype=jnp.int32)[:, None] == source).astype(jnp.bfloat16)
 
-    aligned = contract_rows(jnp.concatenate([two, other], axis=0), one_hot)
     one = core[None]
+
+    def align(other):
+        return contract_rows(jnp.concatenate([two, other], axis=0), one_hot)
 
     def add(kept, theirs):
         return kept.astype(jnp.float32) + theirs.astype(jnp.float32)
@@ -223,7 +224,7 @@
     def over_rows(chip):
         return swap(chip.astype(jnp.bfloat16), ROW)
 
-    def weigh(chip, across, start):
+    def weigh(aligned, chip, across, start):
         sums = add(chip, across)
         at = slice(start, start + sums.shape[1])
         slope = 1.0 - jnp.tanh(sums[:part] - aligned[:, at]) ** 2
@@ -239,29 +240,37 @@
     theirs1, kept1, block1 = project(one, w_out, direction, hop1, (1, 0))
     chip1 = add(kept1, swap(theirs1, CORE))
     across1 = over_rows(chip1)
-    *hop2, kept1 = gate(*hop2, kept1)
+    *hop2, kept1, chip0, across0, other = gate(*hop2, kept1, chip0, across0, other)
+    aligned = align(other)
     hop3 = step(hop2)
     theirs2, kept2, block2 = project(one, w_out, direction, hop2, (1, 0))
     chip2 = add(kept2, swap(theirs2, CORE))
     across2 = over_rows(chip2)
-    scaled0 = weigh(chip0, across0, 0)
-    *hop3, kept2 = gate(*hop3, kept2)
+    scaled0 = weigh(aligned, chip0, across0, 0)
+    *hop3, kept2, chip1, across1 = gate(*hop3, kept2, chip1, across1)
     hop4 = step((hop3[0][:half], hop3[1][half:]))
     theirs3, kept3, block3 = project(one, w_out, direction, hop3, (1, 0))
-    chip3 = add(kept3, swap(theirs3, CORE))
+    theirs3 = swap(theirs3, CORE)
+    scaled1 = weigh(aligned, chip1, across1, rows)
+    *hop4, kept3, chip2, across2 = gate(*hop4, kept3, chip2, across2)
+    scaled2 = weigh(aligned, chip2, across2, 3 * rows)
+    theirs3, mine2 = gate(theirs3, scaled2[0])
+    scaled2 = (mine2, scaled2[1])
+    chip3 = add(kept3, theirs3)
     across3 = over_rows(chip3)
-    scaled1 = weigh(chip1, across1, rows)
-    *hop4, kept3 = gate(*hop4, kept3)
     theirs4, block4 = project(one, w_out, direction, hop4, (1,))
     theirs4 = swap(theirs4, CORE)
     kept4, _ = project(one, w_out, direction, hop4, (0,))
     chip4 = add(kept4, theirs4)
     across4 = over_rows(chip4)
-    scaled2 = weigh(chip2, across2, 3 * rows)
-    total = contract(one, direction, [(*scaled0, hidden), (*scaled1, block1), (*scaled2, block2)], STEP / tokens_all)
-    scaled3 = weigh(chip3, across3, 5 * rows)
-    scaled4 = weigh(chip4, across4, 7 * rows)
-    return contract(one, total, [(*scaled3, block3), (*scaled4, block4)], STEP / tokens_all)
+    share = STEP / tokens_all
+    block2, chip4 = gate(block2, chip4)
+    total = contract(one, direction, [(*scaled0, hidden), (*scaled1, block1), (*scaled2, block2)], share, False)
+    total, chip3 = gate(total, chip3)
+    scaled3 = weigh(aligned, chip3, across3, 5 * rows)
+    mine3, chip4 = gate(scaled3[0], chip4)
+    scaled4 = weigh(aligned, chip4, across4, 7 * rows)
+    return contract(one, total, [(mine3, scaled3[1], block3), (*scaled4, block4)], share, True)
 
 
 def solution(mesh):

time: 101 us -> 89 us (0.88)
  waiting for transfers between devices: 41.4 us -> 33.6 us
  starting transfers between devices: 19.8 us -> 17.7 us
  Pallas kernels: 23.4 us -> 21.9 us
    ppermute x8, waiting for transfers between devices: 27.9 us -> 14.5 us  [step(): return (lax.ppermute(pair[0], 'dp', UP), lax.ppermute(pair[1], 'dp', DOWN))]
    ppermute x17, waiting for transfers between devices: 13.5 us -> 19.1 us  [swap(): return lax.ppermute(value, 'mp', pairs)]
    ppermute x17, starting transfers between devices: 10.6 us -> 8.58 us  [swap(): return lax.ppermute(value, 'mp', pairs)]
    pallas_call x2, Pallas kernels: 9.51 us -> 8.08 us  [contract(): pl.pallas_call(functools.partial(contract_kernel, len(terms), step, tile,...]
  transfers between devices with their start and end apart: 25 -> 25, of which waited for: 11 -> 12; matrix products, arithmetic and copies ran while one was open for 5% -> 5% of each run, Pallas kernels for 18% -> 20%
where the time goes in v3:
time: 89 us; the launch traced here: 88.7 us
  waiting for transfers between devices  33.6 us (38%)
  Pallas kernels  21.9 us (25%)
  starting transfers between devices  17.7 us (20%)
  local copies, waits for them, and re-layouts  11.7 us (13%)
  other arithmetic  2.17 us (2%)
  matrix products  1.07 us (1%)
    ppermute x17, waiting for transfers between devices, swap(): return lax.ppermute(value, 'mp', pairs)  19.1 us
    ppermute x8, waiting for transfers between devices, step(): return (lax.ppermute(pair[0], 'dp', UP), lax.ppermute(pair[1], 'dp', DOWN))  14.5 us
    pallas_call x6, Pallas kernels, project(): pl.pallas_call(functools.partial(project_kernel, wanted, len(parts)), out...  13.8 us
    unnamed x20, local copies, waits for them, and re-layouts  10.5 us
    ppermute x8, starting transfers between devices, step(): return (lax.ppermute(pair[0], 'dp', UP), lax.ppermute(pair[1], 'dp', DOWN))  9.16 us
    ppermute x17, starting transfers between devices, swap(): return lax.ppermute(value, 'mp', pairs)  8.58 us
    pallas_call x2, Pallas kernels, contract(): pl.pallas_call(functools.partial(contract_kernel, len(terms), step, tile,...  8.08 us
  transfers between devices with their start and end apart: 25, of which 12 were waited for; matrix products, arithmetic and copies ran while one was open for 5% of the time, Pallas kernels for 20%

profile of v3, /device:TPU:0, one launch (start us, length us, event | category | flops | bytes accessed | tf_op | source)
XLA Modules:
  0.0 88.7 jit_solution(9206931573550207898)
XLA Ops:
  0.0 2.9 %collective-permute-start.2 = (bf16[128,3072]{1,0:T(8,128)(2,1)}, bf16[128,3072]{1,0:T(8,128)(2,1)S(1)}, u32[]{:S(2)}, u32[]{:S(2)}) collective-permute-start(bf16[128,3072]{1,0:T(8,128)(2,1)} %refs_2_.1), channel_id=1, source_target_pairs={{0,4},{8,0},{16,8},{24,16},{28,24},{20,28},{12,20},{4,12},{1,5},{9... | collective-permute-start | bytes 2359304 | tf_op jit(solution)/shard_map/ppermute | solution.py:193
  3.0 1.1 %constant_dynamic-slice_fusion = (bf16[256,384]{1,0:T(8,128)(2,1)S(1)}, bf16[256,384]{1,0:T(8,128)(2,1)S(1)}) fusion(bf16[256,768]{1,0:T(8,128)(2,1)} %param.10, s32[]{:T(128)S(6)} %select_n.103, s32[]{:T(128)S(6)} %select_n.104), kind=kLoop, calls=%fused_computation.92 | loop fusion | bytes 786440 | tf_op jit(solution)/shard_map/dynamic_slice | solution.py:196
  4.2 2.3 %copy-done = bf16[768,3072]{1,0:T(8,128)(2,1)S(1)} copy-done((bf16[768,3072]{1,0:T(8,128)(2,1)S(1)}, bf16[768,3072]{1,0:T(8,128)(2,1)}, u32[]{:S(2)}) %copy-start) | copy-done | bytes 4718616
  6.5 2.3 %copy-done.2 = bf16[768,3072]{1,0:T(8,128)(2,1)S(1)} copy-done((bf16[768,3072]{1,0:T(8,128)(2,1)S(1)}, bf16[768,3072]{1,0:T(8,128)(2,1)}, u32[]{:S(2)}) %copy-start.2) | copy-done | bytes 4718616
  8.9 1.1 %copy-done.4 = bf16[128,3072]{1,0:T(8,128)(2,1)S(1)} copy-done((bf16[128,3072]{1,0:T(8,128)(2,1)S(1)}, bf16[128,3072]{1,0:T(8,128)(2,1)}, u32[]{:S(2)}) %copy-start.4) | copy-done | bytes 786456
  10.0 2.6 %project.7 = (bf16[768,128]{1,0:T(8,128)(2,1)S(1)}, bf16[768,128]{1,0:T(8,128)(2,1)S(1)}, bf16[128,3072]{1,0:T(8,128)(2,1)}) custom-call(s32[1]{0:T(128)} %bitcast.which_ref, bf16[768,3072]{1,0:T(8,128)(2,1)S(1)} %copy-done.2, bf16[768,3072]{1,0:T(8,128)(2,1)S(1)} %copy-done, bf16[128,3072]{1,0:T(8,128)(2,1)S(1)} %copy-done.4), custom_call_target="tpu_custom_call" | custom-call | flops 362387872 | tf_op jit(solution)/shard_map/project/pallas_call | solution.py:114
  12.6 0.6 collective-permute-start.4
  13.1 0.7 fusion.46
  14.2 6.6 %collective-permute-done.2.refs_1_ = bf16[128,3072]{1,0:T(8,128)(2,1)S(1)} collective-permute-done((bf16[128,3072]{1,0:T(8,128)(2,1)}, bf16[128,3072]{1,0:T(8,128)(2,1)S(1)}, u32[]{:S(2)}, u32[]{:S(2)}) %collective-permute-start.2) | collective-permute-done | bytes 786464 | tf_op jit(solution)/shard_map/ppermute | solution.py:193
  20.8 1.7 %collective-permute-start.3 = (bf16[128,3072]{1,0:T(8,128)(2,1)S(1)}, bf16[128,3072]{1,0:T(8,128)(2,1)S(1)}, u32[]{:S(2)}, u32[]{:S(2)}) collective-permute-start(bf16[128,3072]{1,0:T(8,128)(2,1)S(1)} %collective-permute-done.2.refs_1_), channel_id=1, source_target_pairs={{0,4},{8,0},{16,8},{24,16},{28,24},{20,28},{12,20},{4,12},{1,5},{9... | collective-permute-start | bytes 2359304 | tf_op jit(solution)/shard_map/ppermute | solution.py:193
  22.4 0.4 collective-permute-start.1
  22.9 1.8 %collective-permute-start.7 = (bf16[512,384]{1,0:T(8,128)(2,1)S(1)}, bf16[512,384]{1,0:T(8,128)(2,1)S(1)}, u32[]{:S(2)}, u32[]{:S(2)}) collective-permute-start(bf16[512,384]{1,0:T(8,128)(2,1)S(1)} %pad_maximum_fusion), channel_id=1, source_target_pairs={{0,2},{1,3},{2,0},{3,1},{4,6},{5,7},{6,4},{7,5},{8,10},{9,11},{10,... | collective-permute-start | bytes 1179656 | tf_op jit(solution)/shard_map/ppermute | solution.py:187
  24.6 2.3 %copy-done.1 = bf16[768,3072]{1,0:T(8,128)(2,1)S(1)} copy-done((bf16[768,3072]{1,0:T(8,128)(2,1)S(1)}, bf16[768,3072]{1,0:T(8,128)(2,1)}, u32[]{:S(2)}) %copy-start.1) | copy-done | bytes 4718616
  26.9 2.3 %copy-done.3 = bf16[768,3072]{1,0:T(8,128)(2,1)S(1)} copy-done((bf16[768,3072]{1,0:T(8,128)(2,1)S(1)}, bf16[768,3072]{1,0:T(8,128)(2,1)}, u32[]{:S(2)}) %copy-start.3) | copy-done | bytes 4718616
  29.3 2.6 %project.6 = (bf16[768,256]{1,0:T(8,128)(2,1)S(1)}, bf16[768,256]{1,0:T(8,128)(2,1)S(1)}, bf16[256,3072]{1,0:T(8,128)(2,1)S(1)}) custom-call(s32[1]{0:T(128)} %bitcast.which_ref, bf16[768,3072]{1,0:T(8,128)(2,1)S(1)} %copy-done.3, bf16[768,3072]{1,0:T(8,128)(2,1)S(1)} %copy-done.1, bf16[128,3072]{1,0:T(8,128)(2,1)S(1)} %collective-permute-done.refs_0_, ...), custom_call_target="tpu_custom_call" | custom-call | flops 362387872 | tf_op jit(solution)/shard_map/project/pallas_call | solution.py:114
  32.1 0.4 collective-permute-start.5
  32.5 7.0 %collective-permute-done.5 = bf16[768,128]{1,0:T(8,128)(2,1)S(1)} collective-permute-done((bf16[768,128]{1,0:T(8,128)(2,1)S(1)}, bf16[768,128]{1,0:T(8,128)(2,1)S(1)}, u32[]{:S(2)}, u32[]{:S(2)}) %collective-permute-start.5) | collective-permute-done | bytes 196640 | tf_op jit(solution)/shard_map/ppermute | solution.py:187
  39.5 1.1 %collective-permute-done.1.refs_0_ = bf16[128,3072]{1,0:T(8,128)(2,1)S(1)} collective-permute-done((bf16[128,3072]{1,0:T(8,128)(2,1)S(1)}, bf16[128,3072]{1,0:T(8,128)(2,1)S(1)}, u32[]{:S(2)}, u32[]{:S(2)}) %collective-permute-start.1) | collective-permute-done | bytes 786464 | tf_op jit(solution)/shard_map/ppermute | solution.py:193
  40.6 0.7 collective-permute-start.9
  41.3 1.3 %collective-permute-start.10 = (bf16[128,3072]{1,0:T(8,128)(2,1)S(1)}, bf16[128,3072]{1,0:T(8,128)(2,1)S(1)}, u32[]{:S(2)}, u32[]{:S(2)}) collective-permute-start(bf16[128,3072]{1,0:T(8,128)(2,1)S(1)} %collective-permute-done.3.refs_1_), channel_id=1, source_target_pairs={{0,4},{8,0},{16,8},{24,16},{28,24},{20,28},{12,20},{4,12},{1,5},{9... | collective-permute-start | bytes 2359304 | tf_op jit(solution)/shard_map/ppermute | solution.py:193
  42.6 2.6 %project.8 = (bf16[768,256]{1,0:T(8,128)(2,1)S(1)}, bf16[768,256]{1,0:T(8,128)(2,1)S(1)}, bf16[256,3072]{1,0:T(8,128)(2,1)S(1)}) custom-call(s32[1]{0:T(128)} %bitcast.which_ref, bf16[768,3072]{1,0:T(8,128)(2,1)S(1)} %copy-done.3, bf16[768,3072]{1,0:T(8,128)(2,1)S(1)} %copy-done.1, bf16[128,3072]{1,0:T(8,128)(2,1)S(1)} %collective-permute-done.1.refs_0_, ...), custom_call_target="tpu_custom_call" | custom-call | flops 362387872 | tf_op jit(solution)/shard_map/project/pallas_call | solution.py:114
  45.3 0.1 fusion.50
  45.4 1.6 %collective-permute-start.12 = (bf16[768,256]{1,0:T(8,128)(2,1)S(1)}, bf16[768,256]{1,0:T(8,128)(2,1)S(1)}, u32[]{:S(2)}, u32[]{:S(2)}) collective-permute-start(bf16[768,256]{1,0:T(8,128)(2,1)S(1)} %get-tuple-element.83), channel_id=1, source_target_pairs={{0,2},{1,3},{2,0},{3,1},{4,6},{5,7},{6,4},{7,5},{8,10},{9,11},{10,... | collective-permute-start | bytes 1179656 | tf_op jit(solution)/shard_map/ppermute | solution.py:187
  47.0 1.1 %fusion = f32[384,1024]{1,0:T(8,128)S(1)} fusion(s32[1024]{0:T(1024)S(1)} %fusion.35, bf16[512,384]{1,0:T(8,128)(2,1)S(1)} %collective-permute-done.7, bf16[256,384]{1,0:T(8,128)(2,1)S(1)} %collective-permute-done.6, bf16[256,384]{1,0:T(8,128)(2,1)S(1)} %get-tuple-element.87), kind=kOutput, calls=%fused_computation.1 | convolution fusion | flops 808714240 | bytes 2363392 | tf_op jit(solution)/shard_map/dot_general | solution.py:18
  48.1 0.1 fusion.51
  48.2 0.6 collective-permute-start.18
  48.8 8.6 %collective-permute-done.12 = bf16[768,256]{1,0:T(8,128)(2,1)S(1)} collective-permute-done((bf16[768,256]{1,0:T(8,128)(2,1)S(1)}, bf16[768,256]{1,0:T(8,128)(2,1)S(1)}, u32[]{:S(2)}, u32[]{:S(2)}) %collective-permute-start.12) | collective-permute-done | bytes 393248 | tf_op jit(solution)/shard_map/ppermute | solution.py:187
  57.4 1.3 %collective-permute-done.9.refs_0_ = bf16[128,3072]{1,0:T(8,128)(2,1)S(1)} collective-permute-done((bf16[128,3072]{1,0:T(8,128)(2,1)S(1)}, bf16[128,3072]{1,0:T(8,128)(2,1)S(1)}, u32[]{:S(2)}, u32[]{:S(2)}) %collective-permute-start.9) | collective-permute-done | bytes 786464 | tf_op jit(solution)/shard_map/ppermute | solution.py:193
  58.6 1.3 %collective-permute-done.10.refs_1_ = bf16[128,3072]{1,0:T(8,128)(2,1)S(1)} collective-permute-done((bf16[128,3072]{1,0:T(8,128)(2,1)S(1)}, bf16[128,3072]{1,0:T(8,128)(2,1)S(1)}, u32[]{:S(2)}, u32[]{:S(2)}) %collective-permute-start.10) | collective-permute-done | bytes 786464 | tf_op jit(solution)/shard_map/ppermute | solution.py:193
  60.0 0.5 collective-permute-start.16
  60.5 1.6 %collective-permute-start.15 = (bf16[64,3072]{1,0:T(8,128)(2,1)S(1)}, bf16[64,3072]{1,0:T(8,128)(2,1)S(1)}, u32[]{:S(2)}, u32[]{:S(2)}) collective-permute-start(bf16[64,3072]{1,0:T(8,128)(2,1)S(1)} %slice.75), channel_id=1, source_target_pairs={{0,8},{8,16},{16,24},{24,28},{28,20},{20,12},{12,4},{4,0},{1,9},{9... | collective-permute-start | bytes 1179656 | tf_op jit(solution)/shard_map/ppermute | solution.py:193
  62.1 2.6 %project.9 = (bf16[768,256]{1,0:T(8,128)(2,1)S(1)}, bf16[768,256]{1,0:T(8,128)(2,1)S(1)}, bf16[256,3072]{1,0:T(8,128)(2,1)S(1)}) custom-call(s32[1]{0:T(128)} %bitcast.which_ref, bf16[768,3072]{1,0:T(8,128)(2,1)S(1)} %copy-done.3, bf16[768,3072]{1,0:T(8,128)(2,1)S(1)} %copy-done.1, bf16[128,3072]{1,0:T(8,128)(2,1)S(1)} %collective-permute-done.9.refs_0_, ...), custom_call_target="tpu_custom_call" | custom-call | flops 362387872 | tf_op jit(solution)/shard_map/project/pallas_call | solution.py:114
  64.9 0.5 collective-permute-done.18
  65.4 4.0 %collective-permute-done.16.refs_1_ = bf16[64,3072]{1,0:T(8,128)(2,1)S(1)} collective-permute-done((bf16[64,3072]{1,0:T(8,128)(2,1)S(1)}, bf16[64,3072]{1,0:T(8,128)(2,1)S(1)}, u32[]{:S(2)}, u32[]{:S(2)}) %collective-permute-start.16) | collective-permute-done | bytes 393248 | tf_op jit(solution)/shard_map/ppermute | solution.py:193
  69.4 0.2 collective-permute-done.15.refs_0_
  69.7 0.2 fusion.12
  70.0 0.1 fusion.52
  70.1 1.1 %collective-permute-start.21 = (bf16[768,256]{1,0:T(8,128)(2,1)S(1)}, bf16[768,256]{1,0:T(8,128)(2,1)S(1)}, u32[]{:S(2)}, u32[]{:S(2)}) collective-permute-start(bf16[768,256]{1,0:T(8,128)(2,1)S(1)} %get-tuple-element.79), channel_id=1, source_target_pairs={{0,2},{1,3},{2,0},{3,1},{4,6},{5,7},{6,4},{7,5},{8,10},{9,11},{10,... | collective-permute-start | bytes 1179656 | tf_op jit(solution)/shard_map/ppermute | solution.py:187
  71.2 1.4 %project.11 = (bf16[768,128]{1,0:T(8,128)(2,1)S(1)}, bf16[128,3072]{1,0:T(8,128)(2,1)S(1)}) custom-call(s32[1]{0:T(128)} %bitcast.which_ref, bf16[768,3072]{1,0:T(8,128)(2,1)S(1)} %copy-done.3, bf16[768,3072]{1,0:T(8,128)(2,1)S(1)} %copy-done.1, bf16[64,3072]{1,0:T(8,128)(2,1)S(1)} %collective-permute-done.15.refs_0_, ...), custom_call_target="tpu_custom_call" | custom-call | flops 181193936 | tf_op jit(solution)/shard_map/project/pallas_call | solution.py:114
  72.7 0.6 collective-permute-start.8
  73.3 0.4 collective-permute-start.13
  73.8 2.0 %project.10 = (bf16[768,128]{1,0:T(8,128)(2,1)S(1)}, bf16[128,3072]{1,0:T(8,128)(2,1)}) custom-call(s32[1]{0:T(128)} %bitcast.which_ref, bf16[768,3072]{1,0:T(8,128)(2,1)S(1)} %copy-done.3, bf16[768,3072]{1,0:T(8,128)(2,1)S(1)} %copy-done.1, bf16[64,3072]{1,0:T(8,128)(2,1)S(1)} %collective-permute-done.15.refs_0_, ...), custom_call_target="tpu_custom_call" | custom-call | flops 181193936 | tf_op jit(solution)/shard_map/project/pallas_call | solution.py:114
  75.8 1.1 %collective-permute-start.23 = (bf16[768,128]{1,0:T(8,128)(2,1)S(1)}, bf16[768,128]{1,0:T(8,128)(2,1)S(1)}, u32[]{:S(2)}, u32[]{:S(2)}) collective-permute-start(bf16[768,128]{1,0:T(8,128)(2,1)S(1)} %get-tuple-element.85), channel_id=1, source_target_pairs={{0,2},{1,3},{2,0},{3,1},{4,6},{5,7},{6,4},{7,5},{8,10},{9,11},{10,... | collective-permute-start | bytes 589832 | tf_op jit(solution)/shard_map/ppermute | solution.py:187
  76.9 3.8 %contract.2.base_ref = f32[768,3072]{1,0:T(8,128)S(1)} custom-call(s32[1]{0:T(128)} %bitcast.which_ref, bf16[768,3072]{1,0:T(8,128)(2,1)S(1)} %bitcast.12, bf16[384,128]{1,0:T(8,128)(2,1)S(1)} %fusion.27.refs_0_, bf16[384,128]{1,0:T(8,128)(2,1)S(1)} %collective-permute-done.8.refs_1_, bf16[128,3072]{1,0:T(8,128)(2,1)S(1)} %copy-done.5, ...), custom_call_target="tpu_custom_call" | custom-call | flops 452984832 | tf_op jit(solution)/shard_map/contract/pallas_call | solution.py:165
  80.9 0.1 fusion.7.refs_0_
  81.1 1.7 %collective-permute-done.23 = bf16[768,128]{1,0:T(8,128)(2,1)S(1)} collective-permute-done((bf16[768,128]{1,0:T(8,128)(2,1)S(1)}, bf16[768,128]{1,0:T(8,128)(2,1)S(1)}, u32[]{:S(2)}, u32[]{:S(2)}) %collective-permute-start.23) | collective-permute-done | bytes 196640 | tf_op jit(solution)/shard_map/ppermute | solution.py:187
  83.0 1.3 %collective-permute-done.24.refs_4_ = bf16[384,128]{1,0:T(8,128)(2,1)S(1)} collective-permute-done((bf16[384,128]{1,0:T(8,128)(2,1)S(1)}, bf16[384,128]{1,0:T(8,128)(2,1)S(1)}, u32[]{:S(2)}, u32[]{:S(2)}) %collective-permute-start.24) | collective-permute-done | bytes 98336 | tf_op jit(solution)/shard_map/ppermute | solution.py:187
  84.3 4.3 %contract.3 = f32[768,3072]{1,0:T(8,128)} custom-call(s32[1]{0:T(128)} %bitcast.which_ref, f32[768,3072]{1,0:T(8,128)S(1)} %contract.2.base_ref, bf16[384,256]{1,0:T(8,128)(2,1)S(1)} %fusion.7.refs_0_, bf16[384,256]{1,0:T(8,128)(2,1)S(1)} %collective-permute-done.22.refs_1_, bf16[256,3072]{1,0:T(8,128)(2,1)S(1)} %get-tuple-element.74.refs_2_, ...), custom_call_target="tpu_custom_call" | custom-call | flops 271790912 | tf_op jit(solution)/shard_map/contract/pallas_call | solution.py:165
  (59 shorter events, 1.8 us)
Async XLA Ops:
  0.0 20.8 %collective-permute-start.2 = (bf16[128,3072]{1,0:T(8,128)(2,1)}, bf16[128,3072]{1,0:T(8,128)(2,1)S(1)}, u32[]{:S(2)}, u32[]{:S(2)}) collective-permute-start(bf16[128,3072]{1,0:T(8,128)(2,1)} %refs_2_.1), channel_id=1, source_target_pairs={{0,4},{8,0},{16,8},{24,16},{28,24},{20,28},{12,20},{4,12},{1,5},{9... | collective-permute-start | bytes 2359304 | tf_op jit(solution)/shard_map/ppermute | solution.py:193
  2.9 19.5 %collective-permute-start = (bf16[128,3072]{1,0:T(8,128)(2,1)}, bf16[128,3072]{1,0:T(8,128)(2,1)S(1)}, u32[]{:S(2)}, u32[]{:S(2)}) collective-permute-start(bf16[128,3072]{1,0:T(8,128)(2,1)} %refs_2_.1), channel_id=1, source_target_pairs={{0,8},{8,16},{16,24},{24,28},{28,20},{20,12},{12,4},{4,0},{1,9},{9... | collective-permute-start | bytes 2359304 | tf_op jit(solution)/shard_map/ppermute | solution.py:193
  4.1 18.7 %collective-permute-start.6 = (bf16[256,384]{1,0:T(8,128)(2,1)S(1)}, bf16[256,384]{1,0:T(8,128)(2,1)S(1)}, u32[]{:S(2)}, u32[]{:S(2)}) collective-permute-start(bf16[256,384]{1,0:T(8,128)(2,1)S(1)} %get-tuple-element.88), channel_id=1, source_target_pairs={{0,1},{1,0},{2,3},{3,2},{4,5},{5,4},{6,7},{7,6},{8,9},{9,8},{10,11... | collective-permute-start | bytes 589832 | tf_op jit(solution)/shard_map/ppermute | solution.py:187
  4.2 2.3 %copy-start = (bf16[768,3072]{1,0:T(8,128)(2,1)S(1)}, bf16[768,3072]{1,0:T(8,128)(2,1)}, u32[]{:S(2)}) copy-start(bf16[768,3072]{1,0:T(8,128)(2,1)} %base_ref.1) | copy-start | bytes 14155780
  6.5 2.3 %copy-start.2 = (bf16[768,3072]{1,0:T(8,128)(2,1)S(1)}, bf16[768,3072]{1,0:T(8,128)(2,1)}, u32[]{:S(2)}) copy-start(bf16[768,3072]{1,0:T(8,128)(2,1)} %w_ref.11) | copy-start | bytes 14155780
  8.8 1.1 %copy-start.4 = (bf16[128,3072]{1,0:T(8,128)(2,1)S(1)}, bf16[128,3072]{1,0:T(8,128)(2,1)}, u32[]{:S(2)}) copy-start(bf16[128,3072]{1,0:T(8,128)(2,1)} %refs_2_.1) | copy-start | bytes 2359300
  10.0 4.0 %copy-start.6 = (s32[4]{0:T(128)S(1)}, s32[4]{0:T(128)}, u32[]{:S(2)}) copy-start(s32[4]{0:T(128)} %param.11) | copy-start | bytes 52
  10.0 4.1 %copy-start.7 = (f32[4]{0:T(128)S(1)}, f32[4]{0:T(128)}, u32[]{:S(2)}) copy-start(f32[4]{0:T(128)} %param.12) | copy-start | bytes 52
  12.6 19.4 %collective-permute-start.4 = (bf16[768,128]{1,0:T(8,128)(2,1)S(1)}, bf16[768,128]{1,0:T(8,128)(2,1)S(1)}, u32[]{:S(2)}, u32[]{:S(2)}) collective-permute-start(bf16[768,128]{1,0:T(8,128)(2,1)S(1)} %get-tuple-element.43), channel_id=1, source_target_pairs={{0,1},{1,0},{2,3},{3,2},{4,5},{5,4},{6,7},{7,6},{8,9},{9,8},{10,11... | collective-permute-start | bytes 589832 | tf_op jit(solution)/shard_map/ppermute | solution.py:187
  20.8 18.7 %collective-permute-start.3 = (bf16[128,3072]{1,0:T(8,128)(2,1)S(1)}, bf16[128,3072]{1,0:T(8,128)(2,1)S(1)}, u32[]{:S(2)}, u32[]{:S(2)}) collective-permute-start(bf16[128,3072]{1,0:T(8,128)(2,1)S(1)} %collective-permute-done.2.refs_1_), channel_id=1, source_target_pairs={{0,4},{8,0},{16,8},{24,16},{28,24},{20,28},{12,20},{4,12},{1,5},{9... | collective-permute-start | bytes 2359304 | tf_op jit(solution)/shard_map/ppermute | solution.py:193
  22.4 18.1 %collective-permute-start.1 = (bf16[128,3072]{1,0:T(8,128)(2,1)S(1)}, bf16[128,3072]{1,0:T(8,128)(2,1)S(1)}, u32[]{:S(2)}, u32[]{:S(2)}) collective-permute-start(bf16[128,3072]{1,0:T(8,128)(2,1)S(1)} %collective-permute-done.refs_0_), channel_id=1, source_target_pairs={{0,8},{8,16},{16,24},{24,28},{28,20},{20,12},{12,4},{4,0},{1,9},{9... | collective-permute-start | bytes 2359304 | tf_op jit(solution)/shard_map/ppermute | solution.py:193
  22.9 16.6 %collective-permute-start.7 = (bf16[512,384]{1,0:T(8,128)(2,1)S(1)}, bf16[512,384]{1,0:T(8,128)(2,1)S(1)}, u32[]{:S(2)}, u32[]{:S(2)}) collective-permute-start(bf16[512,384]{1,0:T(8,128)(2,1)S(1)} %pad_maximum_fusion), channel_id=1, source_target_pairs={{0,2},{1,3},{2,0},{3,1},{4,6},{5,7},{6,4},{7,5},{8,10},{9,11},{10,... | collective-permute-start | bytes 1179656 | tf_op jit(solution)/shard_map/ppermute | solution.py:187
  24.6 2.3 %copy-start.1 = (bf16[768,3072]{1,0:T(8,128)(2,1)S(1)}, bf16[768,3072]{1,0:T(8,128)(2,1)}, u32[]{:S(2)}) copy-start(bf16[768,3072]{1,0:T(8,128)(2,1)} %base_ref.1) | copy-start | bytes 14155780
  26.9 2.3 %copy-start.3 = (bf16[768,3072]{1,0:T(8,128)(2,1)S(1)}, bf16[768,3072]{1,0:T(8,128)(2,1)}, u32[]{:S(2)}) copy-start(bf16[768,3072]{1,0:T(8,128)(2,1)} %w_ref.11) | copy-start | bytes 14155780
  31.9 13.4 %collective-permute-start.11 = (bf16[768,256]{1,0:T(8,128)(2,1)S(1)}, bf16[768,256]{1,0:T(8,128)(2,1)S(1)}, u32[]{:S(2)}, u32[]{:S(2)}) collective-permute-start(bf16[768,256]{1,0:T(8,128)(2,1)S(1)} %get-tuple-element.50), channel_id=1, source_target_pairs={{0,1},{1,0},{2,3},{3,2},{4,5},{5,4},{6,7},{7,6},{8,9},{9,8},{10,11... | collective-permute-start | bytes 1179656 | tf_op jit(solution)/shard_map/ppermute | solution.py:187
  32.1 7.4 %collective-permute-start.5 = (bf16[768,128]{1,0:T(8,128)(2,1)S(1)}, bf16[768,128]{1,0:T(8,128)(2,1)S(1)}, u32[]{:S(2)}, u32[]{:S(2)}) collective-permute-start(bf16[768,128]{1,0:T(8,128)(2,1)S(1)} %get-tuple-element.89), channel_id=1, source_target_pairs={{0,2},{1,3},{2,0},{3,1},{4,6},{5,7},{6,4},{7,5},{8,10},{9,11},{10,... | collective-permute-start | bytes 589832 | tf_op jit(solution)/shard_map/ppermute | solution.py:187
  40.6 18.1 %collective-permute-start.9 = (bf16[128,3072]{1,0:T(8,128)(2,1)S(1)}, bf16[128,3072]{1,0:T(8,128)(2,1)S(1)}, u32[]{:S(2)}, u32[]{:S(2)}) collective-permute-start(bf16[128,3072]{1,0:T(8,128)(2,1)S(1)} %collective-permute-done.1.refs_0_), channel_id=1, source_target_pairs={{0,8},{8,16},{16,24},{24,28},{28,20},{20,12},{12,4},{4,0},{1,9},{9... | collective-permute-start | bytes 2359304 | tf_op jit(solution)/shard_map/ppermute | solution.py:193
  41.3 18.7 %collective-permute-start.10 = (bf16[128,3072]{1,0:T(8,128)(2,1)S(1)}, bf16[128,3072]{1,0:T(8,128)(2,1)S(1)}, u32[]{:S(2)}, u32[]{:S(2)}) collective-permute-start(bf16[128,3072]{1,0:T(8,128)(2,1)S(1)} %collective-permute-done.3.refs_1_), channel_id=1, source_target_pairs={{0,4},{8,0},{16,8},{24,16},{28,24},{20,28},{12,20},{4,12},{1,5},{9... | collective-permute-start | bytes 2359304 | tf_op jit(solution)/shard_map/ppermute | solution.py:193
  45.2 2.9 %collective-permute-start.17 = (bf16[768,256]{1,0:T(8,128)(2,1)S(1)}, bf16[768,256]{1,0:T(8,128)(2,1)S(1)}, u32[]{:S(2)}, u32[]{:S(2)}) collective-permute-start(bf16[768,256]{1,0:T(8,128)(2,1)S(1)} %get-tuple-element.58), channel_id=1, source_target_pairs={{0,1},{1,0},{2,3},{3,2},{4,5},{5,4},{6,7},{7,6},{8,9},{9,8},{10,11... | collective-permute-start | bytes 1179656 | tf_op jit(solution)/shard_map/ppermute | solution.py:187
  45.4 12.0 %collective-permute-start.12 = (bf16[768,256]{1,0:T(8,128)(2,1)S(1)}, bf16[768,256]{1,0:T(8,128)(2,1)S(1)}, u32[]{:S(2)}, u32[]{:S(2)}) collective-permute-start(bf16[768,256]{1,0:T(8,128)(2,1)S(1)} %get-tuple-element.83), channel_id=1, source_target_pairs={{0,2},{1,3},{2,0},{3,1},{4,6},{5,7},{6,4},{7,5},{8,10},{9,11},{10,... | collective-permute-start | bytes 1179656 | tf_op jit(solution)/shard_map/ppermute | solution.py:187
  48.2 17.2 %collective-permute-start.18 = (bf16[768,256]{1,0:T(8,128)(2,1)S(1)}, bf16[768,256]{1,0:T(8,128)(2,1)S(1)}, u32[]{:S(2)}, u32[]{:S(2)}) collective-permute-start(bf16[768,256]{1,0:T(8,128)(2,1)S(1)} %get-tuple-element.81), channel_id=1, source_target_pairs={{0,2},{1,3},{2,0},{3,1},{4,6},{5,7},{6,4},{7,5},{8,10},{9,11},{10,... | collective-permute-start | bytes 1179656 | tf_op jit(solution)/shard_map/ppermute | solution.py:187
  60.0 9.4 %collective-permute-start.16 = (bf16[64,3072]{1,0:T(8,128)(2,1)S(1)}, bf16[64,3072]{1,0:T(8,128)(2,1)S(1)}, u32[]{:S(2)}, u32[]{:S(2)}) collective-permute-start(bf16[64,3072]{1,0:T(8,128)(2,1)S(1)} %slice.76), channel_id=1, source_target_pairs={{0,4},{8,0},{16,8},{24,16},{28,24},{20,28},{12,20},{4,12},{1,5},{9... | collective-permute-start | bytes 1179656 | tf_op jit(solution)/shard_map/ppermute | solution.py:193
  60.5 9.1 %collective-permute-start.15 = (bf16[64,3072]{1,0:T(8,128)(2,1)S(1)}, bf16[64,3072]{1,0:T(8,128)(2,1)S(1)}, u32[]{:S(2)}, u32[]{:S(2)}) collective-permute-start(bf16[64,3072]{1,0:T(8,128)(2,1)S(1)} %slice.75), channel_id=1, source_target_pairs={{0,8},{8,16},{16,24},{24,28},{28,20},{20,12},{12,4},{4,0},{1,9},{9... | collective-permute-start | bytes 1179656 | tf_op jit(solution)/shard_map/ppermute | solution.py:193
  64.8 5.2 %collective-permute-start.14 = (bf16[768,256]{1,0:T(8,128)(2,1)S(1)}, bf16[768,256]{1,0:T(8,128)(2,1)S(1)}, u32[]{:S(2)}, u32[]{:S(2)}) collective-permute-start(bf16[768,256]{1,0:T(8,128)(2,1)S(1)} %get-tuple-element.56), channel_id=1, source_target_pairs={{0,1},{1,0},{2,3},{3,2},{4,5},{5,4},{6,7},{7,6},{8,9},{9,8},{10,11... | collective-permute-start | bytes 1179656 | tf_op jit(solution)/shard_map/ppermute | solution.py:187
  70.1 10.7 %collective-permute-start.21 = (bf16[768,256]{1,0:T(8,128)(2,1)S(1)}, bf16[768,256]{1,0:T(8,128)(2,1)S(1)}, u32[]{:S(2)}, u32[]{:S(2)}) collective-permute-start(bf16[768,256]{1,0:T(8,128)(2,1)S(1)} %get-tuple-element.79), channel_id=1, source_target_pairs={{0,2},{1,3},{2,0},{3,1},{4,6},{5,7},{6,4},{7,5},{8,10},{9,11},{10,... | collective-permute-start | bytes 1179656 | tf_op jit(solution)/shard_map/ppermute | solution.py:187
  72.6 3.2 %collective-permute-start.20 = (bf16[768,128]{1,0:T(8,128)(2,1)S(1)}, bf16[768,128]{1,0:T(8,128)(2,1)S(1)}, u32[]{:S(2)}, u32[]{:S(2)}) collective-permute-start(bf16[768,128]{1,0:T(8,128)(2,1)S(1)} %get-tuple-element.66), channel_id=1, source_target_pairs={{0,1},{1,0},{2,3},{3,2},{4,5},{5,4},{6,7},{7,6},{8,9},{9,8},{10,11... | collective-permute-start | bytes 589832 | tf_op jit(solution)/shard_map/ppermute | solution.py:187
  72.7 4.2 %collective-permute-start.8 = (bf16[384,128]{1,0:T(8,128)(2,1)S(1)}, bf16[384,128]{1,0:T(8,128)(2,1)S(1)}, u32[]{:S(2)}, u32[]{:S(2)}) collective-permute-start(bf16[384,128]{1,0:T(8,128)(2,1)S(1)} %fusion.27.refs_0_), channel_id=1, source_target_pairs={{0,1},{1,0},{2,3},{3,2},{4,5},{5,4},{6,7},{7,6},{8,9},{9,8},{10,11... | collective-permute-start | bytes 294920 | tf_op jit(solution)/shard_map/ppermute | solution.py:187
  73.3 3.6 %collective-permute-start.19 = (bf16[384,256]{1,0:T(8,128)(2,1)S(1)}, bf16[384,256]{1,0:T(8,128)(2,1)S(1)}, u32[]{:S(2)}, u32[]{:S(2)}) collective-permute-start(bf16[384,256]{1,0:T(8,128)(2,1)S(1)} %get-tuple-element.61.refs_6_), channel_id=1, source_target_pairs={{0,1},{1,0},{2,3},{3,2},{4,5},{5,4},{6,7},{7,6},{8,9},{9,8},{10,11... | collective-permute-start | bytes 589832 | tf_op jit(solution)/shard_map/ppermute | solution.py:187
  73.3 3.6 %slice-start = ((s8[4718592]{0:T(1024)(128)(4,1)}), s8[4194304]{0:T(1024)(128)(4,1)S(1)}, s32[]{:S(2)}) async-start(s8[4718592]{0:T(1024)(128)(4,1)} %bitcast.11), calls=%async_computation | async-start | bytes 8388608
  73.3 3.6 %slice-start.1 = ((s8[4718592]{0:T(1024)(128)(4,1)}), s8[524288]{0:T(1024)(128)(4,1)S(1)}, s32[]{:S(2)}) async-start(s8[4718592]{0:T(1024)(128)(4,1)} %bitcast.11), calls=%async_computation.1 | async-start | bytes 1048576
  73.3 3.6 %copy-start.5 = (bf16[128,3072]{1,0:T(8,128)(2,1)S(1)}, bf16[128,3072]{1,0:T(8,128)(2,1)}, u32[]{:S(2)}) copy-start(bf16[128,3072]{1,0:T(8,128)(2,1)} %refs_2_.1) | copy-start | bytes 2359300
  73.3 3.6 %collective-permute-start.13 = (bf16[384,256]{1,0:T(8,128)(2,1)S(1)}, bf16[384,256]{1,0:T(8,128)(2,1)S(1)}, u32[]{:S(2)}, u32[]{:S(2)}) collective-permute-start(bf16[384,256]{1,0:T(8,128)(2,1)S(1)} %get-tuple-element.78.refs_3_), channel_id=1, source_target_pairs={{0,1},{1,0},{2,3},{3,2},{4,5},{5,4},{6,7},{7,6},{8,9},{9,8},{10,11... | collective-permute-start | bytes 589832 | tf_op jit(solution)/shard_map/ppermute | solution.py:187
  75.8 7.0 %collective-permute-start.23 = (bf16[768,128]{1,0:T(8,128)(2,1)S(1)}, bf16[768,128]{1,0:T(8,128)(2,1)S(1)}, u32[]{:S(2)}, u32[]{:S(2)}) collective-permute-start(bf16[768,128]{1,0:T(8,128)(2,1)S(1)} %get-tuple-element.85), channel_id=1, source_target_pairs={{0,2},{1,3},{2,0},{3,1},{4,6},{5,7},{6,4},{7,5},{8,10},{9,11},{10,... | collective-permute-start | bytes 589832 | tf_op jit(solution)/shard_map/ppermute | solution.py:187
  81.0 3.3 %collective-permute-start.22 = (bf16[384,256]{1,0:T(8,128)(2,1)S(1)}, bf16[384,256]{1,0:T(8,128)(2,1)S(1)}, u32[]{:S(2)}, u32[]{:S(2)}) collective-permute-start(bf16[384,256]{1,0:T(8,128)(2,1)S(1)} %fusion.7.refs_0_), channel_id=1, source_target_pairs={{0,1},{1,0},{2,3},{3,2},{4,5},{5,4},{6,7},{7,6},{8,9},{9,8},{10,11... | collective-permute-start | bytes 589832 | tf_op jit(solution)/shard_map/ppermute | solution.py:187
  82.9 1.4 %collective-permute-start.24 = (bf16[384,128]{1,0:T(8,128)(2,1)S(1)}, bf16[384,128]{1,0:T(8,128)(2,1)S(1)}, u32[]{:S(2)}, u32[]{:S(2)}) collective-permute-start(bf16[384,128]{1,0:T(8,128)(2,1)S(1)} %fusion.22.refs_3_), channel_id=1, source_target_pairs={{0,1},{1,0},{2,3},{3,2},{4,5},{5,4},{6,7},{7,6},{8,9},{9,8},{10,11... | collective-permute-start | bytes 294920 | tf_op jit(solution)/shard_map/ppermute | solution.py:187

commit v4 on v3

--- a/solution.py
+++ b/solution.py
@@ -94,18 +94,22 @@
 IN_VMEM = pl.BlockSpec(memory_space=pltpu.VMEM)
 
 
+KEEP, GIVE = (0, (0, 1)), (1, (0, 1))
+
+
 def project_kernel(wanted, count, which_ref, w_ref, d_ref, *refs):
-    parts, outs, block = refs[:count], refs[count:-1], refs[-1]
+    parts, outs = refs[:count], refs[count : count + len(wanted)]
     part = w_ref.shape[0] // 2
-    row = 0
-    for ref in parts:
+    block, row = refs[-1] if count > 1 else parts[0], 0
+    for ref in parts if count > 1 else ():
         block[row : row + ref.shape[0], :] = ref[...]
         row += ref.shape[0]
-    for flip, out in zip(wanted, outs):
+    for (flip, sources), out in zip(wanted, outs):
         which = which_ref[0] if flip == 0 else 1 - which_ref[0]
         rows = pl.ds(pl.multiple_of(which * part, part), part)
-        for at, source in enumerate((w_ref, d_ref)):
-            out[at * part : (at + 1) * part, :] = project_rows(source[rows, :], block[...]).astype(out.dtype)
+        for at, source in enumerate(sources):
+            values = project_rows((w_ref, d_ref)[source][rows, :], block[...])
+            out[at * part : (at + 1) * part, :] = values.astype(out.dtype)
 
 
 def project(core, w_out, direction, parts, wanted):
@@ -113,66 +117,98 @@
     width, depth = w_out.shape
     return pl.pallas_call(
         functools.partial(project_kernel, wanted, len(parts)),
-        out_shape=[jax.ShapeDtypeStruct((width, count), jnp.bfloat16) for _ in wanted]
-        + [jax.ShapeDtypeStruct((count, depth), jnp.bfloat16)],
+        out_shape=[jax.ShapeDtypeStruct((width // 2 * len(sources), count), jnp.bfloat16) for _, sources in wanted]
+        + [jax.ShapeDtypeStruct((count, depth), jnp.bfloat16)] * (len(parts) > 1),
         in_specs=[pl.BlockSpec(memory_space=pltpu.SMEM)] + [IN_VMEM] * (2 + len(parts)),
-        out_specs=[IN_VMEM] * (len(wanted) + 1),
+        out_specs=[IN_VMEM] * (len(wanted) + (len(parts) > 1)),
         compiler_params=pltpu.CompilerParams(vmem_limit_bytes=20 * 2**20),
-        cost_estimate=cost(2 * len(wanted) * width * max(count, 256) * depth),
+        cost_estimate=cost(sum(len(sources) for _, sources in wanted) * width * max(count, 256) * depth),
         name="project",
     )(core, w_out, direction, *parts)
 
 
-def contract_kernel(count, step, tile, last, which_ref, base_ref, *refs):
-    terms, out = [refs[3 * i : 3 * i + 3] for i in range(count)], refs[3 * count]
+def merge_kernel(kept_ref, *refs):
+    *pieces, chip, sent = refs
+    row = 0
+    for piece in pieces:
+        rows = slice(row, row + piece.shape[0])
+        total = kept_ref[rows, :].astype(jnp.float32) + piece[...].astype(jnp.float32)
+        chip[rows, :] = total
+        sent[rows, :] = total.astype(sent.dtype)
+        row += piece.shape[0]
+
+
+def merge(kept, *pieces):
+    return pl.pallas_call(
+        merge_kernel,
+        out_shape=[jax.ShapeDtypeStruct(kept.shape, jnp.float32), jax.ShapeDtypeStruct(kept.shape, jnp.bfloat16)],
+        in_specs=[IN_VMEM] * (1 + len(pieces)),
+        out_specs=[IN_VMEM] * 2,
+        compiler_params=pltpu.CompilerParams(vmem_limit_bytes=6 * 2**20),
+        cost_estimate=cost(0),
+        name="merge",
+    )(kept, *pieces)
+
+
+def contract_kernel(count, step, tile, flips, last, which_ref, base_ref, *refs):
+    size = len(flips) + 1
+    terms, refs = [refs[size * i : size * i + size] for i in range(count)], refs[size * count :]
     width, depth = base_ref.shape
     part = width // 2
     tiles = depth // tile
     if last:
-        buffer, sem = refs[3 * count + 1 :]
-
-    def copy_of(i):
-        return pltpu.make_async_copy(buffer.at[i], out.at[:, i * tile : (i + 1) * tile], sem.at[i])
+        *_, out, buffer, sem = refs
+    else:
+        (out,) = refs
+
+    def rows_of(flip):
+        which = which_ref[0] if flip == 0 else 1 - which_ref[0]
+        return pl.ds(pl.multiple_of(which * part, part), part)
+
+    def copy_of(i, flip):
+        columns = slice(i * tile, (i + 1) * tile)
+        return pltpu.make_async_copy(buffer.at[i], out.at[rows_of(flip), columns], sem.at[i])
 
     for i in range(tiles):
         columns = slice(i * tile, (i + 1) * tile)
-        for flip in (0, 1):
-            which = which_ref[0] if flip == 0 else 1 - which_ref[0]
-            rows = pl.ds(pl.multiple_of(which * part, part), part)
+        for at, flip in enumerate(flips):
+            rows = rows_of(flip)
             total = sum(
-                jnp.dot(term[flip][...], term[2][:, columns], preferred_element_type=jnp.float32) for term in terms
+                jnp.dot(term[at][...], term[-1][:, columns], preferred_element_type=jnp.float32) for term in terms
             )
             base = base_ref[rows, columns]
             if base.dtype == jnp.bfloat16:
                 base = 2.0 * base.astype(jnp.float32)
             if last:
-                buffer[i, rows, :] = base - step * total
+                buffer[i, :, :] = base - step * total
             else:
                 out[rows, columns] = base - step * total
         if last:
-            copy_of(i).start()
+            copy_of(i, flips[0]).start()
     if last:
         for i in range(tiles):
-            copy_of(i).wait()
-
-
-def contract(core, base, terms, step, last):
+            copy_of(i, flips[0]).wait()
+
+
+def contract(core, base, terms, step, flips=(0, 1), last=False, into=None):
     width, depth = base.shape
     tile = 512
     while depth % tile:
         tile //= 2
     tiles = depth // tile
+    operands = [v for term in terms for v in term]
+    held = [] if into is None else [into]
     return pl.pallas_call(
-        functools.partial(contract_kernel, len(terms), step, tile, last),
+        functools.partial(contract_kernel, len(terms), step, tile, flips, last),
         out_shape=jax.ShapeDtypeStruct((width, depth), jnp.float32),
-        in_specs=[pl.BlockSpec(memory_space=pltpu.SMEM)] + [IN_VMEM] * (1 + 3 * len(terms)),
+        in_specs=[pl.BlockSpec(memory_space=pltpu.SMEM)] + [IN_VMEM] * (1 + len(operands)) + [pl.BlockSpec(memory_space=pl.ANY)] * len(held),
         out_specs=pl.BlockSpec(memory_space=pl.ANY) if last else IN_VMEM,
-        scratch_shapes=[pltpu.VMEM((tiles, width, tile), jnp.float32), pltpu.SemaphoreType.DMA((tiles,))] if last else [],
-        input_output_aliases={1: 0} if base.dtype == jnp.float32 and not last else {},
+        scratch_shapes=[pltpu.VMEM((tiles, width // 2, tile), jnp.float32), pltpu.SemaphoreType.DMA((tiles,))] if last else [],
+        input_output_aliases={2 + len(operands): 0} if held else {},
         compiler_params=pltpu.CompilerParams(vmem_limit_bytes=20 * 2**20),
-        cost_estimate=cost(2 * width * depth * sum(term[2].shape[0] for term in terms)),
+        cost_estimate=cost(2 * width * depth * sum(term[-1].shape[0] for term in terms)),
         name="contract",
-    )(core, base, *[v for term in terms for v in term])
+    )(core, base, *operands, *held)
 
 
 def on_device(hidden, w_out, direction, targets, codes, code_weights):
@@ -232,45 +268,44 @@
         return mine, swap(mine, CORE)
 
     hop1 = step((hidden, hidden))
-    theirs0, kept0, _ = project(one, w_out, direction, [hidden], (1, 0))
+    theirs0, kept0 = project(one, w_out, direction, [hidden], (GIVE, KEEP))
     chip0 = add(kept0, swap(theirs0, CORE))
     across0 = over_rows(chip0)
 
     hop2 = step(hop1)
-    theirs1, kept1, block1 = project(one, w_out, direction, hop1, (1, 0))
+    theirs1, kept1, block1 = project(one, w_out, direction, hop1, (GIVE, KEEP))
     chip1 = add(kept1, swap(theirs1, CORE))
     across1 = over_rows(chip1)
     *hop2, kept1, chip0, across0, other = gate(*hop2, kept1, chip0, across0, other)
     aligned = align(other)
     hop3 = step(hop2)
-    theirs2, kept2, block2 = project(one, w_out, direction, hop2, (1, 0))
+    theirs2, kept2, block2 = project(one, w_out, direction, hop2, (GIVE, KEEP))
     chip2 = add(kept2, swap(theirs2, CORE))
     across2 = over_rows(chip2)
     scaled0 = weigh(aligned, chip0, across0, 0)
     *hop3, kept2, chip1, across1 = gate(*hop3, kept2, chip1, across1)
     hop4 = step((hop3[0][:half], hop3[1][half:]))
-    theirs3, kept3, block3 = project(one, w_out, direction, hop3, (1, 0))
-    theirs3 = swap(theirs3, CORE)
+    *theirs3, kept3, block3 = project(one, w_out, direction, hop3, ((1, (0,)), (1, (1,)), KEEP))
+    chip3, sent3 = merge(kept3, *[swap(v, CORE) for v in theirs3])
+    across3 = swap(sent3, ROW)
+    *hop4, kept3, chip2, across2, chip1 = gate(*hop4, kept3, chip2, across2, chip1)
     scaled1 = weigh(aligned, chip1, across1, rows)
-    *hop4, kept3, chip2, across2 = gate(*hop4, kept3, chip2, across2)
-    scaled2 = weigh(aligned, chip2, across2, 3 * rows)
-    theirs3, mine2 = gate(theirs3, scaled2[0])
-    scaled2 = (mine2, scaled2[1])
-    chip3 = add(kept3, theirs3)
-    across3 = over_rows(chip3)
-    theirs4, block4 = project(one, w_out, direction, hop4, (1,))
+    theirs4, block4 = project(one, w_out, direction, hop4, (GIVE,))
     theirs4 = swap(theirs4, CORE)
-    kept4, _ = project(one, w_out, direction, hop4, (0,))
+    (kept4,) = project(one, w_out, direction, [block4], (KEEP,))
     chip4 = add(kept4, theirs4)
     across4 = over_rows(chip4)
     share = STEP / tokens_all
+    scaled2 = weigh(aligned, chip2, across2, 3 * rows)
     block2, chip4 = gate(block2, chip4)
-    total = contract(one, direction, [(*scaled0, hidden), (*scaled1, block1), (*scaled2, block2)], share, False)
+    total = contract(one, direction, [(*scaled0, hidden), (*scaled1, block1), (*scaled2, block2)], share)
     total, chip3 = gate(total, chip3)
     scaled3 = weigh(aligned, chip3, across3, 5 * rows)
     mine3, chip4 = gate(scaled3[0], chip4)
     scaled4 = weigh(aligned, chip4, across4, 7 * rows)
-    return contract(one, total, [(mine3, scaled3[1], block3), (*scaled4, block4)], share, True)
+    result = contract(one, total, [(mine3, block3), (scaled4[0], block4)], share, (0,), True)
+    terms = [(scaled3[1], block3), (scaled4[1], block4)]
+    return contract(one, total, terms, share, (1,), True, result)
 
 
 def solution(mesh):

time: 89 us -> 88.1 us (0.990)
  waiting for transfers between devices: 33.6 us -> 32.3 us
    ppermute x8, waiting for transfers between devices: 14.5 us -> 12.6 us  [step(): return (lax.ppermute(pair[0], 'dp', UP), lax.ppermute(pair[1], 'dp', DOWN))]
    pallas_call x2 -> x3, Pallas kernels: 8.08 us -> 9 us  [contract(): pl.pallas_call(functools.partial(contract_kernel, len(terms), step, tile,...]
    ppermute x17 -> x18, waiting for transfers between devices: 19.1 us -> 19.7 us  [swap(): return lax.ppermute(value, 'mp', pairs)]
    ppermute x17 -> x18, starting transfers between devices: 8.58 us -> 8.59 us  [swap(): return lax.ppermute(value, 'mp', pairs)]
  transfers between devices with their start and end apart: 25 -> 26, of which waited for: 12 -> 13; matrix products, arithmetic and copies ran while one was open for 5% -> 5% of each run, Pallas kernels for 20% -> 23%
where the time goes in v4:
time: 88.1 us; the launch traced here: 87.7 us
  waiting for transfers between devices  32.3 us (37%)
  Pallas kernels  22.3 us (25%)
  starting transfers between devices  17.7 us (20%)
  local copies, waits for them, and re-layouts  11.7 us (13%)
  other arithmetic  2.08 us (2%)
  matrix products  1.07 us (1%)
    ppermute x18, waiting for transfers between devices, swap(): return lax.ppermute(value, 'mp', pairs)  19.7 us
    pallas_call x6, Pallas kernels, project(): pl.pallas_call(functools.partial(project_kernel, wanted, len(parts)), out...  13.2 us
    ppermute x8, waiting for transfers between devices, step(): return (lax.ppermute(pair[0], 'dp', UP), lax.ppermute(pair[1], 'dp', DOWN))  12.6 us
    unnamed x20, local copies, waits for them, and re-layouts  10.5 us
    ppermute x8, starting transfers between devices, step(): return (lax.ppermute(pair[0], 'dp', UP), lax.ppermute(pair[1], 'dp', DOWN))  9.16 us
    pallas_call x3, Pallas kernels, contract(): pl.pallas_call(functools.partial(contract_kernel, len(terms), step, tile,...  9 us
    ppermute x18, starting transfers between devices, swap(): return lax.ppermute(value, 'mp', pairs)  8.59 us
  transfers between devices with their start and end apart: 26, of which 13 were waited for; matrix products, arithmetic and copies ran while one was open for 5% of the time, Pallas kernels for 23%

profile of v4, /device:TPU:0, one launch (start us, length us, event | category | flops | bytes accessed | tf_op | source)
XLA Modules:
  0.0 87.7 jit_solution(7157171299692604468)
XLA Ops:
  0.0 2.9 %collective-permute-start.2 = (bf16[128,3072]{1,0:T(8,128)(2,1)}, bf16[128,3072]{1,0:T(8,128)(2,1)S(1)}, u32[]{:S(2)}, u32[]{:S(2)}) collective-permute-start(bf16[128,3072]{1,0:T(8,128)(2,1)} %refs_2_.1), channel_id=1, source_target_pairs={{0,4},{8,0},{16,8},{24,16},{28,24},{20,28},{12,20},{4,12},{1,5},{9... | collective-permute-start | bytes 2359304 | tf_op jit(solution)/shard_map/ppermute | solution.py:229
  3.0 1.1 %constant_dynamic-slice_fusion = (bf16[256,384]{1,0:T(8,128)(2,1)S(1)}, bf16[256,384]{1,0:T(8,128)(2,1)S(1)}) fusion(bf16[256,768]{1,0:T(8,128)(2,1)} %param.10, s32[]{:T(128)S(6)} %select_n.103, s32[]{:T(128)S(6)} %select_n.104), kind=kLoop, calls=%fused_computation.91 | loop fusion | bytes 786440 | tf_op jit(solution)/shard_map/dynamic_slice | solution.py:232
  4.2 2.3 %copy-done = bf16[768,3072]{1,0:T(8,128)(2,1)S(1)} copy-done((bf16[768,3072]{1,0:T(8,128)(2,1)S(1)}, bf16[768,3072]{1,0:T(8,128)(2,1)}, u32[]{:S(2)}) %copy-start) | copy-done | bytes 4718616
  6.5 2.3 %copy-done.2 = bf16[768,3072]{1,0:T(8,128)(2,1)S(1)} copy-done((bf16[768,3072]{1,0:T(8,128)(2,1)S(1)}, bf16[768,3072]{1,0:T(8,128)(2,1)}, u32[]{:S(2)}) %copy-start.2) | copy-done | bytes 4718616
  8.9 1.1 %copy-done.4 = bf16[128,3072]{1,0:T(8,128)(2,1)S(1)} copy-done((bf16[128,3072]{1,0:T(8,128)(2,1)S(1)}, bf16[128,3072]{1,0:T(8,128)(2,1)}, u32[]{:S(2)}) %copy-start.4) | copy-done | bytes 786456
  10.0 2.6 %project.7 = (bf16[768,128]{1,0:T(8,128)(2,1)S(1)}, bf16[768,128]{1,0:T(8,128)(2,1)S(1)}) custom-call(s32[1]{0:T(128)} %bitcast.which_ref, bf16[768,3072]{1,0:T(8,128)(2,1)S(1)} %copy-done.2, bf16[768,3072]{1,0:T(8,128)(2,1)S(1)} %copy-done, bf16[128,3072]{1,0:T(8,128)(2,1)S(1)} %copy-done.4), custom_call_target="tpu_custom_call" | custom-call | flops 362387872 | tf_op jit(solution)/shard_map/project/pallas_call | solution.py:118
  12.6 0.6 collective-permute-start.4
  13.1 0.7 fusion.46
  14.2 6.6 %collective-permute-done.2.refs_1_ = bf16[128,3072]{1,0:T(8,128)(2,1)S(1)} collective-permute-done((bf16[128,3072]{1,0:T(8,128)(2,1)}, bf16[128,3072]{1,0:T(8,128)(2,1)S(1)}, u32[]{:S(2)}, u32[]{:S(2)}) %collective-permute-start.2) | collective-permute-done | bytes 786464 | tf_op jit(solution)/shard_map/ppermute | solution.py:229
  20.8 1.7 %collective-permute-start.3 = (bf16[128,3072]{1,0:T(8,128)(2,1)S(1)}, bf16[128,3072]{1,0:T(8,128)(2,1)S(1)}, u32[]{:S(2)}, u32[]{:S(2)}) collective-permute-start(bf16[128,3072]{1,0:T(8,128)(2,1)S(1)} %collective-permute-done.2.refs_1_), channel_id=1, source_target_pairs={{0,4},{8,0},{16,8},{24,16},{28,24},{20,28},{12,20},{4,12},{1,5},{9... | collective-permute-start | bytes 2359304 | tf_op jit(solution)/shard_map/ppermute | solution.py:229
  22.4 0.4 collective-permute-start.1
  22.9 1.8 %collective-permute-start.7 = (bf16[512,384]{1,0:T(8,128)(2,1)S(1)}, bf16[512,384]{1,0:T(8,128)(2,1)S(1)}, u32[]{:S(2)}, u32[]{:S(2)}) collective-permute-start(bf16[512,384]{1,0:T(8,128)(2,1)S(1)} %pad_maximum_fusion), channel_id=1, source_target_pairs={{0,2},{1,3},{2,0},{3,1},{4,6},{5,7},{6,4},{7,5},{8,10},{9,11},{10,... | collective-permute-start | bytes 1179656 | tf_op jit(solution)/shard_map/ppermute | solution.py:223
  24.6 2.3 %copy-done.1 = bf16[768,3072]{1,0:T(8,128)(2,1)S(1)} copy-done((bf16[768,3072]{1,0:T(8,128)(2,1)S(1)}, bf16[768,3072]{1,0:T(8,128)(2,1)}, u32[]{:S(2)}) %copy-start.1) | copy-done | bytes 4718616
  26.9 2.3 %copy-done.3 = bf16[768,3072]{1,0:T(8,128)(2,1)S(1)} copy-done((bf16[768,3072]{1,0:T(8,128)(2,1)S(1)}, bf16[768,3072]{1,0:T(8,128)(2,1)}, u32[]{:S(2)}) %copy-start.3) | copy-done | bytes 4718616
  29.3 2.6 %project.6 = (bf16[768,256]{1,0:T(8,128)(2,1)S(1)}, bf16[768,256]{1,0:T(8,128)(2,1)S(1)}, bf16[256,3072]{1,0:T(8,128)(2,1)S(1)}) custom-call(s32[1]{0:T(128)} %bitcast.which_ref, bf16[768,3072]{1,0:T(8,128)(2,1)S(1)} %copy-done.3, bf16[768,3072]{1,0:T(8,128)(2,1)S(1)} %copy-done.1, bf16[128,3072]{1,0:T(8,128)(2,1)S(1)} %collective-permute-done.refs_0_, ...), custom_call_target="tpu_custom_call" | custom-call | flops 362387872 | tf_op jit(solution)/shard_map/project/pallas_call | solution.py:118
  32.1 0.4 collective-permute-start.5
  32.5 7.0 %collective-permute-done.5 = bf16[768,128]{1,0:T(8,128)(2,1)S(1)} collective-permute-done((bf16[768,128]{1,0:T(8,128)(2,1)S(1)}, bf16[768,128]{1,0:T(8,128)(2,1)S(1)}, u32[]{:S(2)}, u32[]{:S(2)}) %collective-permute-start.5) | collective-permute-done | bytes 196640 | tf_op jit(solution)/shard_map/ppermute | solution.py:223
  39.5 1.1 %collective-permute-done.1.refs_0_ = bf16[128,3072]{1,0:T(8,128)(2,1)S(1)} collective-permute-done((bf16[128,3072]{1,0:T(8,128)(2,1)S(1)}, bf16[128,3072]{1,0:T(8,128)(2,1)S(1)}, u32[]{:S(2)}, u32[]{:S(2)}) %collective-permute-start.1) | collective-permute-done | bytes 786464 | tf_op jit(solution)/shard_map/ppermute | solution.py:229
  40.6 0.7 collective-permute-start.9
  41.3 1.3 %collective-permute-start.10 = (bf16[128,3072]{1,0:T(8,128)(2,1)S(1)}, bf16[128,3072]{1,0:T(8,128)(2,1)S(1)}, u32[]{:S(2)}, u32[]{:S(2)}) collective-permute-start(bf16[128,3072]{1,0:T(8,128)(2,1)S(1)} %collective-permute-done.3.refs_1_), channel_id=1, source_target_pairs={{0,4},{8,0},{16,8},{24,16},{28,24},{20,28},{12,20},{4,12},{1,5},{9... | collective-permute-start | bytes 2359304 | tf_op jit(solution)/shard_map/ppermute | solution.py:229
  42.6 2.6 %project.8 = (bf16[768,256]{1,0:T(8,128)(2,1)S(1)}, bf16[768,256]{1,0:T(8,128)(2,1)S(1)}, bf16[256,3072]{1,0:T(8,128)(2,1)S(1)}) custom-call(s32[1]{0:T(128)} %bitcast.which_ref, bf16[768,3072]{1,0:T(8,128)(2,1)S(1)} %copy-done.3, bf16[768,3072]{1,0:T(8,128)(2,1)S(1)} %copy-done.1, bf16[128,3072]{1,0:T(8,128)(2,1)S(1)} %collective-permute-done.1.refs_0_, ...), custom_call_target="tpu_custom_call" | custom-call | flops 362387872 | tf_op jit(solution)/shard_map/project/pallas_call | solution.py:118
  45.4 1.6 %collective-permute-start.12 = (bf16[768,256]{1,0:T(8,128)(2,1)S(1)}, bf16[768,256]{1,0:T(8,128)(2,1)S(1)}, u32[]{:S(2)}, u32[]{:S(2)}) collective-permute-start(bf16[768,256]{1,0:T(8,128)(2,1)S(1)} %get-tuple-element.81), channel_id=1, source_target_pairs={{0,2},{1,3},{2,0},{3,1},{4,6},{5,7},{6,4},{7,5},{8,10},{9,11},{10,... | collective-permute-start | bytes 1179656 | tf_op jit(solution)/shard_map/ppermute | solution.py:223
  47.0 1.1 %fusion = f32[384,1024]{1,0:T(8,128)S(1)} fusion(s32[1024]{0:T(1024)S(1)} %fusion.35, bf16[512,384]{1,0:T(8,128)(2,1)S(1)} %collective-permute-done.7, bf16[256,384]{1,0:T(8,128)(2,1)S(1)} %collective-permute-done.6, bf16[256,384]{1,0:T(8,128)(2,1)S(1)} %get-tuple-element.85), kind=kOutput, calls=%fused_computation.1 | convolution fusion | flops 808714240 | bytes 2363392 | tf_op jit(solution)/shard_map/dot_general | solution.py:18
  48.2 0.6 collective-permute-start.16
  48.8 8.6 %collective-permute-done.12 = bf16[768,256]{1,0:T(8,128)(2,1)S(1)} collective-permute-done((bf16[768,256]{1,0:T(8,128)(2,1)S(1)}, bf16[768,256]{1,0:T(8,128)(2,1)S(1)}, u32[]{:S(2)}, u32[]{:S(2)}) %collective-permute-start.12) | collective-permute-done | bytes 393248 | tf_op jit(solution)/shard_map/ppermute | solution.py:223
  57.4 1.3 %collective-permute-done.9.refs_0_ = bf16[128,3072]{1,0:T(8,128)(2,1)S(1)} collective-permute-done((bf16[128,3072]{1,0:T(8,128)(2,1)S(1)}, bf16[128,3072]{1,0:T(8,128)(2,1)S(1)}, u32[]{:S(2)}, u32[]{:S(2)}) %collective-permute-start.9) | collective-permute-done | bytes 786464 | tf_op jit(solution)/shard_map/ppermute | solution.py:229
  58.6 1.3 %collective-permute-done.10.refs_1_ = bf16[128,3072]{1,0:T(8,128)(2,1)S(1)} collective-permute-done((bf16[128,3072]{1,0:T(8,128)(2,1)S(1)}, bf16[128,3072]{1,0:T(8,128)(2,1)S(1)}, u32[]{:S(2)}, u32[]{:S(2)}) %collective-permute-start.10) | collective-permute-done | bytes 786464 | tf_op jit(solution)/shard_map/ppermute | solution.py:229
  60.0 0.5 collective-permute-start.14
  60.5 1.6 %collective-permute-start.13 = (bf16[64,3072]{1,0:T(8,128)(2,1)S(1)}, bf16[64,3072]{1,0:T(8,128)(2,1)S(1)}, u32[]{:S(2)}, u32[]{:S(2)}) collective-permute-start(bf16[64,3072]{1,0:T(8,128)(2,1)S(1)} %slice.71), channel_id=1, source_target_pairs={{0,8},{8,16},{16,24},{24,28},{28,20},{20,12},{12,4},{4,0},{1,9},{9... | collective-permute-start | bytes 1179656 | tf_op jit(solution)/shard_map/ppermute | solution.py:229
  62.1 2.6 %project.9 = (bf16[384,256]{1,0:T(8,128)(2,1)S(1)}, bf16[384,256]{1,0:T(8,128)(2,1)S(1)}, bf16[768,256]{1,0:T(8,128)(2,1)S(1)}, bf16[256,3072]{1,0:T(8,128)(2,1)S(1)}) custom-call(s32[1]{0:T(128)} %bitcast.which_ref, bf16[768,3072]{1,0:T(8,128)(2,1)S(1)} %copy-done.3, bf16[768,3072]{1,0:T(8,128)(2,1)S(1)} %copy-done.1, ...), custom_call_target="tpu_custom_call" | custom-call | flops 362387872 | tf_op jit(solution)/shard_map/project/pallas_call | solution.py:118
  64.8 0.5 collective-permute-start.21
  65.4 0.9 collective-permute-done.20.refs_0_
  66.3 0.1 collective-permute-start.8
  66.4 0.1 collective-permute-done.21.refs_1_
  66.6 0.1 merge.1
  66.7 0.6 collective-permute-start.22
  67.3 2.2 %collective-permute-done.14.refs_1_ = bf16[64,3072]{1,0:T(8,128)(2,1)S(1)} collective-permute-done((bf16[64,3072]{1,0:T(8,128)(2,1)S(1)}, bf16[64,3072]{1,0:T(8,128)(2,1)S(1)}, u32[]{:S(2)}, u32[]{:S(2)}) %collective-permute-start.14) | collective-permute-done | bytes 393248 | tf_op jit(solution)/shard_map/ppermute | solution.py:229
  69.4 0.2 collective-permute-done.13.refs_0_
  69.7 1.4 %project.10 = (bf16[768,128]{1,0:T(8,128)(2,1)S(1)}, bf16[128,3072]{1,0:T(8,128)(2,1)S(1)}) custom-call(s32[1]{0:T(128)} %bitcast.which_ref, bf16[768,3072]{1,0:T(8,128)(2,1)S(1)} %copy-done.3, bf16[768,3072]{1,0:T(8,128)(2,1)S(1)} %copy-done.1, bf16[64,3072]{1,0:T(8,128)(2,1)S(1)} %collective-permute-done.13.refs_0_, ...), custom_call_target="tpu_custom_call" | custom-call | flops 181193936 | tf_op jit(solution)/shard_map/project/pallas_call | solution.py:118
  71.3 0.2 fusion.12
  71.5 0.6 collective-permute-start.18
  72.2 1.4 %project.11 = bf16[768,128]{1,0:T(8,128)(2,1)S(1)} custom-call(s32[1]{0:T(128)} %bitcast.which_ref, bf16[768,3072]{1,0:T(8,128)(2,1)S(1)} %copy-done.3, bf16[768,3072]{1,0:T(8,128)(2,1)S(1)} %copy-done.1, bf16[128,3072]{1,0:T(8,128)(2,1)S(1)} %get-tuple-element.64.refs_0_.refs_3_), custom_call_target="tpu_custom_call" | custom-call | flops 181193936 | tf_op jit(solution)/shard_map/project/pallas_call | solution.py:118
  73.6 1.1 %collective-permute-start.24 = (bf16[768,128]{1,0:T(8,128)(2,1)S(1)}, bf16[768,128]{1,0:T(8,128)(2,1)S(1)}, u32[]{:S(2)}, u32[]{:S(2)}) collective-permute-start(bf16[768,128]{1,0:T(8,128)(2,1)S(1)} %get-tuple-element.83), channel_id=1, source_target_pairs={{0,2},{1,3},{2,0},{3,1},{4,6},{5,7},{6,4},{7,5},{8,10},{9,11},{10,... | collective-permute-start | bytes 589832 | tf_op jit(solution)/shard_map/ppermute | solution.py:223
  74.7 3.8 %contract.3.base_ref = f32[768,3072]{1,0:T(8,128)S(1)} custom-call(s32[1]{0:T(128)} %bitcast.which_ref, bf16[768,3072]{1,0:T(8,128)(2,1)S(1)} %bitcast.12, bf16[384,128]{1,0:T(8,128)(2,1)S(1)} %fusion.27.refs_0_, bf16[384,128]{1,0:T(8,128)(2,1)S(1)} %collective-permute-done.8.refs_1_, bf16[128,3072]{1,0:T(8,128)(2,1)S(1)} %copy-done.5, ...), custom_call_target="tpu_custom_call" | custom-call | flops 452984832 | tf_op jit(solution)/shard_map/contract/pallas_call | solution.py:201
  78.9 0.4 collective-permute-start.23
  79.3 2.9 %collective-permute-done.24 = bf16[768,128]{1,0:T(8,128)(2,1)S(1)} collective-permute-done((bf16[768,128]{1,0:T(8,128)(2,1)S(1)}, bf16[768,128]{1,0:T(8,128)(2,1)S(1)}, u32[]{:S(2)}, u32[]{:S(2)}) %collective-permute-start.24) | collective-permute-done | bytes 196640 | tf_op jit(solution)/shard_map/ppermute | solution.py:223
  82.4 2.6 %contract.4.refs_4_ = f32[768,3072]{1,0:T(8,128)} custom-call(s32[1]{0:T(128)} %bitcast.which_ref, f32[768,3072]{1,0:T(8,128)S(1)} %contract.3.base_ref, bf16[384,256]{1,0:T(8,128)(2,1)S(1)} %fusion.7.refs_0_, bf16[256,3072]{1,0:T(8,128)(2,1)S(1)} %get-tuple-element.73.refs_1_, bf16[384,128]{1,0:T(8,128)(2,1)S(1)} %fusion.22.refs_2_, ...), custom_call_target="tpu_custom_call" | custom-call | flops 271790912 | tf_op jit(solution)/shard_map/contract/pallas_call | solution.py:201
  85.0 2.6 %contract.5 = f32[768,3072]{1,0:T(8,128)} custom-call(s32[1]{0:T(128)} %bitcast.which_ref, f32[768,3072]{1,0:T(8,128)S(1)} %contract.3.base_ref, bf16[384,256]{1,0:T(8,128)(2,1)S(1)} %collective-permute-done.23.refs_0_, bf16[256,3072]{1,0:T(8,128)(2,1)S(1)} %get-tuple-element.73.refs_1_, ...), custom_call_target="tpu_custom_call", output_to_operand_aliasing={{}: (6, {})} | custom-call | flops 271790912 | tf_op jit(solution)/shard_map/contract/pallas_call | solution.py:201
  (62 shorter events, 2.1 us)
Async XLA Ops:
  0.0 20.8 %collective-permute-start.2 = (bf16[128,3072]{1,0:T(8,128)(2,1)}, bf16[128,3072]{1,0:T(8,128)(2,1)S(1)}, u32[]{:S(2)}, u32[]{:S(2)}) collective-permute-start(bf16[128,3072]{1,0:T(8,128)(2,1)} %refs_2_.1), channel_id=1, source_target_pairs={{0,4},{8,0},{16,8},{24,16},{28,24},{20,28},{12,20},{4,12},{1,5},{9... | collective-permute-start | bytes 2359304 | tf_op jit(solution)/shard_map/ppermute | solution.py:229
  2.9 19.5 %collective-permute-start = (bf16[128,3072]{1,0:T(8,128)(2,1)}, bf16[128,3072]{1,0:T(8,128)(2,1)S(1)}, u32[]{:S(2)}, u32[]{:S(2)}) collective-permute-start(bf16[128,3072]{1,0:T(8,128)(2,1)} %refs_2_.1), channel_id=1, source_target_pairs={{0,8},{8,16},{16,24},{24,28},{28,20},{20,12},{12,4},{4,0},{1,9},{9... | collective-permute-start | bytes 2359304 | tf_op jit(solution)/shard_map/ppermute | solution.py:229
  4.1 18.7 %collective-permute-start.6 = (bf16[256,384]{1,0:T(8,128)(2,1)S(1)}, bf16[256,384]{1,0:T(8,128)(2,1)S(1)}, u32[]{:S(2)}, u32[]{:S(2)}) collective-permute-start(bf16[256,384]{1,0:T(8,128)(2,1)S(1)} %get-tuple-element.86), channel_id=1, source_target_pairs={{0,1},{1,0},{2,3},{3,2},{4,5},{5,4},{6,7},{7,6},{8,9},{9,8},{10,11... | collective-permute-start | bytes 589832 | tf_op jit(solution)/shard_map/ppermute | solution.py:223
  4.2 2.3 %copy-start = (bf16[768,3072]{1,0:T(8,128)(2,1)S(1)}, bf16[768,3072]{1,0:T(8,128)(2,1)}, u32[]{:S(2)}) copy-start(bf16[768,3072]{1,0:T(8,128)(2,1)} %base_ref.1) | copy-start | bytes 14155780
  6.5 2.3 %copy-start.2 = (bf16[768,3072]{1,0:T(8,128)(2,1)S(1)}, bf16[768,3072]{1,0:T(8,128)(2,1)}, u32[]{:S(2)}) copy-start(bf16[768,3072]{1,0:T(8,128)(2,1)} %w_ref.11) | copy-start | bytes 14155780
  8.8 1.1 %copy-start.4 = (bf16[128,3072]{1,0:T(8,128)(2,1)S(1)}, bf16[128,3072]{1,0:T(8,128)(2,1)}, u32[]{:S(2)}) copy-start(bf16[128,3072]{1,0:T(8,128)(2,1)} %refs_2_.1) | copy-start | bytes 2359300
  10.0 4.0 %copy-start.6 = (s32[4]{0:T(128)S(1)}, s32[4]{0:T(128)}, u32[]{:S(2)}) copy-start(s32[4]{0:T(128)} %param.11) | copy-start | bytes 52
  10.0 4.1 %copy-start.7 = (f32[4]{0:T(128)S(1)}, f32[4]{0:T(128)}, u32[]{:S(2)}) copy-start(f32[4]{0:T(128)} %param.12) | copy-start | bytes 52
  12.6 19.4 %collective-permute-start.4 = (bf16[768,128]{1,0:T(8,128)(2,1)S(1)}, bf16[768,128]{1,0:T(8,128)(2,1)S(1)}, u32[]{:S(2)}, u32[]{:S(2)}) collective-permute-start(bf16[768,128]{1,0:T(8,128)(2,1)S(1)} %get-tuple-element.43), channel_id=1, source_target_pairs={{0,1},{1,0},{2,3},{3,2},{4,5},{5,4},{6,7},{7,6},{8,9},{9,8},{10,11... | collective-permute-start | bytes 589832 | tf_op jit(solution)/shard_map/ppermute | solution.py:223
  20.8 18.7 %collective-permute-start.3 = (bf16[128,3072]{1,0:T(8,128)(2,1)S(1)}, bf16[128,3072]{1,0:T(8,128)(2,1)S(1)}, u32[]{:S(2)}, u32[]{:S(2)}) collective-permute-start(bf16[128,3072]{1,0:T(8,128)(2,1)S(1)} %collective-permute-done.2.refs_1_), channel_id=1, source_target_pairs={{0,4},{8,0},{16,8},{24,16},{28,24},{20,28},{12,20},{4,12},{1,5},{9... | collective-permute-start | bytes 2359304 | tf_op jit(solution)/shard_map/ppermute | solution.py:229
  22.4 18.1 %collective-permute-start.1 = (bf16[128,3072]{1,0:T(8,128)(2,1)S(1)}, bf16[128,3072]{1,0:T(8,128)(2,1)S(1)}, u32[]{:S(2)}, u32[]{:S(2)}) collective-permute-start(bf16[128,3072]{1,0:T(8,128)(2,1)S(1)} %collective-permute-done.refs_0_), channel_id=1, source_target_pairs={{0,8},{8,16},{16,24},{24,28},{28,20},{20,12},{12,4},{4,0},{1,9},{9... | collective-permute-start | bytes 2359304 | tf_op jit(solution)/shard_map/ppermute | solution.py:229
  22.9 16.6 %collective-permute-start.7 = (bf16[512,384]{1,0:T(8,128)(2,1)S(1)}, bf16[512,384]{1,0:T(8,128)(2,1)S(1)}, u32[]{:S(2)}, u32[]{:S(2)}) collective-permute-start(bf16[512,384]{1,0:T(8,128)(2,1)S(1)} %pad_maximum_fusion), channel_id=1, source_target_pairs={{0,2},{1,3},{2,0},{3,1},{4,6},{5,7},{6,4},{7,5},{8,10},{9,11},{10,... | collective-permute-start | bytes 1179656 | tf_op jit(solution)/shard_map/ppermute | solution.py:223
  24.6 2.3 %copy-start.1 = (bf16[768,3072]{1,0:T(8,128)(2,1)S(1)}, bf16[768,3072]{1,0:T(8,128)(2,1)}, u32[]{:S(2)}) copy-start(bf16[768,3072]{1,0:T(8,128)(2,1)} %base_ref.1) | copy-start | bytes 14155780
  26.9 2.3 %copy-start.3 = (bf16[768,3072]{1,0:T(8,128)(2,1)S(1)}, bf16[768,3072]{1,0:T(8,128)(2,1)}, u32[]{:S(2)}) copy-start(bf16[768,3072]{1,0:T(8,128)(2,1)} %w_ref.11) | copy-start | bytes 14155780
  31.9 13.4 %collective-permute-start.11 = (bf16[768,256]{1,0:T(8,128)(2,1)S(1)}, bf16[768,256]{1,0:T(8,128)(2,1)S(1)}, u32[]{:S(2)}, u32[]{:S(2)}) collective-permute-start(bf16[768,256]{1,0:T(8,128)(2,1)S(1)} %get-tuple-element.50), channel_id=1, source_target_pairs={{0,1},{1,0},{2,3},{3,2},{4,5},{5,4},{6,7},{7,6},{8,9},{9,8},{10,11... | collective-permute-start | bytes 1179656 | tf_op jit(solution)/shard_map/ppermute | solution.py:223
  32.1 7.4 %collective-permute-start.5 = (bf16[768,128]{1,0:T(8,128)(2,1)S(1)}, bf16[768,128]{1,0:T(8,128)(2,1)S(1)}, u32[]{:S(2)}, u32[]{:S(2)}) collective-permute-start(bf16[768,128]{1,0:T(8,128)(2,1)S(1)} %get-tuple-element.87), channel_id=1, source_target_pairs={{0,2},{1,3},{2,0},{3,1},{4,6},{5,7},{6,4},{7,5},{8,10},{9,11},{10,... | collective-permute-start | bytes 589832 | tf_op jit(solution)/shard_map/ppermute | solution.py:223
  40.6 18.1 %collective-permute-start.9 = (bf16[128,3072]{1,0:T(8,128)(2,1)S(1)}, bf16[128,3072]{1,0:T(8,128)(2,1)S(1)}, u32[]{:S(2)}, u32[]{:S(2)}) collective-permute-start(bf16[128,3072]{1,0:T(8,128)(2,1)S(1)} %collective-permute-done.1.refs_0_), channel_id=1, source_target_pairs={{0,8},{8,16},{16,24},{24,28},{28,20},{20,12},{12,4},{4,0},{1,9},{9... | collective-permute-start | bytes 2359304 | tf_op jit(solution)/shard_map/ppermute | solution.py:229
  41.3 18.7 %collective-permute-start.10 = (bf16[128,3072]{1,0:T(8,128)(2,1)S(1)}, bf16[128,3072]{1,0:T(8,128)(2,1)S(1)}, u32[]{:S(2)}, u32[]{:S(2)}) collective-permute-start(bf16[128,3072]{1,0:T(8,128)(2,1)S(1)} %collective-permute-done.3.refs_1_), channel_id=1, source_target_pairs={{0,4},{8,0},{16,8},{24,16},{28,24},{20,28},{12,20},{4,12},{1,5},{9... | collective-permute-start | bytes 2359304 | tf_op jit(solution)/shard_map/ppermute | solution.py:229
  45.2 2.9 %collective-permute-start.15 = (bf16[768,256]{1,0:T(8,128)(2,1)S(1)}, bf16[768,256]{1,0:T(8,128)(2,1)S(1)}, u32[]{:S(2)}, u32[]{:S(2)}) collective-permute-start(bf16[768,256]{1,0:T(8,128)(2,1)S(1)} %get-tuple-element.54), channel_id=1, source_target_pairs={{0,1},{1,0},{2,3},{3,2},{4,5},{5,4},{6,7},{7,6},{8,9},{9,8},{10,11... | collective-permute-start | bytes 1179656 | tf_op jit(solution)/shard_map/ppermute | solution.py:223
  45.4 12.0 %collective-permute-start.12 = (bf16[768,256]{1,0:T(8,128)(2,1)S(1)}, bf16[768,256]{1,0:T(8,128)(2,1)S(1)}, u32[]{:S(2)}, u32[]{:S(2)}) collective-permute-start(bf16[768,256]{1,0:T(8,128)(2,1)S(1)} %get-tuple-element.81), channel_id=1, source_target_pairs={{0,2},{1,3},{2,0},{3,1},{4,6},{5,7},{6,4},{7,5},{8,10},{9,11},{10,... | collective-permute-start | bytes 1179656 | tf_op jit(solution)/shard_map/ppermute | solution.py:223
  48.2 19.1 %collective-permute-start.16 = (bf16[768,256]{1,0:T(8,128)(2,1)S(1)}, bf16[768,256]{1,0:T(8,128)(2,1)S(1)}, u32[]{:S(2)}, u32[]{:S(2)}) collective-permute-start(bf16[768,256]{1,0:T(8,128)(2,1)S(1)} %get-tuple-element.79), channel_id=1, source_target_pairs={{0,2},{1,3},{2,0},{3,1},{4,6},{5,7},{6,4},{7,5},{8,10},{9,11},{10,... | collective-permute-start | bytes 1179656 | tf_op jit(solution)/shard_map/ppermute | solution.py:223
  60.0 9.4 %collective-permute-start.14 = (bf16[64,3072]{1,0:T(8,128)(2,1)S(1)}, bf16[64,3072]{1,0:T(8,128)(2,1)S(1)}, u32[]{:S(2)}, u32[]{:S(2)}) collective-permute-start(bf16[64,3072]{1,0:T(8,128)(2,1)S(1)} %slice.72), channel_id=1, source_target_pairs={{0,4},{8,0},{16,8},{24,16},{28,24},{20,28},{12,20},{4,12},{1,5},{9... | collective-permute-start | bytes 1179656 | tf_op jit(solution)/shard_map/ppermute | solution.py:229
  60.5 9.1 %collective-permute-start.13 = (bf16[64,3072]{1,0:T(8,128)(2,1)S(1)}, bf16[64,3072]{1,0:T(8,128)(2,1)S(1)}, u32[]{:S(2)}, u32[]{:S(2)}) collective-permute-start(bf16[64,3072]{1,0:T(8,128)(2,1)S(1)} %slice.71), channel_id=1, source_target_pairs={{0,8},{8,16},{16,24},{24,28},{28,20},{20,12},{12,4},{4,0},{1,9},{9... | collective-permute-start | bytes 1179656 | tf_op jit(solution)/shard_map/ppermute | solution.py:229
  64.8 1.5 %collective-permute-start.20 = (bf16[384,256]{1,0:T(8,128)(2,1)S(1)}, bf16[384,256]{1,0:T(8,128)(2,1)S(1)}, u32[]{:S(2)}, u32[]{:S(2)}) collective-permute-start(bf16[384,256]{1,0:T(8,128)(2,1)S(1)} %get-tuple-element.67), channel_id=1, source_target_pairs={{0,1},{1,0},{2,3},{3,2},{4,5},{5,4},{6,7},{7,6},{8,9},{9,8},{10,11... | collective-permute-start | bytes 589832 | tf_op jit(solution)/shard_map/ppermute | solution.py:223
  64.8 1.7 %collective-permute-start.21 = (bf16[384,256]{1,0:T(8,128)(2,1)S(1)}, bf16[384,256]{1,0:T(8,128)(2,1)S(1)}, u32[]{:S(2)}, u32[]{:S(2)}) collective-permute-start(bf16[384,256]{1,0:T(8,128)(2,1)S(1)} %get-tuple-element.68), channel_id=1, source_target_pairs={{0,1},{1,0},{2,3},{3,2},{4,5},{5,4},{6,7},{7,6},{8,9},{9,8},{10,11... | collective-permute-start | bytes 589832 | tf_op jit(solution)/shard_map/ppermute | solution.py:223
  66.3 8.4 %collective-permute-start.8 = (bf16[384,128]{1,0:T(8,128)(2,1)S(1)}, bf16[384,128]{1,0:T(8,128)(2,1)S(1)}, u32[]{:S(2)}, u32[]{:S(2)}) collective-permute-start(bf16[384,128]{1,0:T(8,128)(2,1)S(1)} %fusion.27.refs_0_), channel_id=1, source_target_pairs={{0,1},{1,0},{2,3},{3,2},{4,5},{5,4},{6,7},{7,6},{8,9},{9,8},{10,11... | collective-permute-start | bytes 294920 | tf_op jit(solution)/shard_map/ppermute | solution.py:223
  66.7 12.0 %collective-permute-start.22 = (bf16[768,256]{1,0:T(8,128)(2,1)S(1)}, bf16[768,256]{1,0:T(8,128)(2,1)S(1)}, u32[]{:S(2)}, u32[]{:S(2)}) collective-permute-start(bf16[768,256]{1,0:T(8,128)(2,1)S(1)} %get-tuple-element.72), channel_id=1, source_target_pairs={{0,2},{1,3},{2,0},{3,1},{4,6},{5,7},{6,4},{7,5},{8,10},{9,11},{10,... | collective-permute-start | bytes 1179656 | tf_op jit(solution)/shard_map/ppermute | solution.py:223
  71.0 2.5 %collective-permute-start.19 = (bf16[768,128]{1,0:T(8,128)(2,1)S(1)}, bf16[768,128]{1,0:T(8,128)(2,1)S(1)}, u32[]{:S(2)}, u32[]{:S(2)}) collective-permute-start(bf16[768,128]{1,0:T(8,128)(2,1)S(1)} %get-tuple-element.65), channel_id=1, source_target_pairs={{0,1},{1,0},{2,3},{3,2},{4,5},{5,4},{6,7},{7,6},{8,9},{9,8},{10,11... | collective-permute-start | bytes 589832 | tf_op jit(solution)/shard_map/ppermute | solution.py:223
  71.5 3.2 %collective-permute-start.18 = (bf16[384,256]{1,0:T(8,128)(2,1)S(1)}, bf16[384,256]{1,0:T(8,128)(2,1)S(1)}, u32[]{:S(2)}, u32[]{:S(2)}) collective-permute-start(bf16[384,256]{1,0:T(8,128)(2,1)S(1)} %get-tuple-element.77.refs_6_), channel_id=1, source_target_pairs={{0,1},{1,0},{2,3},{3,2},{4,5},{5,4},{6,7},{7,6},{8,9},{9,8},{10,11... | collective-permute-start | bytes 589832 | tf_op jit(solution)/shard_map/ppermute | solution.py:223
  72.1 2.6 %collective-permute-start.17 = (bf16[384,256]{1,0:T(8,128)(2,1)S(1)}, bf16[384,256]{1,0:T(8,128)(2,1)S(1)}, u32[]{:S(2)}, u32[]{:S(2)}) collective-permute-start(bf16[384,256]{1,0:T(8,128)(2,1)S(1)} %get-tuple-element.78.refs_3_), channel_id=1, source_target_pairs={{0,1},{1,0},{2,3},{3,2},{4,5},{5,4},{6,7},{7,6},{8,9},{9,8},{10,11... | collective-permute-start | bytes 589832 | tf_op jit(solution)/shard_map/ppermute | solution.py:223
  72.2 2.5 %slice-start = ((s8[4718592]{0:T(1024)(128)(4,1)}), s8[4194304]{0:T(1024)(128)(4,1)S(1)}, s32[]{:S(2)}) async-start(s8[4718592]{0:T(1024)(128)(4,1)} %bitcast.11), calls=%async_computation | async-start | bytes 8388608
  72.2 2.5 %slice-start.1 = ((s8[4718592]{0:T(1024)(128)(4,1)}), s8[524288]{0:T(1024)(128)(4,1)S(1)}, s32[]{:S(2)}) async-start(s8[4718592]{0:T(1024)(128)(4,1)} %bitcast.11), calls=%async_computation.1 | async-start | bytes 1048576
  72.2 2.6 %copy-start.5 = (bf16[128,3072]{1,0:T(8,128)(2,1)S(1)}, bf16[128,3072]{1,0:T(8,128)(2,1)}, u32[]{:S(2)}) copy-start(bf16[128,3072]{1,0:T(8,128)(2,1)} %refs_2_.1) | copy-start | bytes 2359300
  73.6 8.6 %collective-permute-start.24 = (bf16[768,128]{1,0:T(8,128)(2,1)S(1)}, bf16[768,128]{1,0:T(8,128)(2,1)S(1)}, u32[]{:S(2)}, u32[]{:S(2)}) collective-permute-start(bf16[768,128]{1,0:T(8,128)(2,1)S(1)} %get-tuple-element.83), channel_id=1, source_target_pairs={{0,2},{1,3},{2,0},{3,1},{4,6},{5,7},{6,4},{7,5},{8,10},{9,11},{10,... | collective-permute-start | bytes 589832 | tf_op jit(solution)/shard_map/ppermute | solution.py:223
  78.9 6.1 %collective-permute-start.23 = (bf16[384,256]{1,0:T(8,128)(2,1)S(1)}, bf16[384,256]{1,0:T(8,128)(2,1)S(1)}, u32[]{:S(2)}, u32[]{:S(2)}) collective-permute-start(bf16[384,256]{1,0:T(8,128)(2,1)S(1)} %fusion.7.refs_0_), channel_id=1, source_target_pairs={{0,1},{1,0},{2,3},{3,2},{4,5},{5,4},{6,7},{7,6},{8,9},{9,8},{10,11... | collective-permute-start | bytes 589832 | tf_op jit(solution)/shard_map/ppermute | solution.py:223
  82.3 2.7 %collective-permute-start.25 = (bf16[384,128]{1,0:T(8,128)(2,1)S(1)}, bf16[384,128]{1,0:T(8,128)(2,1)S(1)}, u32[]{:S(2)}, u32[]{:S(2)}) collective-permute-start(bf16[384,128]{1,0:T(8,128)(2,1)S(1)} %fusion.22.refs_2_), channel_id=1, source_target_pairs={{0,1},{1,0},{2,3},{3,2},{4,5},{5,4},{6,7},{7,6},{8,9},{9,8},{10,11... | collective-permute-start | bytes 294920 | tf_op jit(solution)/shard_map/ppermute | solution.py:223

commit v5 on v4

--- a/solution.py
+++ b/solution.py
@@ -285,8 +285,10 @@
     scaled0 = weigh(aligned, chip0, across0, 0)
     *hop3, kept2, chip1, across1 = gate(*hop3, kept2, chip1, across1)
     hop4 = step((hop3[0][:half], hop3[1][half:]))
-    *theirs3, kept3, block3 = project(one, w_out, direction, hop3, ((1, (0,)), (1, (1,)), KEEP))
-    chip3, sent3 = merge(kept3, *[swap(v, CORE) for v in theirs3])
+    *theirs3, block3 = project(one, w_out, direction, hop3, ((1, (0,)), (1, (1,))))
+    theirs3 = [swap(v, CORE) for v in theirs3]
+    (kept3,) = project(one, w_out, direction, [block3], (KEEP,))
+    chip3, sent3 = merge(kept3, *theirs3)
     across3 = swap(sent3, ROW)
     *hop4, kept3, chip2, across2, chip1 = gate(*hop4, kept3, chip2, across2, chip1)
     scaled1 = weigh(aligned, chip1, across1, rows)

time: 88.1 us -> 87.6 us (level)
  waiting for transfers between devices: 32.3 us -> 31.4 us
    ppermute x18, waiting for transfers between devices: 19.7 us -> 18 us  [swap(): return lax.ppermute(value, 'mp', pairs)]
    pallas_call x6 -> x7, Pallas kernels: 13.2 us -> 13.4 us  [project(): pl.pallas_call(functools.partial(project_kernel, wanted, len(parts)), out...]
  transfers between devices with their start and end apart: 26 -> 26, of which waited for: 13 -> 10; matrix products, arithmetic and copies ran while one was open for 5% -> 5% of each run, Pallas kernels for 23% -> 23%
where the time goes in v5:
time: 87.6 us; the launch traced here: 87.2 us
  waiting for transfers between devices  31.4 us (36%)
  Pallas kernels  22.5 us (26%)
  starting transfers between devices  17.8 us (20%)
  local copies, waits for them, and re-layouts  11.7 us (13%)
  other arithmetic  2.08 us (2%)
  matrix products  1.07 us (1%)
    ppermute x18, waiting for transfers between devices, swap(): return lax.ppermute(value, 'mp', pairs)  18 us
    pallas_call x7, Pallas kernels, project(): pl.pallas_call(functools.partial(project_kernel, wanted, len(parts)), out...  13.4 us
    ppermute x8, waiting for transfers between devices, step(): return (lax.ppermute(pair[0], 'dp', UP), lax.ppermute(pair[1], 'dp', DOWN))  13.4 us
    unnamed x20, local copies, waits for them, and re-layouts  10.5 us
    ppermute x8, starting transfers between devices, step(): return (lax.ppermute(pair[0], 'dp', UP), lax.ppermute(pair[1], 'dp', DOWN))  9.16 us
    pallas_call x3, Pallas kernels, contract(): pl.pallas_call(functools.partial(contract_kernel, len(terms), step, tile,...  9 us
    ppermute x18, starting transfers between devices, swap(): return lax.ppermute(value, 'mp', pairs)  8.69 us
  transfers between devices with their start and end apart: 26, of which 10 were waited for; matrix products, arithmetic and copies ran while one was open for 5% of the time, Pallas kernels for 23%

profile of v5, /device:TPU:0, one launch (start us, length us, event | category | flops | bytes accessed | tf_op | source)
XLA Modules:
  0.0 87.2 jit_solution(13843744073731690360)
XLA Ops:
  0.0 2.9 %collective-permute-start.2 = (bf16[128,3072]{1,0:T(8,128)(2,1)}, bf16[128,3072]{1,0:T(8,128)(2,1)S(1)}, u32[]{:S(2)}, u32[]{:S(2)}) collective-permute-start(bf16[128,3072]{1,0:T(8,128)(2,1)} %refs_2_.1), channel_id=1, source_target_pairs={{0,4},{8,0},{16,8},{24,16},{28,24},{20,28},{12,20},{4,12},{1,5},{9... | collective-permute-start | bytes 2359304 | tf_op jit(solution)/shard_map/ppermute | solution.py:229
  3.0 1.1 %constant_dynamic-slice_fusion = (bf16[256,384]{1,0:T(8,128)(2,1)S(1)}, bf16[256,384]{1,0:T(8,128)(2,1)S(1)}) fusion(bf16[256,768]{1,0:T(8,128)(2,1)} %param.10, s32[]{:T(128)S(6)} %select_n.103, s32[]{:T(128)S(6)} %select_n.104), kind=kLoop, calls=%fused_computation.91 | loop fusion | bytes 786440 | tf_op jit(solution)/shard_map/dynamic_slice | solution.py:232
  4.2 2.3 %copy-done = bf16[768,3072]{1,0:T(8,128)(2,1)S(1)} copy-done((bf16[768,3072]{1,0:T(8,128)(2,1)S(1)}, bf16[768,3072]{1,0:T(8,128)(2,1)}, u32[]{:S(2)}) %copy-start) | copy-done | bytes 4718616
  6.5 2.3 %copy-done.2 = bf16[768,3072]{1,0:T(8,128)(2,1)S(1)} copy-done((bf16[768,3072]{1,0:T(8,128)(2,1)S(1)}, bf16[768,3072]{1,0:T(8,128)(2,1)}, u32[]{:S(2)}) %copy-start.2) | copy-done | bytes 4718616
  8.9 1.1 %copy-done.4 = bf16[128,3072]{1,0:T(8,128)(2,1)S(1)} copy-done((bf16[128,3072]{1,0:T(8,128)(2,1)S(1)}, bf16[128,3072]{1,0:T(8,128)(2,1)}, u32[]{:S(2)}) %copy-start.4) | copy-done | bytes 786456
  10.0 2.6 %project.8 = (bf16[768,128]{1,0:T(8,128)(2,1)S(1)}, bf16[768,128]{1,0:T(8,128)(2,1)S(1)}) custom-call(s32[1]{0:T(128)} %bitcast.which_ref, bf16[768,3072]{1,0:T(8,128)(2,1)S(1)} %copy-done.2, bf16[768,3072]{1,0:T(8,128)(2,1)S(1)} %copy-done, bf16[128,3072]{1,0:T(8,128)(2,1)S(1)} %copy-done.4), custom_call_target="tpu_custom_call" | custom-call | flops 362387872 | tf_op jit(solution)/shard_map/project/pallas_call | solution.py:118
  12.6 0.6 collective-permute-start.4
  13.1 0.7 fusion.46
  14.2 6.6 %collective-permute-done.2.refs_1_ = bf16[128,3072]{1,0:T(8,128)(2,1)S(1)} collective-permute-done((bf16[128,3072]{1,0:T(8,128)(2,1)}, bf16[128,3072]{1,0:T(8,128)(2,1)S(1)}, u32[]{:S(2)}, u32[]{:S(2)}) %collective-permute-start.2) | collective-permute-done | bytes 786464 | tf_op jit(solution)/shard_map/ppermute | solution.py:229
  20.8 1.7 %collective-permute-start.3 = (bf16[128,3072]{1,0:T(8,128)(2,1)S(1)}, bf16[128,3072]{1,0:T(8,128)(2,1)S(1)}, u32[]{:S(2)}, u32[]{:S(2)}) collective-permute-start(bf16[128,3072]{1,0:T(8,128)(2,1)S(1)} %collective-permute-done.2.refs_1_), channel_id=1, source_target_pairs={{0,4},{8,0},{16,8},{24,16},{28,24},{20,28},{12,20},{4,12},{1,5},{9... | collective-permute-start | bytes 2359304 | tf_op jit(solution)/shard_map/ppermute | solution.py:229
  22.4 0.4 collective-permute-start.1
  22.9 1.8 %collective-permute-start.7 = (bf16[512,384]{1,0:T(8,128)(2,1)S(1)}, bf16[512,384]{1,0:T(8,128)(2,1)S(1)}, u32[]{:S(2)}, u32[]{:S(2)}) collective-permute-start(bf16[512,384]{1,0:T(8,128)(2,1)S(1)} %pad_maximum_fusion), channel_id=1, source_target_pairs={{0,2},{1,3},{2,0},{3,1},{4,6},{5,7},{6,4},{7,5},{8,10},{9,11},{10,... | collective-permute-start | bytes 1179656 | tf_op jit(solution)/shard_map/ppermute | solution.py:223
  24.6 2.3 %copy-done.1 = bf16[768,3072]{1,0:T(8,128)(2,1)S(1)} copy-done((bf16[768,3072]{1,0:T(8,128)(2,1)S(1)}, bf16[768,3072]{1,0:T(8,128)(2,1)}, u32[]{:S(2)}) %copy-start.1) | copy-done | bytes 4718616
  26.9 2.3 %copy-done.3 = bf16[768,3072]{1,0:T(8,128)(2,1)S(1)} copy-done((bf16[768,3072]{1,0:T(8,128)(2,1)S(1)}, bf16[768,3072]{1,0:T(8,128)(2,1)}, u32[]{:S(2)}) %copy-start.3) | copy-done | bytes 4718616
  29.3 2.6 %project.7 = (bf16[768,256]{1,0:T(8,128)(2,1)S(1)}, bf16[768,256]{1,0:T(8,128)(2,1)S(1)}, bf16[256,3072]{1,0:T(8,128)(2,1)S(1)}) custom-call(s32[1]{0:T(128)} %bitcast.which_ref, bf16[768,3072]{1,0:T(8,128)(2,1)S(1)} %copy-done.3, bf16[768,3072]{1,0:T(8,128)(2,1)S(1)} %copy-done.1, bf16[128,3072]{1,0:T(8,128)(2,1)S(1)} %collective-permute-done.refs_0_, ...), custom_call_target="tpu_custom_call" | custom-call | flops 362387872 | tf_op jit(solution)/shard_map/project/pallas_call | solution.py:118
  32.1 0.4 collective-permute-start.5
  32.5 7.0 %collective-permute-done.5 = bf16[768,128]{1,0:T(8,128)(2,1)S(1)} collective-permute-done((bf16[768,128]{1,0:T(8,128)(2,1)S(1)}, bf16[768,128]{1,0:T(8,128)(2,1)S(1)}, u32[]{:S(2)}, u32[]{:S(2)}) %collective-permute-start.5) | collective-permute-done | bytes 196640 | tf_op jit(solution)/shard_map/ppermute | solution.py:223
  39.5 1.1 %collective-permute-done.1.refs_0_ = bf16[128,3072]{1,0:T(8,128)(2,1)S(1)} collective-permute-done((bf16[128,3072]{1,0:T(8,128)(2,1)S(1)}, bf16[128,3072]{1,0:T(8,128)(2,1)S(1)}, u32[]{:S(2)}, u32[]{:S(2)}) %collective-permute-start.1) | collective-permute-done | bytes 786464 | tf_op jit(solution)/shard_map/ppermute | solution.py:229
  40.6 0.7 collective-permute-start.9
  41.3 1.3 %collective-permute-start.10 = (bf16[128,3072]{1,0:T(8,128)(2,1)S(1)}, bf16[128,3072]{1,0:T(8,128)(2,1)S(1)}, u32[]{:S(2)}, u32[]{:S(2)}) collective-permute-start(bf16[128,3072]{1,0:T(8,128)(2,1)S(1)} %collective-permute-done.3.refs_1_), channel_id=1, source_target_pairs={{0,4},{8,0},{16,8},{24,16},{28,24},{20,28},{12,20},{4,12},{1,5},{9... | collective-permute-start | bytes 2359304 | tf_op jit(solution)/shard_map/ppermute | solution.py:229
  42.6 2.6 %project.9 = (bf16[768,256]{1,0:T(8,128)(2,1)S(1)}, bf16[768,256]{1,0:T(8,128)(2,1)S(1)}, bf16[256,3072]{1,0:T(8,128)(2,1)S(1)}) custom-call(s32[1]{0:T(128)} %bitcast.which_ref, bf16[768,3072]{1,0:T(8,128)(2,1)S(1)} %copy-done.3, bf16[768,3072]{1,0:T(8,128)(2,1)S(1)} %copy-done.1, bf16[128,3072]{1,0:T(8,128)(2,1)S(1)} %collective-permute-done.1.refs_0_, ...), custom_call_target="tpu_custom_call" | custom-call | flops 362387872 | tf_op jit(solution)/shard_map/project/pallas_call | solution.py:118
  45.4 1.6 %collective-permute-start.12 = (bf16[768,256]{1,0:T(8,128)(2,1)S(1)}, bf16[768,256]{1,0:T(8,128)(2,1)S(1)}, u32[]{:S(2)}, u32[]{:S(2)}) collective-permute-start(bf16[768,256]{1,0:T(8,128)(2,1)S(1)} %get-tuple-element.79), channel_id=1, source_target_pairs={{0,2},{1,3},{2,0},{3,1},{4,6},{5,7},{6,4},{7,5},{8,10},{9,11},{10,... | collective-permute-start | bytes 1179656 | tf_op jit(solution)/shard_map/ppermute | solution.py:223
  47.0 1.1 %fusion = f32[384,1024]{1,0:T(8,128)S(1)} fusion(s32[1024]{0:T(1024)S(1)} %fusion.35, bf16[512,384]{1,0:T(8,128)(2,1)S(1)} %collective-permute-done.7, bf16[256,384]{1,0:T(8,128)(2,1)S(1)} %collective-permute-done.6, bf16[256,384]{1,0:T(8,128)(2,1)S(1)} %get-tuple-element.83), kind=kOutput, calls=%fused_computation.1 | convolution fusion | flops 808714240 | bytes 2363392 | tf_op jit(solution)/shard_map/dot_general | solution.py:18
  48.2 0.6 collective-permute-start.16
  48.8 8.6 %collective-permute-done.12 = bf16[768,256]{1,0:T(8,128)(2,1)S(1)} collective-permute-done((bf16[768,256]{1,0:T(8,128)(2,1)S(1)}, bf16[768,256]{1,0:T(8,128)(2,1)S(1)}, u32[]{:S(2)}, u32[]{:S(2)}) %collective-permute-start.12) | collective-permute-done | bytes 393248 | tf_op jit(solution)/shard_map/ppermute | solution.py:223
  57.4 1.3 %collective-permute-done.9.refs_0_ = bf16[128,3072]{1,0:T(8,128)(2,1)S(1)} collective-permute-done((bf16[128,3072]{1,0:T(8,128)(2,1)S(1)}, bf16[128,3072]{1,0:T(8,128)(2,1)S(1)}, u32[]{:S(2)}, u32[]{:S(2)}) %collective-permute-start.9) | collective-permute-done | bytes 786464 | tf_op jit(solution)/shard_map/ppermute | solution.py:229
  58.6 1.3 %collective-permute-done.10.refs_1_ = bf16[128,3072]{1,0:T(8,128)(2,1)S(1)} collective-permute-done((bf16[128,3072]{1,0:T(8,128)(2,1)S(1)}, bf16[128,3072]{1,0:T(8,128)(2,1)S(1)}, u32[]{:S(2)}, u32[]{:S(2)}) %collective-permute-start.10) | collective-permute-done | bytes 786464 | tf_op jit(solution)/shard_map/ppermute | solution.py:229
  60.0 0.5 collective-permute-start.14
  60.5 1.6 %collective-permute-start.13 = (bf16[64,3072]{1,0:T(8,128)(2,1)S(1)}, bf16[64,3072]{1,0:T(8,128)(2,1)S(1)}, u32[]{:S(2)}, u32[]{:S(2)}) collective-permute-start(bf16[64,3072]{1,0:T(8,128)(2,1)S(1)} %slice.71), channel_id=1, source_target_pairs={{0,8},{8,16},{16,24},{24,28},{28,20},{20,12},{12,4},{4,0},{1,9},{9... | collective-permute-start | bytes 1179656 | tf_op jit(solution)/shard_map/ppermute | solution.py:229
  62.1 1.4 %project.10 = (bf16[384,256]{1,0:T(8,128)(2,1)S(1)}, bf16[384,256]{1,0:T(8,128)(2,1)S(1)}, bf16[256,3072]{1,0:T(8,128)(2,1)S(1)}) custom-call(s32[1]{0:T(128)} %bitcast.which_ref, bf16[768,3072]{1,0:T(8,128)(2,1)S(1)} %copy-done.3, bf16[768,3072]{1,0:T(8,128)(2,1)S(1)} %copy-done.1, bf16[128,3072]{1,0:T(8,128)(2,1)S(1)} %collective-permute-done.9.refs_0_, ...), custom_call_target="tpu_custom_call" | custom-call | flops 181193936 | tf_op jit(solution)/shard_map/project/pallas_call | solution.py:118
  63.6 0.5 collective-permute-start.21
  64.2 1.4 %project.11.kept_ref = bf16[768,256]{1,0:T(8,128)(2,1)S(1)} custom-call(s32[1]{0:T(128)} %bitcast.which_ref, bf16[768,3072]{1,0:T(8,128)(2,1)S(1)} %copy-done.3, bf16[768,3072]{1,0:T(8,128)(2,1)S(1)} %copy-done.1, bf16[256,3072]{1,0:T(8,128)(2,1)S(1)} %get-tuple-element.52.refs_0_.refs_1_), custom_call_target="tpu_custom_call" | custom-call | flops 181193936 | tf_op jit(solution)/shard_map/project/pallas_call | solution.py:118
  65.6 0.2 collective-permute-start.8
  65.8 0.1 merge.1
  65.9 0.6 collective-permute-start.22
  66.5 2.9 %collective-permute-done.14.refs_1_ = bf16[64,3072]{1,0:T(8,128)(2,1)S(1)} collective-permute-done((bf16[64,3072]{1,0:T(8,128)(2,1)S(1)}, bf16[64,3072]{1,0:T(8,128)(2,1)S(1)}, u32[]{:S(2)}, u32[]{:S(2)}) %collective-permute-start.14) | collective-permute-done | bytes 393248 | tf_op jit(solution)/shard_map/ppermute | solution.py:229
  69.4 0.2 collective-permute-done.13.refs_0_
  69.7 1.4 %project.12 = (bf16[768,128]{1,0:T(8,128)(2,1)S(1)}, bf16[128,3072]{1,0:T(8,128)(2,1)S(1)}) custom-call(s32[1]{0:T(128)} %bitcast.which_ref, bf16[768,3072]{1,0:T(8,128)(2,1)S(1)} %copy-done.3, bf16[768,3072]{1,0:T(8,128)(2,1)S(1)} %copy-done.1, bf16[64,3072]{1,0:T(8,128)(2,1)S(1)} %collective-permute-done.13.refs_0_, ...), custom_call_target="tpu_custom_call" | custom-call | flops 181193936 | tf_op jit(solution)/shard_map/project/pallas_call | solution.py:118
  71.3 0.2 fusion.12
  71.5 0.6 collective-permute-start.18
  72.2 1.4 %project.13 = bf16[768,128]{1,0:T(8,128)(2,1)S(1)} custom-call(s32[1]{0:T(128)} %bitcast.which_ref, bf16[768,3072]{1,0:T(8,128)(2,1)S(1)} %copy-done.3, bf16[768,3072]{1,0:T(8,128)(2,1)S(1)} %copy-done.1, bf16[128,3072]{1,0:T(8,128)(2,1)S(1)} %get-tuple-element.63.refs_0_.refs_3_), custom_call_target="tpu_custom_call" | custom-call | flops 181193936 | tf_op jit(solution)/shard_map/project/pallas_call | solution.py:118
  73.6 1.1 %collective-permute-start.24 = (bf16[768,128]{1,0:T(8,128)(2,1)S(1)}, bf16[768,128]{1,0:T(8,128)(2,1)S(1)}, u32[]{:S(2)}, u32[]{:S(2)}) collective-permute-start(bf16[768,128]{1,0:T(8,128)(2,1)S(1)} %get-tuple-element.81), channel_id=1, source_target_pairs={{0,2},{1,3},{2,0},{3,1},{4,6},{5,7},{6,4},{7,5},{8,10},{9,11},{10,... | collective-permute-start | bytes 589832 | tf_op jit(solution)/shard_map/ppermute | solution.py:223
  74.7 3.8 %contract.3.base_ref = f32[768,3072]{1,0:T(8,128)S(1)} custom-call(s32[1]{0:T(128)} %bitcast.which_ref, bf16[768,3072]{1,0:T(8,128)(2,1)S(1)} %bitcast.12, bf16[384,128]{1,0:T(8,128)(2,1)S(1)} %fusion.27.refs_0_, bf16[384,128]{1,0:T(8,128)(2,1)S(1)} %collective-permute-done.8.refs_1_, bf16[128,3072]{1,0:T(8,128)(2,1)S(1)} %copy-done.5, ...), custom_call_target="tpu_custom_call" | custom-call | flops 452984832 | tf_op jit(solution)/shard_map/contract/pallas_call | solution.py:201
  78.7 0.1 fusion.7.refs_0_
  78.8 0.5 collective-permute-start.23
  79.3 2.4 %collective-permute-done.24 = bf16[768,128]{1,0:T(8,128)(2,1)S(1)} collective-permute-done((bf16[768,128]{1,0:T(8,128)(2,1)S(1)}, bf16[768,128]{1,0:T(8,128)(2,1)S(1)}, u32[]{:S(2)}, u32[]{:S(2)}) %collective-permute-start.24) | collective-permute-done | bytes 196640 | tf_op jit(solution)/shard_map/ppermute | solution.py:223
  81.8 2.6 %contract.4.refs_4_ = f32[768,3072]{1,0:T(8,128)} custom-call(s32[1]{0:T(128)} %bitcast.which_ref, f32[768,3072]{1,0:T(8,128)S(1)} %contract.3.base_ref, bf16[384,256]{1,0:T(8,128)(2,1)S(1)} %fusion.7.refs_0_, bf16[256,3072]{1,0:T(8,128)(2,1)S(1)} %get-tuple-element.52.refs_0_.refs_1_, bf16[384,128]{1,0:T(8,128)(2,1)S(1)} %fusion.22.refs_2_, ...), custom_call_target="tpu_custom_call" | custom-call | flops 271790912 | tf_op jit(solution)/shard_map/contract/pallas_call | solution.py:201
  84.4 2.6 %contract.5 = f32[768,3072]{1,0:T(8,128)} custom-call(s32[1]{0:T(128)} %bitcast.which_ref, f32[768,3072]{1,0:T(8,128)S(1)} %contract.3.base_ref, bf16[384,256]{1,0:T(8,128)(2,1)S(1)} %collective-permute-done.23.refs_0_, bf16[256,3072]{1,0:T(8,128)(2,1)S(1)} %get-tuple-element.52.refs_0_.refs_1_, ...), custom_call_target="tpu_custom_call", output_to_operand_aliasing={{}: (6, {})} | custom-call | flops 271790912 | tf_op jit(solution)/shard_map/contract/pallas_call | solution.py:201
  (63 shorter events, 1.9 us)
Async XLA Ops:
  0.0 20.8 %collective-permute-start.2 = (bf16[128,3072]{1,0:T(8,128)(2,1)}, bf16[128,3072]{1,0:T(8,128)(2,1)S(1)}, u32[]{:S(2)}, u32[]{:S(2)}) collective-permute-start(bf16[128,3072]{1,0:T(8,128)(2,1)} %refs_2_.1), channel_id=1, source_target_pairs={{0,4},{8,0},{16,8},{24,16},{28,24},{20,28},{12,20},{4,12},{1,5},{9... | collective-permute-start | bytes 2359304 | tf_op jit(solution)/shard_map/ppermute | solution.py:229
  2.9 19.5 %collective-permute-start = (bf16[128,3072]{1,0:T(8,128)(2,1)}, bf16[128,3072]{1,0:T(8,128)(2,1)S(1)}, u32[]{:S(2)}, u32[]{:S(2)}) collective-permute-start(bf16[128,3072]{1,0:T(8,128)(2,1)} %refs_2_.1), channel_id=1, source_target_pairs={{0,8},{8,16},{16,24},{24,28},{28,20},{20,12},{12,4},{4,0},{1,9},{9... | collective-permute-start | bytes 2359304 | tf_op jit(solution)/shard_map/ppermute | solution.py:229
  4.1 18.7 %collective-permute-start.6 = (bf16[256,384]{1,0:T(8,128)(2,1)S(1)}, bf16[256,384]{1,0:T(8,128)(2,1)S(1)}, u32[]{:S(2)}, u32[]{:S(2)}) collective-permute-start(bf16[256,384]{1,0:T(8,128)(2,1)S(1)} %get-tuple-element.84), channel_id=1, source_target_pairs={{0,1},{1,0},{2,3},{3,2},{4,5},{5,4},{6,7},{7,6},{8,9},{9,8},{10,11... | collective-permute-start | bytes 589832 | tf_op jit(solution)/shard_map/ppermute | solution.py:223
  4.2 2.3 %copy-start = (bf16[768,3072]{1,0:T(8,128)(2,1)S(1)}, bf16[768,3072]{1,0:T(8,128)(2,1)}, u32[]{:S(2)}) copy-start(bf16[768,3072]{1,0:T(8,128)(2,1)} %base_ref.1) | copy-start | bytes 14155780
  6.5 2.3 %copy-start.2 = (bf16[768,3072]{1,0:T(8,128)(2,1)S(1)}, bf16[768,3072]{1,0:T(8,128)(2,1)}, u32[]{:S(2)}) copy-start(bf16[768,3072]{1,0:T(8,128)(2,1)} %w_ref.13) | copy-start | bytes 14155780
  8.8 1.1 %copy-start.4 = (bf16[128,3072]{1,0:T(8,128)(2,1)S(1)}, bf16[128,3072]{1,0:T(8,128)(2,1)}, u32[]{:S(2)}) copy-start(bf16[128,3072]{1,0:T(8,128)(2,1)} %refs_2_.1) | copy-start | bytes 2359300
  10.0 4.0 %copy-start.6 = (s32[4]{0:T(128)S(1)}, s32[4]{0:T(128)}, u32[]{:S(2)}) copy-start(s32[4]{0:T(128)} %param.11) | copy-start | bytes 52
  10.0 4.1 %copy-start.7 = (f32[4]{0:T(128)S(1)}, f32[4]{0:T(128)}, u32[]{:S(2)}) copy-start(f32[4]{0:T(128)} %param.12) | copy-start | bytes 52
  12.6 19.4 %collective-permute-start.4 = (bf16[768,128]{1,0:T(8,128)(2,1)S(1)}, bf16[768,128]{1,0:T(8,128)(2,1)S(1)}, u32[]{:S(2)}, u32[]{:S(2)}) collective-permute-start(bf16[768,128]{1,0:T(8,128)(2,1)S(1)} %get-tuple-element.42), channel_id=1, source_target_pairs={{0,1},{1,0},{2,3},{3,2},{4,5},{5,4},{6,7},{7,6},{8,9},{9,8},{10,11... | collective-permute-start | bytes 589832 | tf_op jit(solution)/shard_map/ppermute | solution.py:223
  20.8 18.7 %collective-permute-start.3 = (bf16[128,3072]{1,0:T(8,128)(2,1)S(1)}, bf16[128,3072]{1,0:T(8,128)(2,1)S(1)}, u32[]{:S(2)}, u32[]{:S(2)}) collective-permute-start(bf16[128,3072]{1,0:T(8,128)(2,1)S(1)} %collective-permute-done.2.refs_1_), channel_id=1, source_target_pairs={{0,4},{8,0},{16,8},{24,16},{28,24},{20,28},{12,20},{4,12},{1,5},{9... | collective-permute-start | bytes 2359304 | tf_op jit(solution)/shard_map/ppermute | solution.py:229
  22.4 18.1 %collective-permute-start.1 = (bf16[128,3072]{1,0:T(8,128)(2,1)S(1)}, bf16[128,3072]{1,0:T(8,128)(2,1)S(1)}, u32[]{:S(2)}, u32[]{:S(2)}) collective-permute-start(bf16[128,3072]{1,0:T(8,128)(2,1)S(1)} %collective-permute-done.refs_0_), channel_id=1, source_target_pairs={{0,8},{8,16},{16,24},{24,28},{28,20},{20,12},{12,4},{4,0},{1,9},{9... | collective-permute-start | bytes 2359304 | tf_op jit(solution)/shard_map/ppermute | solution.py:229
  22.9 16.6 %collective-permute-start.7 = (bf16[512,384]{1,0:T(8,128)(2,1)S(1)}, bf16[512,384]{1,0:T(8,128)(2,1)S(1)}, u32[]{:S(2)}, u32[]{:S(2)}) collective-permute-start(bf16[512,384]{1,0:T(8,128)(2,1)S(1)} %pad_maximum_fusion), channel_id=1, source_target_pairs={{0,2},{1,3},{2,0},{3,1},{4,6},{5,7},{6,4},{7,5},{8,10},{9,11},{10,... | collective-permute-start | bytes 1179656 | tf_op jit(solution)/shard_map/ppermute | solution.py:223
  24.6 2.3 %copy-start.1 = (bf16[768,3072]{1,0:T(8,128)(2,1)S(1)}, bf16[768,3072]{1,0:T(8,128)(2,1)}, u32[]{:S(2)}) copy-start(bf16[768,3072]{1,0:T(8,128)(2,1)} %base_ref.1) | copy-start | bytes 14155780
  26.9 2.3 %copy-start.3 = (bf16[768,3072]{1,0:T(8,128)(2,1)S(1)}, bf16[768,3072]{1,0:T(8,128)(2,1)}, u32[]{:S(2)}) copy-start(bf16[768,3072]{1,0:T(8,128)(2,1)} %w_ref.13) | copy-start | bytes 14155780
  31.9 13.4 %collective-permute-start.11 = (bf16[768,256]{1,0:T(8,128)(2,1)S(1)}, bf16[768,256]{1,0:T(8,128)(2,1)S(1)}, u32[]{:S(2)}, u32[]{:S(2)}) collective-permute-start(bf16[768,256]{1,0:T(8,128)(2,1)S(1)} %get-tuple-element.49), channel_id=1, source_target_pairs={{0,1},{1,0},{2,3},{3,2},{4,5},{5,4},{6,7},{7,6},{8,9},{9,8},{10,11... | collective-permute-start | bytes 1179656 | tf_op jit(solution)/shard_map/ppermute | solution.py:223
  32.1 7.4 %collective-permute-start.5 = (bf16[768,128]{1,0:T(8,128)(2,1)S(1)}, bf16[768,128]{1,0:T(8,128)(2,1)S(1)}, u32[]{:S(2)}, u32[]{:S(2)}) collective-permute-start(bf16[768,128]{1,0:T(8,128)(2,1)S(1)} %get-tuple-element.85), channel_id=1, source_target_pairs={{0,2},{1,3},{2,0},{3,1},{4,6},{5,7},{6,4},{7,5},{8,10},{9,11},{10,... | collective-permute-start | bytes 589832 | tf_op jit(solution)/shard_map/ppermute | solution.py:223
  40.6 18.1 %collective-permute-start.9 = (bf16[128,3072]{1,0:T(8,128)(2,1)S(1)}, bf16[128,3072]{1,0:T(8,128)(2,1)S(1)}, u32[]{:S(2)}, u32[]{:S(2)}) collective-permute-start(bf16[128,3072]{1,0:T(8,128)(2,1)S(1)} %collective-permute-done.1.refs_0_), channel_id=1, source_target_pairs={{0,8},{8,16},{16,24},{24,28},{28,20},{20,12},{12,4},{4,0},{1,9},{9... | collective-permute-start | bytes 2359304 | tf_op jit(solution)/shard_map/ppermute | solution.py:229
  41.3 18.7 %collective-permute-start.10 = (bf16[128,3072]{1,0:T(8,128)(2,1)S(1)}, bf16[128,3072]{1,0:T(8,128)(2,1)S(1)}, u32[]{:S(2)}, u32[]{:S(2)}) collective-permute-start(bf16[128,3072]{1,0:T(8,128)(2,1)S(1)} %collective-permute-done.3.refs_1_), channel_id=1, source_target_pairs={{0,4},{8,0},{16,8},{24,16},{28,24},{20,28},{12,20},{4,12},{1,5},{9... | collective-permute-start | bytes 2359304 | tf_op jit(solution)/shard_map/ppermute | solution.py:229
  45.2 2.9 %collective-permute-start.15 = (bf16[768,256]{1,0:T(8,128)(2,1)S(1)}, bf16[768,256]{1,0:T(8,128)(2,1)S(1)}, u32[]{:S(2)}, u32[]{:S(2)}) collective-permute-start(bf16[768,256]{1,0:T(8,128)(2,1)S(1)} %get-tuple-element.53), channel_id=1, source_target_pairs={{0,1},{1,0},{2,3},{3,2},{4,5},{5,4},{6,7},{7,6},{8,9},{9,8},{10,11... | collective-permute-start | bytes 1179656 | tf_op jit(solution)/shard_map/ppermute | solution.py:223
  45.4 12.0 %collective-permute-start.12 = (bf16[768,256]{1,0:T(8,128)(2,1)S(1)}, bf16[768,256]{1,0:T(8,128)(2,1)S(1)}, u32[]{:S(2)}, u32[]{:S(2)}) collective-permute-start(bf16[768,256]{1,0:T(8,128)(2,1)S(1)} %get-tuple-element.79), channel_id=1, source_target_pairs={{0,2},{1,3},{2,0},{3,1},{4,6},{5,7},{6,4},{7,5},{8,10},{9,11},{10,... | collective-permute-start | bytes 1179656 | tf_op jit(solution)/shard_map/ppermute | solution.py:223
  48.2 18.3 %collective-permute-start.16 = (bf16[768,256]{1,0:T(8,128)(2,1)S(1)}, bf16[768,256]{1,0:T(8,128)(2,1)S(1)}, u32[]{:S(2)}, u32[]{:S(2)}) collective-permute-start(bf16[768,256]{1,0:T(8,128)(2,1)S(1)} %get-tuple-element.77), channel_id=1, source_target_pairs={{0,2},{1,3},{2,0},{3,1},{4,6},{5,7},{6,4},{7,5},{8,10},{9,11},{10,... | collective-permute-start | bytes 1179656 | tf_op jit(solution)/shard_map/ppermute | solution.py:223
  60.0 9.4 %collective-permute-start.14 = (bf16[64,3072]{1,0:T(8,128)(2,1)S(1)}, bf16[64,3072]{1,0:T(8,128)(2,1)S(1)}, u32[]{:S(2)}, u32[]{:S(2)}) collective-permute-start(bf16[64,3072]{1,0:T(8,128)(2,1)S(1)} %slice.72), channel_id=1, source_target_pairs={{0,4},{8,0},{16,8},{24,16},{28,24},{20,28},{12,20},{4,12},{1,5},{9... | collective-permute-start | bytes 1179656 | tf_op jit(solution)/shard_map/ppermute | solution.py:229
  60.5 9.1 %collective-permute-start.13 = (bf16[64,3072]{1,0:T(8,128)(2,1)S(1)}, bf16[64,3072]{1,0:T(8,128)(2,1)S(1)}, u32[]{:S(2)}, u32[]{:S(2)}) collective-permute-start(bf16[64,3072]{1,0:T(8,128)(2,1)S(1)} %slice.71), channel_id=1, source_target_pairs={{0,8},{8,16},{16,24},{24,28},{28,20},{20,12},{12,4},{4,0},{1,9},{9... | collective-permute-start | bytes 1179656 | tf_op jit(solution)/shard_map/ppermute | solution.py:229
  63.5 2.1 %collective-permute-start.20 = (bf16[384,256]{1,0:T(8,128)(2,1)S(1)}, bf16[384,256]{1,0:T(8,128)(2,1)S(1)}, u32[]{:S(2)}, u32[]{:S(2)}) collective-permute-start(bf16[384,256]{1,0:T(8,128)(2,1)S(1)} %get-tuple-element.66), channel_id=1, source_target_pairs={{0,1},{1,0},{2,3},{3,2},{4,5},{5,4},{6,7},{7,6},{8,9},{9,8},{10,11... | collective-permute-start | bytes 589832 | tf_op jit(solution)/shard_map/ppermute | solution.py:223
  63.6 2.1 %collective-permute-start.21 = (bf16[384,256]{1,0:T(8,128)(2,1)S(1)}, bf16[384,256]{1,0:T(8,128)(2,1)S(1)}, u32[]{:S(2)}, u32[]{:S(2)}) collective-permute-start(bf16[384,256]{1,0:T(8,128)(2,1)S(1)} %get-tuple-element.67), channel_id=1, source_target_pairs={{0,1},{1,0},{2,3},{3,2},{4,5},{5,4},{6,7},{7,6},{8,9},{9,8},{10,11... | collective-permute-start | bytes 589832 | tf_op jit(solution)/shard_map/ppermute | solution.py:223
  65.6 9.1 %collective-permute-start.8 = (bf16[384,128]{1,0:T(8,128)(2,1)S(1)}, bf16[384,128]{1,0:T(8,128)(2,1)S(1)}, u32[]{:S(2)}, u32[]{:S(2)}) collective-permute-start(bf16[384,128]{1,0:T(8,128)(2,1)S(1)} %fusion.27.refs_0_), channel_id=1, source_target_pairs={{0,1},{1,0},{2,3},{3,2},{4,5},{5,4},{6,7},{7,6},{8,9},{9,8},{10,11... | collective-permute-start | bytes 294920 | tf_op jit(solution)/shard_map/ppermute | solution.py:223
  65.9 12.7 %collective-permute-start.22 = (bf16[768,256]{1,0:T(8,128)(2,1)S(1)}, bf16[768,256]{1,0:T(8,128)(2,1)S(1)}, u32[]{:S(2)}, u32[]{:S(2)}) collective-permute-start(bf16[768,256]{1,0:T(8,128)(2,1)S(1)} %get-tuple-element.71), channel_id=1, source_target_pairs={{0,2},{1,3},{2,0},{3,1},{4,6},{5,7},{6,4},{7,5},{8,10},{9,11},{10,... | collective-permute-start | bytes 1179656 | tf_op jit(solution)/shard_map/ppermute | solution.py:223
  71.0 2.5 %collective-permute-start.19 = (bf16[768,128]{1,0:T(8,128)(2,1)S(1)}, bf16[768,128]{1,0:T(8,128)(2,1)S(1)}, u32[]{:S(2)}, u32[]{:S(2)}) collective-permute-start(bf16[768,128]{1,0:T(8,128)(2,1)S(1)} %get-tuple-element.64), channel_id=1, source_target_pairs={{0,1},{1,0},{2,3},{3,2},{4,5},{5,4},{6,7},{7,6},{8,9},{9,8},{10,11... | collective-permute-start | bytes 589832 | tf_op jit(solution)/shard_map/ppermute | solution.py:223
  71.5 3.2 %collective-permute-start.18 = (bf16[384,256]{1,0:T(8,128)(2,1)S(1)}, bf16[384,256]{1,0:T(8,128)(2,1)S(1)}, u32[]{:S(2)}, u32[]{:S(2)}) collective-permute-start(bf16[384,256]{1,0:T(8,128)(2,1)S(1)} %get-tuple-element.75.refs_6_), channel_id=1, source_target_pairs={{0,1},{1,0},{2,3},{3,2},{4,5},{5,4},{6,7},{7,6},{8,9},{9,8},{10,11... | collective-permute-start | bytes 589832 | tf_op jit(solution)/shard_map/ppermute | solution.py:223
  72.1 2.6 %collective-permute-start.17 = (bf16[384,256]{1,0:T(8,128)(2,1)S(1)}, bf16[384,256]{1,0:T(8,128)(2,1)S(1)}, u32[]{:S(2)}, u32[]{:S(2)}) collective-permute-start(bf16[384,256]{1,0:T(8,128)(2,1)S(1)} %get-tuple-element.76.refs_3_), channel_id=1, source_target_pairs={{0,1},{1,0},{2,3},{3,2},{4,5},{5,4},{6,7},{7,6},{8,9},{9,8},{10,11... | collective-permute-start | bytes 589832 | tf_op jit(solution)/shard_map/ppermute | solution.py:223
  72.2 2.5 %slice-start = ((s8[4718592]{0:T(1024)(128)(4,1)}), s8[4194304]{0:T(1024)(128)(4,1)S(1)}, s32[]{:S(2)}) async-start(s8[4718592]{0:T(1024)(128)(4,1)} %bitcast.11), calls=%async_computation | async-start | bytes 8388608
  72.2 2.5 %slice-start.1 = ((s8[4718592]{0:T(1024)(128)(4,1)}), s8[524288]{0:T(1024)(128)(4,1)S(1)}, s32[]{:S(2)}) async-start(s8[4718592]{0:T(1024)(128)(4,1)} %bitcast.11), calls=%async_computation.1 | async-start | bytes 1048576
  72.2 2.6 %copy-start.5 = (bf16[128,3072]{1,0:T(8,128)(2,1)S(1)}, bf16[128,3072]{1,0:T(8,128)(2,1)}, u32[]{:S(2)}) copy-start(bf16[128,3072]{1,0:T(8,128)(2,1)} %refs_2_.1) | copy-start | bytes 2359300
  73.6 8.0 %collective-permute-start.24 = (bf16[768,128]{1,0:T(8,128)(2,1)S(1)}, bf16[768,128]{1,0:T(8,128)(2,1)S(1)}, u32[]{:S(2)}, u32[]{:S(2)}) collective-permute-start(bf16[768,128]{1,0:T(8,128)(2,1)S(1)} %get-tuple-element.81), channel_id=1, source_target_pairs={{0,2},{1,3},{2,0},{3,1},{4,6},{5,7},{6,4},{7,5},{8,10},{9,11},{10,... | collective-permute-start | bytes 589832 | tf_op jit(solution)/shard_map/ppermute | solution.py:223
  78.8 5.6 %collective-permute-start.23 = (bf16[384,256]{1,0:T(8,128)(2,1)S(1)}, bf16[384,256]{1,0:T(8,128)(2,1)S(1)}, u32[]{:S(2)}, u32[]{:S(2)}) collective-permute-start(bf16[384,256]{1,0:T(8,128)(2,1)S(1)} %fusion.7.refs_0_), channel_id=1, source_target_pairs={{0,1},{1,0},{2,3},{3,2},{4,5},{5,4},{6,7},{7,6},{8,9},{9,8},{10,11... | collective-permute-start | bytes 589832 | tf_op jit(solution)/shard_map/ppermute | solution.py:223
  81.7 2.7 %collective-permute-start.25 = (bf16[384,128]{1,0:T(8,128)(2,1)S(1)}, bf16[384,128]{1,0:T(8,128)(2,1)S(1)}, u32[]{:S(2)}, u32[]{:S(2)}) collective-permute-start(bf16[384,128]{1,0:T(8,128)(2,1)S(1)} %fusion.22.refs_2_), channel_id=1, source_target_pairs={{0,1},{1,0},{2,3},{3,2},{4,5},{5,4},{6,7},{7,6},{8,9},{9,8},{10,11... | collective-permute-start | bytes 294920 | tf_op jit(solution)/shard_map/ppermute | solution.py:223

commit v6 on v5

--- a/solution.py
+++ b/solution.py
@@ -204,7 +204,7 @@
         in_specs=[pl.BlockSpec(memory_space=pltpu.SMEM)] + [IN_VMEM] * (1 + len(operands)) + [pl.BlockSpec(memory_space=pl.ANY)] * len(held),
         out_specs=pl.BlockSpec(memory_space=pl.ANY) if last else IN_VMEM,
         scratch_shapes=[pltpu.VMEM((tiles, width // 2, tile), jnp.float32), pltpu.SemaphoreType.DMA((tiles,))] if last else [],
-        input_output_aliases={2 + len(operands): 0} if held else {},
+        input_output_aliases={2 + len(operands): 0} if held else {1: 0} if not last and len(flips) == 1 else {},
         compiler_params=pltpu.CompilerParams(vmem_limit_bytes=20 * 2**20),
         cost_estimate=cost(2 * width * depth * sum(term[-1].shape[0] for term in terms)),
         name="contract",
@@ -303,9 +303,10 @@
     total = contract(one, direction, [(*scaled0, hidden), (*scaled1, block1), (*scaled2, block2)], share)
     total, chip3 = gate(total, chip3)
     scaled3 = weigh(aligned, chip3, across3, 5 * rows)
-    mine3, chip4 = gate(scaled3[0], chip4)
+    total = contract(one, total, [(scaled3[0], block3)], share, (0,))
+    total, chip4 = gate(total, chip4)
     scaled4 = weigh(aligned, chip4, across4, 7 * rows)
-    result = contract(one, total, [(mine3, block3), (scaled4[0], block4)], share, (0,), True)
+    result = contract(one, total, [(scaled4[0], block4)], share, (0,), True)
     terms = [(scaled3[1], block3), (scaled4[1], block4)]
     return contract(one, total, terms, share, (1,), True, result)
 

time: 87.6 us -> 87.4 us (level)
  waiting for transfers between devices: 31.4 us -> 30.3 us
  Pallas kernels: 22.5 us -> 23.5 us
    ppermute x18, waiting for transfers between devices: 18 us -> 16.9 us  [swap(): return lax.ppermute(value, 'mp', pairs)]
    pallas_call x3 -> x4, Pallas kernels: 9 us -> 9.98 us  [contract(): pl.pallas_call(functools.partial(contract_kernel, len(terms), step, tile,...]
  transfers between devices with their start and end apart: 26 -> 26, of which waited for: 10 -> 10; matrix products, arithmetic and copies ran while one was open for 5% -> 5% of each run, Pallas kernels for 23% -> 24%
where the time goes in v6:
time: 87.4 us; the launch traced here: 87.1 us
  waiting for transfers between devices  30.3 us (35%)
  Pallas kernels  23.5 us (27%)
  starting transfers between devices  17.8 us (20%)
  local copies, waits for them, and re-layouts  11.7 us (13%)
  other arithmetic  2.08 us (2%)
  matrix products  1.07 us (1%)
    ppermute x18, waiting for transfers between devices, swap(): return lax.ppermute(value, 'mp', pairs)  16.9 us
    pallas_call x7, Pallas kernels, project(): pl.pallas_call(functools.partial(project_kernel, wanted, len(parts)), out...  13.4 us
    ppermute x8, waiting for transfers between devices, step(): return (lax.ppermute(pair[0], 'dp', UP), lax.ppermute(pair[1], 'dp', DOWN))  13.4 us
    unnamed x20, local copies, waits for them, and re-layouts  10.5 us
    pallas_call x4, Pallas kernels, contract(): pl.pallas_call(functools.partial(contract_kernel, len(terms), step, tile,...  9.98 us
    ppermute x8, starting transfers between devices, step(): return (lax.ppermute(pair[0], 'dp', UP), lax.ppermute(pair[1], 'dp', DOWN))  9.16 us
    ppermute x18, starting transfers between devices, swap(): return lax.ppermute(value, 'mp', pairs)  8.69 us
  transfers between devices with their start and end apart: 26, of which 10 were waited for; matrix products, arithmetic and copies ran while one was open for 5% of the time, Pallas kernels for 24%

profile of v6, /device:TPU:0, one launch (start us, length us, event | category | flops | bytes accessed | tf_op | source)
XLA Modules:
  0.0 87.1 jit_solution(12551712887697711206)
XLA Ops:
  0.0 2.9 %collective-permute-start.2 = (bf16[128,3072]{1,0:T(8,128)(2,1)}, bf16[128,3072]{1,0:T(8,128)(2,1)S(1)}, u32[]{:S(2)}, u32[]{:S(2)}) collective-permute-start(bf16[128,3072]{1,0:T(8,128)(2,1)} %refs_2_.1), channel_id=1, source_target_pairs={{0,4},{8,0},{16,8},{24,16},{28,24},{20,28},{12,20},{4,12},{1,5},{9... | collective-permute-start | bytes 2359304 | tf_op jit(solution)/shard_map/ppermute | solution.py:229
  3.0 1.1 %constant_dynamic-slice_fusion = (bf16[256,384]{1,0:T(8,128)(2,1)S(1)}, bf16[256,384]{1,0:T(8,128)(2,1)S(1)}) fusion(bf16[256,768]{1,0:T(8,128)(2,1)} %param.10, s32[]{:T(128)S(6)} %select_n.103, s32[]{:T(128)S(6)} %select_n.104), kind=kLoop, calls=%fused_computation.91 | loop fusion | bytes 786440 | tf_op jit(solution)/shard_map/dynamic_slice | solution.py:232
  4.2 2.3 %copy-done = bf16[768,3072]{1,0:T(8,128)(2,1)S(1)} copy-done((bf16[768,3072]{1,0:T(8,128)(2,1)S(1)}, bf16[768,3072]{1,0:T(8,128)(2,1)}, u32[]{:S(2)}) %copy-start) | copy-done | bytes 4718616
  6.5 2.3 %copy-done.2 = bf16[768,3072]{1,0:T(8,128)(2,1)S(1)} copy-done((bf16[768,3072]{1,0:T(8,128)(2,1)S(1)}, bf16[768,3072]{1,0:T(8,128)(2,1)}, u32[]{:S(2)}) %copy-start.2) | copy-done | bytes 4718616
  8.9 1.1 %copy-done.4 = bf16[128,3072]{1,0:T(8,128)(2,1)S(1)} copy-done((bf16[128,3072]{1,0:T(8,128)(2,1)S(1)}, bf16[128,3072]{1,0:T(8,128)(2,1)}, u32[]{:S(2)}) %copy-start.4) | copy-done | bytes 786456
  10.0 2.6 %project.8 = (bf16[768,128]{1,0:T(8,128)(2,1)S(1)}, bf16[768,128]{1,0:T(8,128)(2,1)S(1)}) custom-call(s32[1]{0:T(128)} %bitcast.which_ref, bf16[768,3072]{1,0:T(8,128)(2,1)S(1)} %copy-done.2, bf16[768,3072]{1,0:T(8,128)(2,1)S(1)} %copy-done, bf16[128,3072]{1,0:T(8,128)(2,1)S(1)} %copy-done.4), custom_call_target="tpu_custom_call" | custom-call | flops 362387872 | tf_op jit(solution)/shard_map/project/pallas_call | solution.py:118
  12.6 0.6 collective-permute-start.4
  13.1 0.7 fusion.46
  14.2 6.6 %collective-permute-done.2.refs_1_ = bf16[128,3072]{1,0:T(8,128)(2,1)S(1)} collective-permute-done((bf16[128,3072]{1,0:T(8,128)(2,1)}, bf16[128,3072]{1,0:T(8,128)(2,1)S(1)}, u32[]{:S(2)}, u32[]{:S(2)}) %collective-permute-start.2) | collective-permute-done | bytes 786464 | tf_op jit(solution)/shard_map/ppermute | solution.py:229
  20.8 1.7 %collective-permute-start.3 = (bf16[128,3072]{1,0:T(8,128)(2,1)S(1)}, bf16[128,3072]{1,0:T(8,128)(2,1)S(1)}, u32[]{:S(2)}, u32[]{:S(2)}) collective-permute-start(bf16[128,3072]{1,0:T(8,128)(2,1)S(1)} %collective-permute-done.2.refs_1_), channel_id=1, source_target_pairs={{0,4},{8,0},{16,8},{24,16},{28,24},{20,28},{12,20},{4,12},{1,5},{9... | collective-permute-start | bytes 2359304 | tf_op jit(solution)/shard_map/ppermute | solution.py:229
  22.4 0.4 collective-permute-start.1
  22.9 1.8 %collective-permute-start.7 = (bf16[512,384]{1,0:T(8,128)(2,1)S(1)}, bf16[512,384]{1,0:T(8,128)(2,1)S(1)}, u32[]{:S(2)}, u32[]{:S(2)}) collective-permute-start(bf16[512,384]{1,0:T(8,128)(2,1)S(1)} %pad_maximum_fusion), channel_id=1, source_target_pairs={{0,2},{1,3},{2,0},{3,1},{4,6},{5,7},{6,4},{7,5},{8,10},{9,11},{10,... | collective-permute-start | bytes 1179656 | tf_op jit(solution)/shard_map/ppermute | solution.py:223
  24.6 2.3 %copy-done.1 = bf16[768,3072]{1,0:T(8,128)(2,1)S(1)} copy-done((bf16[768,3072]{1,0:T(8,128)(2,1)S(1)}, bf16[768,3072]{1,0:T(8,128)(2,1)}, u32[]{:S(2)}) %copy-start.1) | copy-done | bytes 4718616
  26.9 2.3 %copy-done.3 = bf16[768,3072]{1,0:T(8,128)(2,1)S(1)} copy-done((bf16[768,3072]{1,0:T(8,128)(2,1)S(1)}, bf16[768,3072]{1,0:T(8,128)(2,1)}, u32[]{:S(2)}) %copy-start.3) | copy-done | bytes 4718616
  29.3 2.6 %project.7 = (bf16[768,256]{1,0:T(8,128)(2,1)S(1)}, bf16[768,256]{1,0:T(8,128)(2,1)S(1)}, bf16[256,3072]{1,0:T(8,128)(2,1)S(1)}) custom-call(s32[1]{0:T(128)} %bitcast.which_ref, bf16[768,3072]{1,0:T(8,128)(2,1)S(1)} %copy-done.3, bf16[768,3072]{1,0:T(8,128)(2,1)S(1)} %copy-done.1, bf16[128,3072]{1,0:T(8,128)(2,1)S(1)} %collective-permute-done.refs_0_, ...), custom_call_target="tpu_custom_call" | custom-call | flops 362387872 | tf_op jit(solution)/shard_map/project/pallas_call | solution.py:118
  32.1 0.4 collective-permute-start.5
  32.5 7.0 %collective-permute-done.5 = bf16[768,128]{1,0:T(8,128)(2,1)S(1)} collective-permute-done((bf16[768,128]{1,0:T(8,128)(2,1)S(1)}, bf16[768,128]{1,0:T(8,128)(2,1)S(1)}, u32[]{:S(2)}, u32[]{:S(2)}) %collective-permute-start.5) | collective-permute-done | bytes 196640 | tf_op jit(solution)/shard_map/ppermute | solution.py:223
  39.5 1.1 %collective-permute-done.1.refs_0_ = bf16[128,3072]{1,0:T(8,128)(2,1)S(1)} collective-permute-done((bf16[128,3072]{1,0:T(8,128)(2,1)S(1)}, bf16[128,3072]{1,0:T(8,128)(2,1)S(1)}, u32[]{:S(2)}, u32[]{:S(2)}) %collective-permute-start.1) | collective-permute-done | bytes 786464 | tf_op jit(solution)/shard_map/ppermute | solution.py:229
  40.6 0.7 collective-permute-start.9
  41.3 1.3 %collective-permute-start.10 = (bf16[128,3072]{1,0:T(8,128)(2,1)S(1)}, bf16[128,3072]{1,0:T(8,128)(2,1)S(1)}, u32[]{:S(2)}, u32[]{:S(2)}) collective-permute-start(bf16[128,3072]{1,0:T(8,128)(2,1)S(1)} %collective-permute-done.3.refs_1_), channel_id=1, source_target_pairs={{0,4},{8,0},{16,8},{24,16},{28,24},{20,28},{12,20},{4,12},{1,5},{9... | collective-permute-start | bytes 2359304 | tf_op jit(solution)/shard_map/ppermute | solution.py:229
  42.6 2.6 %project.9 = (bf16[768,256]{1,0:T(8,128)(2,1)S(1)}, bf16[768,256]{1,0:T(8,128)(2,1)S(1)}, bf16[256,3072]{1,0:T(8,128)(2,1)S(1)}) custom-call(s32[1]{0:T(128)} %bitcast.which_ref, bf16[768,3072]{1,0:T(8,128)(2,1)S(1)} %copy-done.3, bf16[768,3072]{1,0:T(8,128)(2,1)S(1)} %copy-done.1, bf16[128,3072]{1,0:T(8,128)(2,1)S(1)} %collective-permute-done.1.refs_0_, ...), custom_call_target="tpu_custom_call" | custom-call | flops 362387872 | tf_op jit(solution)/shard_map/project/pallas_call | solution.py:118
  45.4 1.6 %collective-permute-start.12 = (bf16[768,256]{1,0:T(8,128)(2,1)S(1)}, bf16[768,256]{1,0:T(8,128)(2,1)S(1)}, u32[]{:S(2)}, u32[]{:S(2)}) collective-permute-start(bf16[768,256]{1,0:T(8,128)(2,1)S(1)} %get-tuple-element.79), channel_id=1, source_target_pairs={{0,2},{1,3},{2,0},{3,1},{4,6},{5,7},{6,4},{7,5},{8,10},{9,11},{10,... | collective-permute-start | bytes 1179656 | tf_op jit(solution)/shard_map/ppermute | solution.py:223
  47.0 1.1 %fusion = f32[384,1024]{1,0:T(8,128)S(1)} fusion(s32[1024]{0:T(1024)S(1)} %fusion.35, bf16[512,384]{1,0:T(8,128)(2,1)S(1)} %collective-permute-done.7, bf16[256,384]{1,0:T(8,128)(2,1)S(1)} %collective-permute-done.6, bf16[256,384]{1,0:T(8,128)(2,1)S(1)} %get-tuple-element.83), kind=kOutput, calls=%fused_computation.1 | convolution fusion | flops 808714240 | bytes 2363392 | tf_op jit(solution)/shard_map/dot_general | solution.py:18
  48.2 0.6 collective-permute-start.16
  48.8 8.6 %collective-permute-done.12 = bf16[768,256]{1,0:T(8,128)(2,1)S(1)} collective-permute-done((bf16[768,256]{1,0:T(8,128)(2,1)S(1)}, bf16[768,256]{1,0:T(8,128)(2,1)S(1)}, u32[]{:S(2)}, u32[]{:S(2)}) %collective-permute-start.12) | collective-permute-done | bytes 393248 | tf_op jit(solution)/shard_map/ppermute | solution.py:223
  57.4 1.3 %collective-permute-done.9.refs_0_ = bf16[128,3072]{1,0:T(8,128)(2,1)S(1)} collective-permute-done((bf16[128,3072]{1,0:T(8,128)(2,1)S(1)}, bf16[128,3072]{1,0:T(8,128)(2,1)S(1)}, u32[]{:S(2)}, u32[]{:S(2)}) %collective-permute-start.9) | collective-permute-done | bytes 786464 | tf_op jit(solution)/shard_map/ppermute | solution.py:229
  58.6 1.3 %collective-permute-done.10.refs_1_ = bf16[128,3072]{1,0:T(8,128)(2,1)S(1)} collective-permute-done((bf16[128,3072]{1,0:T(8,128)(2,1)S(1)}, bf16[128,3072]{1,0:T(8,128)(2,1)S(1)}, u32[]{:S(2)}, u32[]{:S(2)}) %collective-permute-start.10) | collective-permute-done | bytes 786464 | tf_op jit(solution)/shard_map/ppermute | solution.py:229
  60.0 0.5 collective-permute-start.14
  60.5 1.6 %collective-permute-start.13 = (bf16[64,3072]{1,0:T(8,128)(2,1)S(1)}, bf16[64,3072]{1,0:T(8,128)(2,1)S(1)}, u32[]{:S(2)}, u32[]{:S(2)}) collective-permute-start(bf16[64,3072]{1,0:T(8,128)(2,1)S(1)} %slice.71), channel_id=1, source_target_pairs={{0,8},{8,16},{16,24},{24,28},{28,20},{20,12},{12,4},{4,0},{1,9},{9... | collective-permute-start | bytes 1179656 | tf_op jit(solution)/shard_map/ppermute | solution.py:229
  62.1 1.4 %project.10 = (bf16[384,256]{1,0:T(8,128)(2,1)S(1)}, bf16[384,256]{1,0:T(8,128)(2,1)S(1)}, bf16[256,3072]{1,0:T(8,128)(2,1)S(1)}) custom-call(s32[1]{0:T(128)} %bitcast.which_ref, bf16[768,3072]{1,0:T(8,128)(2,1)S(1)} %copy-done.3, bf16[768,3072]{1,0:T(8,128)(2,1)S(1)} %copy-done.1, bf16[128,3072]{1,0:T(8,128)(2,1)S(1)} %collective-permute-done.9.refs_0_, ...), custom_call_target="tpu_custom_call" | custom-call | flops 181193936 | tf_op jit(solution)/shard_map/project/pallas_call | solution.py:118
  63.6 0.5 collective-permute-start.21
  64.2 1.4 %project.11.kept_ref = bf16[768,256]{1,0:T(8,128)(2,1)S(1)} custom-call(s32[1]{0:T(128)} %bitcast.which_ref, bf16[768,3072]{1,0:T(8,128)(2,1)S(1)} %copy-done.3, bf16[768,3072]{1,0:T(8,128)(2,1)S(1)} %copy-done.1, bf16[256,3072]{1,0:T(8,128)(2,1)S(1)} %get-tuple-element.52.refs_0_.refs_1_), custom_call_target="tpu_custom_call" | custom-call | flops 181193936 | tf_op jit(solution)/shard_map/project/pallas_call | solution.py:118
  65.6 0.2 collective-permute-start.8
  65.8 0.1 merge.1
  65.9 0.6 collective-permute-start.22
  66.5 2.9 %collective-permute-done.14.refs_1_ = bf16[64,3072]{1,0:T(8,128)(2,1)S(1)} collective-permute-done((bf16[64,3072]{1,0:T(8,128)(2,1)S(1)}, bf16[64,3072]{1,0:T(8,128)(2,1)S(1)}, u32[]{:S(2)}, u32[]{:S(2)}) %collective-permute-start.14) | collective-permute-done | bytes 393248 | tf_op jit(solution)/shard_map/ppermute | solution.py:229
  69.4 0.2 collective-permute-done.13.refs_0_
  69.7 1.4 %project.12 = (bf16[768,128]{1,0:T(8,128)(2,1)S(1)}, bf16[128,3072]{1,0:T(8,128)(2,1)S(1)}) custom-call(s32[1]{0:T(128)} %bitcast.which_ref, bf16[768,3072]{1,0:T(8,128)(2,1)S(1)} %copy-done.3, bf16[768,3072]{1,0:T(8,128)(2,1)S(1)} %copy-done.1, bf16[64,3072]{1,0:T(8,128)(2,1)S(1)} %collective-permute-done.13.refs_0_, ...), custom_call_target="tpu_custom_call" | custom-call | flops 181193936 | tf_op jit(solution)/shard_map/project/pallas_call | solution.py:118
  71.3 0.2 fusion.12
  71.5 0.6 collective-permute-start.18
  72.2 1.4 %project.13 = bf16[768,128]{1,0:T(8,128)(2,1)S(1)} custom-call(s32[1]{0:T(128)} %bitcast.which_ref, bf16[768,3072]{1,0:T(8,128)(2,1)S(1)} %copy-done.3, bf16[768,3072]{1,0:T(8,128)(2,1)S(1)} %copy-done.1, bf16[128,3072]{1,0:T(8,128)(2,1)S(1)} %get-tuple-element.63.refs_0_.refs_1_.refs_3_), custom_call_target="tpu_custom_call" | custom-call | flops 181193936 | tf_op jit(solution)/shard_map/project/pallas_call | solution.py:118
  73.6 1.1 %collective-permute-start.24 = (bf16[768,128]{1,0:T(8,128)(2,1)S(1)}, bf16[768,128]{1,0:T(8,128)(2,1)S(1)}, u32[]{:S(2)}, u32[]{:S(2)}) collective-permute-start(bf16[768,128]{1,0:T(8,128)(2,1)S(1)} %get-tuple-element.81), channel_id=1, source_target_pairs={{0,2},{1,3},{2,0},{3,1},{4,6},{5,7},{6,4},{7,5},{8,10},{9,11},{10,... | collective-permute-start | bytes 589832 | tf_op jit(solution)/shard_map/ppermute | solution.py:223
  74.7 3.8 %contract.4.base_ref = f32[768,3072]{1,0:T(8,128)S(1)} custom-call(s32[1]{0:T(128)} %bitcast.which_ref, bf16[768,3072]{1,0:T(8,128)(2,1)S(1)} %bitcast.12, bf16[384,128]{1,0:T(8,128)(2,1)S(1)} %fusion.27.refs_0_, bf16[384,128]{1,0:T(8,128)(2,1)S(1)} %collective-permute-done.8.refs_1_, bf16[128,3072]{1,0:T(8,128)(2,1)S(1)} %copy-done.5, ...), custom_call_target="tpu_custom_call" | custom-call | flops 452984832 | tf_op jit(solution)/shard_map/contract/pallas_call | solution.py:201
  78.8 0.5 collective-permute-start.23
  79.3 1.1 %contract.5.base_ref = f32[768,3072]{1,0:T(8,128)S(1)} custom-call(s32[1]{0:T(128)} %bitcast.which_ref, f32[768,3072]{1,0:T(8,128)S(1)} %contract.4.base_ref, bf16[384,256]{1,0:T(8,128)(2,1)S(1)} %fusion.7.refs_0_, bf16[256,3072]{1,0:T(8,128)(2,1)S(1)} %get-tuple-element.52.refs_0_.refs_1_), custom_call_target="tpu_custom_call", output_to_operand_aliasing={{}: (1, {})} | custom-call | flops 181193936 | tf_op jit(solution)/shard_map/contract/pallas_call | solution.py:201
  80.4 1.3 %collective-permute-done.24 = bf16[768,128]{1,0:T(8,128)(2,1)S(1)} collective-permute-done((bf16[768,128]{1,0:T(8,128)(2,1)S(1)}, bf16[768,128]{1,0:T(8,128)(2,1)S(1)}, u32[]{:S(2)}, u32[]{:S(2)}) %collective-permute-start.24) | collective-permute-done | bytes 196640 | tf_op jit(solution)/shard_map/ppermute | solution.py:223
  81.8 2.5 %contract.6.refs_4_ = f32[768,3072]{1,0:T(8,128)} custom-call(s32[1]{0:T(128)} %bitcast.which_ref, f32[768,3072]{1,0:T(8,128)S(1)} %contract.5.base_ref, bf16[384,128]{1,0:T(8,128)(2,1)S(1)} %fusion.22.refs_0_, bf16[128,3072]{1,0:T(8,128)(2,1)S(1)} %get-tuple-element.63.refs_0_.refs_1_.refs_3_), custom_call_target="tpu_custom_call" | custom-call | flops 90596968 | tf_op jit(solution)/shard_map/contract/pallas_call | solution.py:201
  84.3 2.6 %contract.7 = f32[768,3072]{1,0:T(8,128)} custom-call(s32[1]{0:T(128)} %bitcast.which_ref, f32[768,3072]{1,0:T(8,128)S(1)} %contract.5.base_ref, bf16[384,256]{1,0:T(8,128)(2,1)S(1)} %collective-permute-done.23.refs_0_, bf16[256,3072]{1,0:T(8,128)(2,1)S(1)} %get-tuple-element.52.refs_0_.refs_1_, ...), custom_call_target="tpu_custom_call", output_to_operand_aliasing={{}: (6, {})} | custom-call | flops 271790912 | tf_op jit(solution)/shard_map/contract/pallas_call | solution.py:201
  (64 shorter events, 2.0 us)
Async XLA Ops:
  0.0 20.8 %collective-permute-start.2 = (bf16[128,3072]{1,0:T(8,128)(2,1)}, bf16[128,3072]{1,0:T(8,128)(2,1)S(1)}, u32[]{:S(2)}, u32[]{:S(2)}) collective-permute-start(bf16[128,3072]{1,0:T(8,128)(2,1)} %refs_2_.1), channel_id=1, source_target_pairs={{0,4},{8,0},{16,8},{24,16},{28,24},{20,28},{12,20},{4,12},{1,5},{9... | collective-permute-start | bytes 2359304 | tf_op jit(solution)/shard_map/ppermute | solution.py:229
  2.9 19.5 %collective-permute-start = (bf16[128,3072]{1,0:T(8,128)(2,1)}, bf16[128,3072]{1,0:T(8,128)(2,1)S(1)}, u32[]{:S(2)}, u32[]{:S(2)}) collective-permute-start(bf16[128,3072]{1,0:T(8,128)(2,1)} %refs_2_.1), channel_id=1, source_target_pairs={{0,8},{8,16},{16,24},{24,28},{28,20},{20,12},{12,4},{4,0},{1,9},{9... | collective-permute-start | bytes 2359304 | tf_op jit(solution)/shard_map/ppermute | solution.py:229
  4.1 18.7 %collective-permute-start.6 = (bf16[256,384]{1,0:T(8,128)(2,1)S(1)}, bf16[256,384]{1,0:T(8,128)(2,1)S(1)}, u32[]{:S(2)}, u32[]{:S(2)}) collective-permute-start(bf16[256,384]{1,0:T(8,128)(2,1)S(1)} %get-tuple-element.84), channel_id=1, source_target_pairs={{0,1},{1,0},{2,3},{3,2},{4,5},{5,4},{6,7},{7,6},{8,9},{9,8},{10,11... | collective-permute-start | bytes 589832 | tf_op jit(solution)/shard_map/ppermute | solution.py:223
  4.2 2.3 %copy-start = (bf16[768,3072]{1,0:T(8,128)(2,1)S(1)}, bf16[768,3072]{1,0:T(8,128)(2,1)}, u32[]{:S(2)}) copy-start(bf16[768,3072]{1,0:T(8,128)(2,1)} %base_ref.1) | copy-start | bytes 14155780
  6.5 2.3 %copy-start.2 = (bf16[768,3072]{1,0:T(8,128)(2,1)S(1)}, bf16[768,3072]{1,0:T(8,128)(2,1)}, u32[]{:S(2)}) copy-start(bf16[768,3072]{1,0:T(8,128)(2,1)} %w_ref.13) | copy-start | bytes 14155780
  8.8 1.1 %copy-start.4 = (bf16[128,3072]{1,0:T(8,128)(2,1)S(1)}, bf16[128,3072]{1,0:T(8,128)(2,1)}, u32[]{:S(2)}) copy-start(bf16[128,3072]{1,0:T(8,128)(2,1)} %refs_2_.1) | copy-start | bytes 2359300
  10.0 4.0 %copy-start.6 = (s32[4]{0:T(128)S(1)}, s32[4]{0:T(128)}, u32[]{:S(2)}) copy-start(s32[4]{0:T(128)} %param.11) | copy-start | bytes 52
  10.0 4.1 %copy-start.7 = (f32[4]{0:T(128)S(1)}, f32[4]{0:T(128)}, u32[]{:S(2)}) copy-start(f32[4]{0:T(128)} %param.12) | copy-start | bytes 52
  12.6 19.4 %collective-permute-start.4 = (bf16[768,128]{1,0:T(8,128)(2,1)S(1)}, bf16[768,128]{1,0:T(8,128)(2,1)S(1)}, u32[]{:S(2)}, u32[]{:S(2)}) collective-permute-start(bf16[768,128]{1,0:T(8,128)(2,1)S(1)} %get-tuple-element.42), channel_id=1, source_target_pairs={{0,1},{1,0},{2,3},{3,2},{4,5},{5,4},{6,7},{7,6},{8,9},{9,8},{10,11... | collective-permute-start | bytes 589832 | tf_op jit(solution)/shard_map/ppermute | solution.py:223
  20.8 18.7 %collective-permute-start.3 = (bf16[128,3072]{1,0:T(8,128)(2,1)S(1)}, bf16[128,3072]{1,0:T(8,128)(2,1)S(1)}, u32[]{:S(2)}, u32[]{:S(2)}) collective-permute-start(bf16[128,3072]{1,0:T(8,128)(2,1)S(1)} %collective-permute-done.2.refs_1_), channel_id=1, source_target_pairs={{0,4},{8,0},{16,8},{24,16},{28,24},{20,28},{12,20},{4,12},{1,5},{9... | collective-permute-start | bytes 2359304 | tf_op jit(solution)/shard_map/ppermute | solution.py:229
  22.4 18.1 %collective-permute-start.1 = (bf16[128,3072]{1,0:T(8,128)(2,1)S(1)}, bf16[128,3072]{1,0:T(8,128)(2,1)S(1)}, u32[]{:S(2)}, u32[]{:S(2)}) collective-permute-start(bf16[128,3072]{1,0:T(8,128)(2,1)S(1)} %collective-permute-done.refs_0_), channel_id=1, source_target_pairs={{0,8},{8,16},{16,24},{24,28},{28,20},{20,12},{12,4},{4,0},{1,9},{9... | collective-permute-start | bytes 2359304 | tf_op jit(solution)/shard_map/ppermute | solution.py:229
  22.9 16.6 %collective-permute-start.7 = (bf16[512,384]{1,0:T(8,128)(2,1)S(1)}, bf16[512,384]{1,0:T(8,128)(2,1)S(1)}, u32[]{:S(2)}, u32[]{:S(2)}) collective-permute-start(bf16[512,384]{1,0:T(8,128)(2,1)S(1)} %pad_maximum_fusion), channel_id=1, source_target_pairs={{0,2},{1,3},{2,0},{3,1},{4,6},{5,7},{6,4},{7,5},{8,10},{9,11},{10,... | collective-permute-start | bytes 1179656 | tf_op jit(solution)/shard_map/ppermute | solution.py:223
  24.6 2.3 %copy-start.1 = (bf16[768,3072]{1,0:T(8,128)(2,1)S(1)}, bf16[768,3072]{1,0:T(8,128)(2,1)}, u32[]{:S(2)}) copy-start(bf16[768,3072]{1,0:T(8,128)(2,1)} %base_ref.1) | copy-start | bytes 14155780
  26.9 2.3 %copy-start.3 = (bf16[768,3072]{1,0:T(8,128)(2,1)S(1)}, bf16[768,3072]{1,0:T(8,128)(2,1)}, u32[]{:S(2)}) copy-start(bf16[768,3072]{1,0:T(8,128)(2,1)} %w_ref.13) | copy-start | bytes 14155780
  31.9 13.4 %collective-permute-start.11 = (bf16[768,256]{1,0:T(8,128)(2,1)S(1)}, bf16[768,256]{1,0:T(8,128)(2,1)S(1)}, u32[]{:S(2)}, u32[]{:S(2)}) collective-permute-start(bf16[768,256]{1,0:T(8,128)(2,1)S(1)} %get-tuple-element.49), channel_id=1, source_target_pairs={{0,1},{1,0},{2,3},{3,2},{4,5},{5,4},{6,7},{7,6},{8,9},{9,8},{10,11... | collective-permute-start | bytes 1179656 | tf_op jit(solution)/shard_map/ppermute | solution.py:223
  32.1 7.4 %collective-permute-start.5 = (bf16[768,128]{1,0:T(8,128)(2,1)S(1)}, bf16[768,128]{1,0:T(8,128)(2,1)S(1)}, u32[]{:S(2)}, u32[]{:S(2)}) collective-permute-start(bf16[768,128]{1,0:T(8,128)(2,1)S(1)} %get-tuple-element.85), channel_id=1, source_target_pairs={{0,2},{1,3},{2,0},{3,1},{4,6},{5,7},{6,4},{7,5},{8,10},{9,11},{10,... | collective-permute-start | bytes 589832 | tf_op jit(solution)/shard_map/ppermute | solution.py:223
  40.6 18.1 %collective-permute-start.9 = (bf16[128,3072]{1,0:T(8,128)(2,1)S(1)}, bf16[128,3072]{1,0:T(8,128)(2,1)S(1)}, u32[]{:S(2)}, u32[]{:S(2)}) collective-permute-start(bf16[128,3072]{1,0:T(8,128)(2,1)S(1)} %collective-permute-done.1.refs_0_), channel_id=1, source_target_pairs={{0,8},{8,16},{16,24},{24,28},{28,20},{20,12},{12,4},{4,0},{1,9},{9... | collective-permute-start | bytes 2359304 | tf_op jit(solution)/shard_map/ppermute | solution.py:229
  41.3 18.7 %collective-permute-start.10 = (bf16[128,3072]{1,0:T(8,128)(2,1)S(1)}, bf16[128,3072]{1,0:T(8,128)(2,1)S(1)}, u32[]{:S(2)}, u32[]{:S(2)}) collective-permute-start(bf16[128,3072]{1,0:T(8,128)(2,1)S(1)} %collective-permute-done.3.refs_1_), channel_id=1, source_target_pairs={{0,4},{8,0},{16,8},{24,16},{28,24},{20,28},{12,20},{4,12},{1,5},{9... | collective-permute-start | bytes 2359304 | tf_op jit(solution)/shard_map/ppermute | solution.py:229
  45.2 2.9 %collective-permute-start.15 = (bf16[768,256]{1,0:T(8,128)(2,1)S(1)}, bf16[768,256]{1,0:T(8,128)(2,1)S(1)}, u32[]{:S(2)}, u32[]{:S(2)}) collective-permute-start(bf16[768,256]{1,0:T(8,128)(2,1)S(1)} %get-tuple-element.53), channel_id=1, source_target_pairs={{0,1},{1,0},{2,3},{3,2},{4,5},{5,4},{6,7},{7,6},{8,9},{9,8},{10,11... | collective-permute-start | bytes 1179656 | tf_op jit(solution)/shard_map/ppermute | solution.py:223
  45.4 12.0 %collective-permute-start.12 = (bf16[768,256]{1,0:T(8,128)(2,1)S(1)}, bf16[768,256]{1,0:T(8,128)(2,1)S(1)}, u32[]{:S(2)}, u32[]{:S(2)}) collective-permute-start(bf16[768,256]{1,0:T(8,128)(2,1)S(1)} %get-tuple-element.79), channel_id=1, source_target_pairs={{0,2},{1,3},{2,0},{3,1},{4,6},{5,7},{6,4},{7,5},{8,10},{9,11},{10,... | collective-permute-start | bytes 1179656 | tf_op jit(solution)/shard_map/ppermute | solution.py:223
  48.2 18.3 %collective-permute-start.16 = (bf16[768,256]{1,0:T(8,128)(2,1)S(1)}, bf16[768,256]{1,0:T(8,128)(2,1)S(1)}, u32[]{:S(2)}, u32[]{:S(2)}) collective-permute-start(bf16[768,256]{1,0:T(8,128)(2,1)S(1)} %get-tuple-element.77), channel_id=1, source_target_pairs={{0,2},{1,3},{2,0},{3,1},{4,6},{5,7},{6,4},{7,5},{8,10},{9,11},{10,... | collective-permute-start | bytes 1179656 | tf_op jit(solution)/shard_map/ppermute | solution.py:223
  60.0 9.4 %collective-permute-start.14 = (bf16[64,3072]{1,0:T(8,128)(2,1)S(1)}, bf16[64,3072]{1,0:T(8,128)(2,1)S(1)}, u32[]{:S(2)}, u32[]{:S(2)}) collective-permute-start(bf16[64,3072]{1,0:T(8,128)(2,1)S(1)} %slice.72), channel_id=1, source_target_pairs={{0,4},{8,0},{16,8},{24,16},{28,24},{20,28},{12,20},{4,12},{1,5},{9... | collective-permute-start | bytes 1179656 | tf_op jit(solution)/shard_map/ppermute | solution.py:229
  60.5 9.1 %collective-permute-start.13 = (bf16[64,3072]{1,0:T(8,128)(2,1)S(1)}, bf16[64,3072]{1,0:T(8,128)(2,1)S(1)}, u32[]{:S(2)}, u32[]{:S(2)}) collective-permute-start(bf16[64,3072]{1,0:T(8,128)(2,1)S(1)} %slice.71), channel_id=1, source_target_pairs={{0,8},{8,16},{16,24},{24,28},{28,20},{20,12},{12,4},{4,0},{1,9},{9... | collective-permute-start | bytes 1179656 | tf_op jit(solution)/shard_map/ppermute | solution.py:229
  63.5 2.1 %collective-permute-start.20 = (bf16[384,256]{1,0:T(8,128)(2,1)S(1)}, bf16[384,256]{1,0:T(8,128)(2,1)S(1)}, u32[]{:S(2)}, u32[]{:S(2)}) collective-permute-start(bf16[384,256]{1,0:T(8,128)(2,1)S(1)} %get-tuple-element.66), channel_id=1, source_target_pairs={{0,1},{1,0},{2,3},{3,2},{4,5},{5,4},{6,7},{7,6},{8,9},{9,8},{10,11... | collective-permute-start | bytes 589832 | tf_op jit(solution)/shard_map/ppermute | solution.py:223
  63.6 2.1 %collective-permute-start.21 = (bf16[384,256]{1,0:T(8,128)(2,1)S(1)}, bf16[384,256]{1,0:T(8,128)(2,1)S(1)}, u32[]{:S(2)}, u32[]{:S(2)}) collective-permute-start(bf16[384,256]{1,0:T(8,128)(2,1)S(1)} %get-tuple-element.67), channel_id=1, source_target_pairs={{0,1},{1,0},{2,3},{3,2},{4,5},{5,4},{6,7},{7,6},{8,9},{9,8},{10,11... | collective-permute-start | bytes 589832 | tf_op jit(solution)/shard_map/ppermute | solution.py:223
  65.6 9.1 %collective-permute-start.8 = (bf16[384,128]{1,0:T(8,128)(2,1)S(1)}, bf16[384,128]{1,0:T(8,128)(2,1)S(1)}, u32[]{:S(2)}, u32[]{:S(2)}) collective-permute-start(bf16[384,128]{1,0:T(8,128)(2,1)S(1)} %fusion.27.refs_0_), channel_id=1, source_target_pairs={{0,1},{1,0},{2,3},{3,2},{4,5},{5,4},{6,7},{7,6},{8,9},{9,8},{10,11... | collective-permute-start | bytes 294920 | tf_op jit(solution)/shard_map/ppermute | solution.py:223
  65.9 12.7 %collective-permute-start.22 = (bf16[768,256]{1,0:T(8,128)(2,1)S(1)}, bf16[768,256]{1,0:T(8,128)(2,1)S(1)}, u32[]{:S(2)}, u32[]{:S(2)}) collective-permute-start(bf16[768,256]{1,0:T(8,128)(2,1)S(1)} %get-tuple-element.71), channel_id=1, source_target_pairs={{0,2},{1,3},{2,0},{3,1},{4,6},{5,7},{6,4},{7,5},{8,10},{9,11},{10,... | collective-permute-start | bytes 1179656 | tf_op jit(solution)/shard_map/ppermute | solution.py:223
  71.0 2.5 %collective-permute-start.19 = (bf16[768,128]{1,0:T(8,128)(2,1)S(1)}, bf16[768,128]{1,0:T(8,128)(2,1)S(1)}, u32[]{:S(2)}, u32[]{:S(2)}) collective-permute-start(bf16[768,128]{1,0:T(8,128)(2,1)S(1)} %get-tuple-element.64), channel_id=1, source_target_pairs={{0,1},{1,0},{2,3},{3,2},{4,5},{5,4},{6,7},{7,6},{8,9},{9,8},{10,11... | collective-permute-start | bytes 589832 | tf_op jit(solution)/shard_map/ppermute | solution.py:223
  71.5 3.2 %collective-permute-start.18 = (bf16[384,256]{1,0:T(8,128)(2,1)S(1)}, bf16[384,256]{1,0:T(8,128)(2,1)S(1)}, u32[]{:S(2)}, u32[]{:S(2)}) collective-permute-start(bf16[384,256]{1,0:T(8,128)(2,1)S(1)} %get-tuple-element.75.refs_6_), channel_id=1, source_target_pairs={{0,1},{1,0},{2,3},{3,2},{4,5},{5,4},{6,7},{7,6},{8,9},{9,8},{10,11... | collective-permute-start | bytes 589832 | tf_op jit(solution)/shard_map/ppermute | solution.py:223
  72.1 2.6 %collective-permute-start.17 = (bf16[384,256]{1,0:T(8,128)(2,1)S(1)}, bf16[384,256]{1,0:T(8,128)(2,1)S(1)}, u32[]{:S(2)}, u32[]{:S(2)}) collective-permute-start(bf16[384,256]{1,0:T(8,128)(2,1)S(1)} %get-tuple-element.76.refs_3_), channel_id=1, source_target_pairs={{0,1},{1,0},{2,3},{3,2},{4,5},{5,4},{6,7},{7,6},{8,9},{9,8},{10,11... | collective-permute-start | bytes 589832 | tf_op jit(solution)/shard_map/ppermute | solution.py:223
  72.2 2.5 %slice-start = ((s8[4718592]{0:T(1024)(128)(4,1)}), s8[4194304]{0:T(1024)(128)(4,1)S(1)}, s32[]{:S(2)}) async-start(s8[4718592]{0:T(1024)(128)(4,1)} %bitcast.11), calls=%async_computation | async-start | bytes 8388608
  72.2 2.5 %slice-start.1 = ((s8[4718592]{0:T(1024)(128)(4,1)}), s8[524288]{0:T(1024)(128)(4,1)S(1)}, s32[]{:S(2)}) async-start(s8[4718592]{0:T(1024)(128)(4,1)} %bitcast.11), calls=%async_computation.1 | async-start | bytes 1048576
  72.2 2.6 %copy-start.5 = (bf16[128,3072]{1,0:T(8,128)(2,1)S(1)}, bf16[128,3072]{1,0:T(8,128)(2,1)}, u32[]{:S(2)}) copy-start(bf16[128,3072]{1,0:T(8,128)(2,1)} %refs_2_.1) | copy-start | bytes 2359300
  73.6 8.0 %collective-permute-start.24 = (bf16[768,128]{1,0:T(8,128)(2,1)S(1)}, bf16[768,128]{1,0:T(8,128)(2,1)S(1)}, u32[]{:S(2)}, u32[]{:S(2)}) collective-permute-start(bf16[768,128]{1,0:T(8,128)(2,1)S(1)} %get-tuple-element.81), channel_id=1, source_target_pairs={{0,2},{1,3},{2,0},{3,1},{4,6},{5,7},{6,4},{7,5},{8,10},{9,11},{10,... | collective-permute-start | bytes 589832 | tf_op jit(solution)/shard_map/ppermute | solution.py:223
  78.8 5.5 %collective-permute-start.23 = (bf16[384,256]{1,0:T(8,128)(2,1)S(1)}, bf16[384,256]{1,0:T(8,128)(2,1)S(1)}, u32[]{:S(2)}, u32[]{:S(2)}) collective-permute-start(bf16[384,256]{1,0:T(8,128)(2,1)S(1)} %fusion.7.refs_0_), channel_id=1, source_target_pairs={{0,1},{1,0},{2,3},{3,2},{4,5},{5,4},{6,7},{7,6},{8,9},{9,8},{10,11... | collective-permute-start | bytes 589832 | tf_op jit(solution)/shard_map/ppermute | solution.py:223
  81.7 2.6 %collective-permute-start.25 = (bf16[384,128]{1,0:T(8,128)(2,1)S(1)}, bf16[384,128]{1,0:T(8,128)(2,1)S(1)}, u32[]{:S(2)}, u32[]{:S(2)}) collective-permute-start(bf16[384,128]{1,0:T(8,128)(2,1)S(1)} %fusion.22.refs_0_), channel_id=1, source_target_pairs={{0,1},{1,0},{2,3},{3,2},{4,5},{5,4},{6,7},{7,6},{8,9},{9,8},{10,11... | collective-permute-start | bytes 294920 | tf_op jit(solution)/shard_map/ppermute | solution.py:223

commit v7 on v6

--- a/solution.py
+++ b/solution.py
@@ -283,8 +283,8 @@
     chip2 = add(kept2, swap(theirs2, CORE))
     across2 = over_rows(chip2)
     scaled0 = weigh(aligned, chip0, across0, 0)
+    hop4 = step((hop3[0][:half], hop3[1][half:]))
     *hop3, kept2, chip1, across1 = gate(*hop3, kept2, chip1, across1)
-    hop4 = step((hop3[0][:half], hop3[1][half:]))
     *theirs3, block3 = project(one, w_out, direction, hop3, ((1, (0,)), (1, (1,))))
     theirs3 = [swap(v, CORE) for v in theirs3]
     (kept3,) = project(one, w_out, direction, [block3], (KEEP,))

time: 87.4 us -> 87 us (level)
  waiting for transfers between devices: 30.3 us -> 29.1 us
  local copies, waits for them, and re-layouts: 11.7 us -> 12.7 us
    ppermute x18, waiting for transfers between devices: 16.9 us -> 7.56 us  [swap(): return lax.ppermute(value, 'mp', pairs)]
    ppermute x8, waiting for transfers between devices: 13.4 us -> 21.5 us  [step(): return (lax.ppermute(pair[0], 'dp', UP), lax.ppermute(pair[1], 'dp', DOWN))]
    unnamed x20, local copies, waits for them, and re-layouts: 10.5 us -> 11.5 us
  transfers between devices with their start and end apart: 26 -> 26, of which waited for: 10 -> 8; matrix products, arithmetic and copies ran while one was open for 5% -> 5% of each run, Pallas kernels for 24% -> 24%
where the time goes in v7:
time: 87 us; the launch traced here: 86.6 us
  waiting for transfers between devices  29.1 us (33%)
  Pallas kernels  23.5 us (27%)
  starting transfers between devices  17.7 us (20%)
  local copies, waits for them, and re-layouts  12.7 us (15%)
  other arithmetic  2.08 us (2%)
  matrix products  1.07 us (1%)
    ppermute x8, waiting for transfers between devices, step(): return (lax.ppermute(pair[0], 'dp', UP), lax.ppermute(pair[1], 'dp', DOWN))  21.5 us
    pallas_call x7, Pallas kernels, project(): pl.pallas_call(functools.partial(project_kernel, wanted, len(parts)), out...  13.4 us
    unnamed x20, local copies, waits for them, and re-layouts  11.5 us
    pallas_call x4, Pallas kernels, contract(): pl.pallas_call(functools.partial(contract_kernel, len(terms), step, tile,...  9.98 us
    ppermute x8, starting transfers between devices, step(): return (lax.ppermute(pair[0], 'dp', UP), lax.ppermute(pair[1], 'dp', DOWN))  9.39 us
    ppermute x18, starting transfers between devices, swap(): return lax.ppermute(value, 'mp', pairs)  8.28 us
    ppermute x18, waiting for transfers between devices, swap(): return lax.ppermute(value, 'mp', pairs)  7.56 us
  transfers between devices with their start and end apart: 26, of which 8 were waited for; matrix products, arithmetic and copies ran while one was open for 5% of the time, Pallas kernels for 24%

profile of v7, /device:TPU:0, one launch (start us, length us, event | category | flops | bytes accessed | tf_op | source)
XLA Modules:
  0.0 86.6 jit_solution(5063237895353923609)
XLA Ops:
  0.0 2.9 %collective-permute-start.2 = (bf16[128,3072]{1,0:T(8,128)(2,1)}, bf16[128,3072]{1,0:T(8,128)(2,1)S(1)}, u32[]{:S(2)}, u32[]{:S(2)}) collective-permute-start(bf16[128,3072]{1,0:T(8,128)(2,1)} %refs_2_.1), channel_id=1, source_target_pairs={{0,4},{8,0},{16,8},{24,16},{28,24},{20,28},{12,20},{4,12},{1,5},{9... | collective-permute-start | bytes 2359304 | tf_op jit(solution)/shard_map/ppermute | solution.py:229
  3.0 1.1 %constant_dynamic-slice_fusion = (bf16[256,384]{1,0:T(8,128)(2,1)S(1)}, bf16[256,384]{1,0:T(8,128)(2,1)S(1)}) fusion(bf16[256,768]{1,0:T(8,128)(2,1)} %param.10, s32[]{:T(128)S(6)} %select_n.103, s32[]{:T(128)S(6)} %select_n.104), kind=kLoop, calls=%fused_computation.91 | loop fusion | bytes 786440 | tf_op jit(solution)/shard_map/dynamic_slice | solution.py:232
  4.2 2.3 %copy-done = bf16[768,3072]{1,0:T(8,128)(2,1)S(1)} copy-done((bf16[768,3072]{1,0:T(8,128)(2,1)S(1)}, bf16[768,3072]{1,0:T(8,128)(2,1)}, u32[]{:S(2)}) %copy-start) | copy-done | bytes 4718616
  6.5 2.3 %copy-done.2 = bf16[768,3072]{1,0:T(8,128)(2,1)S(1)} copy-done((bf16[768,3072]{1,0:T(8,128)(2,1)S(1)}, bf16[768,3072]{1,0:T(8,128)(2,1)}, u32[]{:S(2)}) %copy-start.2) | copy-done | bytes 4718616
  8.9 1.1 %copy-done.4 = bf16[128,3072]{1,0:T(8,128)(2,1)S(1)} copy-done((bf16[128,3072]{1,0:T(8,128)(2,1)S(1)}, bf16[128,3072]{1,0:T(8,128)(2,1)}, u32[]{:S(2)}) %copy-start.4) | copy-done | bytes 786456
  10.0 2.6 %project.8 = (bf16[768,128]{1,0:T(8,128)(2,1)S(1)}, bf16[768,128]{1,0:T(8,128)(2,1)S(1)}) custom-call(s32[1]{0:T(128)} %bitcast.which_ref, bf16[768,3072]{1,0:T(8,128)(2,1)S(1)} %copy-done.2, bf16[768,3072]{1,0:T(8,128)(2,1)S(1)} %copy-done, bf16[128,3072]{1,0:T(8,128)(2,1)S(1)} %copy-done.4), custom_call_target="tpu_custom_call" | custom-call | flops 362387872 | tf_op jit(solution)/shard_map/project/pallas_call | solution.py:118
  12.6 0.6 collective-permute-start.4
  13.1 0.7 fusion.46
  14.2 6.6 %collective-permute-done.2.refs_1_ = bf16[128,3072]{1,0:T(8,128)(2,1)S(1)} collective-permute-done((bf16[128,3072]{1,0:T(8,128)(2,1)}, bf16[128,3072]{1,0:T(8,128)(2,1)S(1)}, u32[]{:S(2)}, u32[]{:S(2)}) %collective-permute-start.2) | collective-permute-done | bytes 786464 | tf_op jit(solution)/shard_map/ppermute | solution.py:229
  20.8 1.7 %collective-permute-start.3 = (bf16[128,3072]{1,0:T(8,128)(2,1)S(1)}, bf16[128,3072]{1,0:T(8,128)(2,1)S(1)}, u32[]{:S(2)}, u32[]{:S(2)}) collective-permute-start(bf16[128,3072]{1,0:T(8,128)(2,1)S(1)} %collective-permute-done.2.refs_1_), channel_id=1, source_target_pairs={{0,4},{8,0},{16,8},{24,16},{28,24},{20,28},{12,20},{4,12},{1,5},{9... | collective-permute-start | bytes 2359304 | tf_op jit(solution)/shard_map/ppermute | solution.py:229
  22.4 0.4 collective-permute-start.1
  22.9 1.8 %collective-permute-start.7 = (bf16[512,384]{1,0:T(8,128)(2,1)S(1)}, bf16[512,384]{1,0:T(8,128)(2,1)S(1)}, u32[]{:S(2)}, u32[]{:S(2)}) collective-permute-start(bf16[512,384]{1,0:T(8,128)(2,1)S(1)} %pad_maximum_fusion), channel_id=1, source_target_pairs={{0,2},{1,3},{2,0},{3,1},{4,6},{5,7},{6,4},{7,5},{8,10},{9,11},{10,... | collective-permute-start | bytes 1179656 | tf_op jit(solution)/shard_map/ppermute | solution.py:223
  24.6 2.3 %copy-done.1 = bf16[768,3072]{1,0:T(8,128)(2,1)S(1)} copy-done((bf16[768,3072]{1,0:T(8,128)(2,1)S(1)}, bf16[768,3072]{1,0:T(8,128)(2,1)}, u32[]{:S(2)}) %copy-start.1) | copy-done | bytes 4718616
  26.9 2.3 %copy-done.3 = bf16[768,3072]{1,0:T(8,128)(2,1)S(1)} copy-done((bf16[768,3072]{1,0:T(8,128)(2,1)S(1)}, bf16[768,3072]{1,0:T(8,128)(2,1)}, u32[]{:S(2)}) %copy-start.3) | copy-done | bytes 4718616
  29.3 2.6 %project.7 = (bf16[768,256]{1,0:T(8,128)(2,1)S(1)}, bf16[768,256]{1,0:T(8,128)(2,1)S(1)}, bf16[256,3072]{1,0:T(8,128)(2,1)S(1)}) custom-call(s32[1]{0:T(128)} %bitcast.which_ref, bf16[768,3072]{1,0:T(8,128)(2,1)S(1)} %copy-done.3, bf16[768,3072]{1,0:T(8,128)(2,1)S(1)} %copy-done.1, bf16[128,3072]{1,0:T(8,128)(2,1)S(1)} %collective-permute-done.refs_0_, ...), custom_call_target="tpu_custom_call" | custom-call | flops 362387872 | tf_op jit(solution)/shard_map/project/pallas_call | solution.py:118
  32.1 0.4 collective-permute-start.5
  32.5 7.0 %collective-permute-done.5 = bf16[768,128]{1,0:T(8,128)(2,1)S(1)} collective-permute-done((bf16[768,128]{1,0:T(8,128)(2,1)S(1)}, bf16[768,128]{1,0:T(8,128)(2,1)S(1)}, u32[]{:S(2)}, u32[]{:S(2)}) %collective-permute-start.5) | collective-permute-done | bytes 196640 | tf_op jit(solution)/shard_map/ppermute | solution.py:223
  39.5 1.1 %collective-permute-done.1.refs_0_ = bf16[128,3072]{1,0:T(8,128)(2,1)S(1)} collective-permute-done((bf16[128,3072]{1,0:T(8,128)(2,1)S(1)}, bf16[128,3072]{1,0:T(8,128)(2,1)S(1)}, u32[]{:S(2)}, u32[]{:S(2)}) %collective-permute-start.1) | collective-permute-done | bytes 786464 | tf_op jit(solution)/shard_map/ppermute | solution.py:229
  40.6 0.7 collective-permute-start.9
  41.3 1.3 %collective-permute-start.11 = (bf16[128,3072]{1,0:T(8,128)(2,1)S(1)}, bf16[128,3072]{1,0:T(8,128)(2,1)S(1)}, u32[]{:S(2)}, u32[]{:S(2)}) collective-permute-start(bf16[128,3072]{1,0:T(8,128)(2,1)S(1)} %collective-permute-done.3.refs_1_), channel_id=1, source_target_pairs={{0,4},{8,0},{16,8},{24,16},{28,24},{20,28},{12,20},{4,12},{1,5},{9... | collective-permute-start | bytes 2359304 | tf_op jit(solution)/shard_map/ppermute | solution.py:229
  42.6 2.6 %project.9 = (bf16[768,256]{1,0:T(8,128)(2,1)S(1)}, bf16[768,256]{1,0:T(8,128)(2,1)S(1)}, bf16[256,3072]{1,0:T(8,128)(2,1)S(1)}) custom-call(s32[1]{0:T(128)} %bitcast.which_ref, bf16[768,3072]{1,0:T(8,128)(2,1)S(1)} %copy-done.3, bf16[768,3072]{1,0:T(8,128)(2,1)S(1)} %copy-done.1, bf16[128,3072]{1,0:T(8,128)(2,1)S(1)} %collective-permute-done.1.refs_0_, ...), custom_call_target="tpu_custom_call" | custom-call | flops 362387872 | tf_op jit(solution)/shard_map/project/pallas_call | solution.py:118
  45.4 1.6 %collective-permute-start.14 = (bf16[768,256]{1,0:T(8,128)(2,1)S(1)}, bf16[768,256]{1,0:T(8,128)(2,1)S(1)}, u32[]{:S(2)}, u32[]{:S(2)}) collective-permute-start(bf16[768,256]{1,0:T(8,128)(2,1)S(1)} %get-tuple-element.79), channel_id=1, source_target_pairs={{0,2},{1,3},{2,0},{3,1},{4,6},{5,7},{6,4},{7,5},{8,10},{9,11},{10,... | collective-permute-start | bytes 1179656 | tf_op jit(solution)/shard_map/ppermute | solution.py:223
  47.0 1.1 %fusion = f32[384,1024]{1,0:T(8,128)S(1)} fusion(s32[1024]{0:T(1024)S(1)} %fusion.35, bf16[512,384]{1,0:T(8,128)(2,1)S(1)} %collective-permute-done.7, bf16[256,384]{1,0:T(8,128)(2,1)S(1)} %collective-permute-done.6, bf16[256,384]{1,0:T(8,128)(2,1)S(1)} %get-tuple-element.83), kind=kOutput, calls=%fused_computation.1 | convolution fusion | flops 808714240 | bytes 2363392 | tf_op jit(solution)/shard_map/dot_general | solution.py:18
  48.2 0.6 collective-permute-start.16
  48.8 9.9 %collective-permute-done.9.refs_0_ = bf16[128,3072]{1,0:T(8,128)(2,1)S(1)} collective-permute-done((bf16[128,3072]{1,0:T(8,128)(2,1)S(1)}, bf16[128,3072]{1,0:T(8,128)(2,1)S(1)}, u32[]{:S(2)}, u32[]{:S(2)}) %collective-permute-start.9) | collective-permute-done | bytes 786464 | tf_op jit(solution)/shard_map/ppermute | solution.py:229
  58.7 1.6 %collective-permute-start.10 = (bf16[64,3072]{1,0:T(8,128)(2,1)S(1)}, bf16[64,3072]{1,0:T(8,128)(2,1)S(1)}, u32[]{:S(2)}, u32[]{:S(2)}) collective-permute-start(bf16[64,3072]{1,0:T(8,128)(2,1)S(1)} %slice.93), channel_id=1, source_target_pairs={{0,8},{8,16},{16,24},{24,28},{28,20},{20,12},{12,4},{4,0},{1,9},{9... | collective-permute-start | bytes 1179656 | tf_op jit(solution)/shard_map/ppermute | solution.py:229
  60.3 0.7 collective-permute-start.12
  61.1 1.4 %project.10 = (bf16[384,256]{1,0:T(8,128)(2,1)S(1)}, bf16[384,256]{1,0:T(8,128)(2,1)S(1)}, bf16[256,3072]{1,0:T(8,128)(2,1)S(1)}) custom-call(s32[1]{0:T(128)} %bitcast.which_ref, bf16[768,3072]{1,0:T(8,128)(2,1)S(1)} %copy-done.3, bf16[768,3072]{1,0:T(8,128)(2,1)S(1)} %copy-done.1, bf16[128,3072]{1,0:T(8,128)(2,1)S(1)} %collective-permute-done.9.refs_0_, ...), custom_call_target="tpu_custom_call" | custom-call | flops 181193936 | tf_op jit(solution)/shard_map/project/pallas_call | solution.py:118
  62.6 0.5 collective-permute-start.21
  63.1 1.4 %project.11.kept_ref = bf16[768,256]{1,0:T(8,128)(2,1)S(1)} custom-call(s32[1]{0:T(128)} %bitcast.which_ref, bf16[768,3072]{1,0:T(8,128)(2,1)S(1)} %copy-done.3, bf16[768,3072]{1,0:T(8,128)(2,1)S(1)} %copy-done.1, bf16[256,3072]{1,0:T(8,128)(2,1)S(1)} %get-tuple-element.52.refs_0_.refs_1_), custom_call_target="tpu_custom_call" | custom-call | flops 181193936 | tf_op jit(solution)/shard_map/project/pallas_call | solution.py:118
  64.6 0.2 collective-permute-start.8
  64.7 0.1 merge.1
  64.8 1.1 %collective-permute-start.22 = (bf16[768,256]{1,0:T(8,128)(2,1)S(1)}, bf16[768,256]{1,0:T(8,128)(2,1)S(1)}, u32[]{:S(2)}, u32[]{:S(2)}) collective-permute-start(bf16[768,256]{1,0:T(8,128)(2,1)S(1)} %get-tuple-element.71), channel_id=1, source_target_pairs={{0,2},{1,3},{2,0},{3,1},{4,6},{5,7},{6,4},{7,5},{8,10},{9,11},{10,... | collective-permute-start | bytes 1179656 | tf_op jit(solution)/shard_map/ppermute | solution.py:223
  66.0 1.5 %collective-permute-done.10.refs_0_ = bf16[64,3072]{1,0:T(8,128)(2,1)S(1)} collective-permute-done((bf16[64,3072]{1,0:T(8,128)(2,1)S(1)}, bf16[64,3072]{1,0:T(8,128)(2,1)S(1)}, u32[]{:S(2)}, u32[]{:S(2)}) %collective-permute-start.10) | collective-permute-done | bytes 393248 | tf_op jit(solution)/shard_map/ppermute | solution.py:229
  67.5 2.5 %collective-permute-done.12.refs_1_ = bf16[64,3072]{1,0:T(8,128)(2,1)S(1)} collective-permute-done((bf16[64,3072]{1,0:T(8,128)(2,1)S(1)}, bf16[64,3072]{1,0:T(8,128)(2,1)S(1)}, u32[]{:S(2)}, u32[]{:S(2)}) %collective-permute-start.12) | collective-permute-done | bytes 393248 | tf_op jit(solution)/shard_map/ppermute | solution.py:229
  69.9 1.4 %project.12 = (bf16[768,128]{1,0:T(8,128)(2,1)S(1)}, bf16[128,3072]{1,0:T(8,128)(2,1)S(1)}) custom-call(s32[1]{0:T(128)} %bitcast.which_ref, bf16[768,3072]{1,0:T(8,128)(2,1)S(1)} %copy-done.3, bf16[768,3072]{1,0:T(8,128)(2,1)S(1)} %copy-done.1, bf16[64,3072]{1,0:T(8,128)(2,1)S(1)} %collective-permute-done.10.refs_0_, ...), custom_call_target="tpu_custom_call" | custom-call | flops 181193936 | tf_op jit(solution)/shard_map/project/pallas_call | solution.py:118
  71.5 0.2 fusion.12
  71.8 0.6 collective-permute-start.18
  72.4 1.4 %project.13 = bf16[768,128]{1,0:T(8,128)(2,1)S(1)} custom-call(s32[1]{0:T(128)} %bitcast.which_ref, bf16[768,3072]{1,0:T(8,128)(2,1)S(1)} %copy-done.3, bf16[768,3072]{1,0:T(8,128)(2,1)S(1)} %copy-done.1, bf16[128,3072]{1,0:T(8,128)(2,1)S(1)} %get-tuple-element.63.refs_0_.refs_1_.refs_3_), custom_call_target="tpu_custom_call" | custom-call | flops 181193936 | tf_op jit(solution)/shard_map/project/pallas_call | solution.py:118
  74.0 0.6 slice-done
  74.6 0.1 slice-done.1
  74.7 0.2 copy-done.5
  75.0 3.8 %contract.4.base_ref = f32[768,3072]{1,0:T(8,128)S(1)} custom-call(s32[1]{0:T(128)} %bitcast.which_ref, bf16[768,3072]{1,0:T(8,128)(2,1)S(1)} %bitcast.12, bf16[384,128]{1,0:T(8,128)(2,1)S(1)} %fusion.27.refs_0_, bf16[384,128]{1,0:T(8,128)(2,1)S(1)} %collective-permute-done.8.refs_1_, bf16[128,3072]{1,0:T(8,128)(2,1)S(1)} %copy-done.5, ...), custom_call_target="tpu_custom_call" | custom-call | flops 452984832 | tf_op jit(solution)/shard_map/contract/pallas_call | solution.py:201
  79.0 0.5 collective-permute-start.23
  79.5 1.1 %contract.5.base_ref = f32[768,3072]{1,0:T(8,128)S(1)} custom-call(s32[1]{0:T(128)} %bitcast.which_ref, f32[768,3072]{1,0:T(8,128)S(1)} %contract.4.base_ref, bf16[384,256]{1,0:T(8,128)(2,1)S(1)} %fusion.7.refs_0_, bf16[256,3072]{1,0:T(8,128)(2,1)S(1)} %get-tuple-element.52.refs_0_.refs_1_), custom_call_target="tpu_custom_call", output_to_operand_aliasing={{}: (1, {})} | custom-call | flops 181193936 | tf_op jit(solution)/shard_map/contract/pallas_call | solution.py:201
  80.6 0.6 collective-permute-done.24
  81.4 2.5 %contract.6.refs_4_ = f32[768,3072]{1,0:T(8,128)} custom-call(s32[1]{0:T(128)} %bitcast.which_ref, f32[768,3072]{1,0:T(8,128)S(1)} %contract.5.base_ref, bf16[384,128]{1,0:T(8,128)(2,1)S(1)} %fusion.22.refs_0_, bf16[128,3072]{1,0:T(8,128)(2,1)S(1)} %get-tuple-element.63.refs_0_.refs_1_.refs_3_), custom_call_target="tpu_custom_call" | custom-call | flops 90596968 | tf_op jit(solution)/shard_map/contract/pallas_call | solution.py:201
  83.9 2.6 %contract.7 = f32[768,3072]{1,0:T(8,128)} custom-call(s32[1]{0:T(128)} %bitcast.which_ref, f32[768,3072]{1,0:T(8,128)S(1)} %contract.5.base_ref, bf16[384,256]{1,0:T(8,128)(2,1)S(1)} %collective-permute-done.23.refs_0_, bf16[256,3072]{1,0:T(8,128)(2,1)S(1)} %get-tuple-element.52.refs_0_.refs_1_, ...), custom_call_target="tpu_custom_call", output_to_operand_aliasing={{}: (6, {})} | custom-call | flops 271790912 | tf_op jit(solution)/shard_map/contract/pallas_call | solution.py:201
  (64 shorter events, 2.1 us)
Async XLA Ops:
  0.0 20.8 %collective-permute-start.2 = (bf16[128,3072]{1,0:T(8,128)(2,1)}, bf16[128,3072]{1,0:T(8,128)(2,1)S(1)}, u32[]{:S(2)}, u32[]{:S(2)}) collective-permute-start(bf16[128,3072]{1,0:T(8,128)(2,1)} %refs_2_.1), channel_id=1, source_target_pairs={{0,4},{8,0},{16,8},{24,16},{28,24},{20,28},{12,20},{4,12},{1,5},{9... | collective-permute-start | bytes 2359304 | tf_op jit(solution)/shard_map/ppermute | solution.py:229
  2.9 19.5 %collective-permute-start = (bf16[128,3072]{1,0:T(8,128)(2,1)}, bf16[128,3072]{1,0:T(8,128)(2,1)S(1)}, u32[]{:S(2)}, u32[]{:S(2)}) collective-permute-start(bf16[128,3072]{1,0:T(8,128)(2,1)} %refs_2_.1), channel_id=1, source_target_pairs={{0,8},{8,16},{16,24},{24,28},{28,20},{20,12},{12,4},{4,0},{1,9},{9... | collective-permute-start | bytes 2359304 | tf_op jit(solution)/shard_map/ppermute | solution.py:229
  4.1 18.7 %collective-permute-start.6 = (bf16[256,384]{1,0:T(8,128)(2,1)S(1)}, bf16[256,384]{1,0:T(8,128)(2,1)S(1)}, u32[]{:S(2)}, u32[]{:S(2)}) collective-permute-start(bf16[256,384]{1,0:T(8,128)(2,1)S(1)} %get-tuple-element.84), channel_id=1, source_target_pairs={{0,1},{1,0},{2,3},{3,2},{4,5},{5,4},{6,7},{7,6},{8,9},{9,8},{10,11... | collective-permute-start | bytes 589832 | tf_op jit(solution)/shard_map/ppermute | solution.py:223
  4.2 2.3 %copy-start = (bf16[768,3072]{1,0:T(8,128)(2,1)S(1)}, bf16[768,3072]{1,0:T(8,128)(2,1)}, u32[]{:S(2)}) copy-start(bf16[768,3072]{1,0:T(8,128)(2,1)} %base_ref.1) | copy-start | bytes 14155780
  6.5 2.3 %copy-start.2 = (bf16[768,3072]{1,0:T(8,128)(2,1)S(1)}, bf16[768,3072]{1,0:T(8,128)(2,1)}, u32[]{:S(2)}) copy-start(bf16[768,3072]{1,0:T(8,128)(2,1)} %w_ref.13) | copy-start | bytes 14155780
  8.8 1.1 %copy-start.4 = (bf16[128,3072]{1,0:T(8,128)(2,1)S(1)}, bf16[128,3072]{1,0:T(8,128)(2,1)}, u32[]{:S(2)}) copy-start(bf16[128,3072]{1,0:T(8,128)(2,1)} %refs_2_.1) | copy-start | bytes 2359300
  10.0 4.0 %copy-start.6 = (s32[4]{0:T(128)S(1)}, s32[4]{0:T(128)}, u32[]{:S(2)}) copy-start(s32[4]{0:T(128)} %param.11) | copy-start | bytes 52
  10.0 4.1 %copy-start.7 = (f32[4]{0:T(128)S(1)}, f32[4]{0:T(128)}, u32[]{:S(2)}) copy-start(f32[4]{0:T(128)} %param.12) | copy-start | bytes 52
  12.6 19.4 %collective-permute-start.4 = (bf16[768,128]{1,0:T(8,128)(2,1)S(1)}, bf16[768,128]{1,0:T(8,128)(2,1)S(1)}, u32[]{:S(2)}, u32[]{:S(2)}) collective-permute-start(bf16[768,128]{1,0:T(8,128)(2,1)S(1)} %get-tuple-element.42), channel_id=1, source_target_pairs={{0,1},{1,0},{2,3},{3,2},{4,5},{5,4},{6,7},{7,6},{8,9},{9,8},{10,11... | collective-permute-start | bytes 589832 | tf_op jit(solution)/shard_map/ppermute | solution.py:223
  20.8 18.7 %collective-permute-start.3 = (bf16[128,3072]{1,0:T(8,128)(2,1)S(1)}, bf16[128,3072]{1,0:T(8,128)(2,1)S(1)}, u32[]{:S(2)}, u32[]{:S(2)}) collective-permute-start(bf16[128,3072]{1,0:T(8,128)(2,1)S(1)} %collective-permute-done.2.refs_1_), channel_id=1, source_target_pairs={{0,4},{8,0},{16,8},{24,16},{28,24},{20,28},{12,20},{4,12},{1,5},{9... | collective-permute-start | bytes 2359304 | tf_op jit(solution)/shard_map/ppermute | solution.py:229
  22.4 18.1 %collective-permute-start.1 = (bf16[128,3072]{1,0:T(8,128)(2,1)S(1)}, bf16[128,3072]{1,0:T(8,128)(2,1)S(1)}, u32[]{:S(2)}, u32[]{:S(2)}) collective-permute-start(bf16[128,3072]{1,0:T(8,128)(2,1)S(1)} %collective-permute-done.refs_0_), channel_id=1, source_target_pairs={{0,8},{8,16},{16,24},{24,28},{28,20},{20,12},{12,4},{4,0},{1,9},{9... | collective-permute-start | bytes 2359304 | tf_op jit(solution)/shard_map/ppermute | solution.py:229
  22.9 16.6 %collective-permute-start.7 = (bf16[512,384]{1,0:T(8,128)(2,1)S(1)}, bf16[512,384]{1,0:T(8,128)(2,1)S(1)}, u32[]{:S(2)}, u32[]{:S(2)}) collective-permute-start(bf16[512,384]{1,0:T(8,128)(2,1)S(1)} %pad_maximum_fusion), channel_id=1, source_target_pairs={{0,2},{1,3},{2,0},{3,1},{4,6},{5,7},{6,4},{7,5},{8,10},{9,11},{10,... | collective-permute-start | bytes 1179656 | tf_op jit(solution)/shard_map/ppermute | solution.py:223
  24.6 2.3 %copy-start.1 = (bf16[768,3072]{1,0:T(8,128)(2,1)S(1)}, bf16[768,3072]{1,0:T(8,128)(2,1)}, u32[]{:S(2)}) copy-start(bf16[768,3072]{1,0:T(8,128)(2,1)} %base_ref.1) | copy-start | bytes 14155780
  26.9 2.3 %copy-start.3 = (bf16[768,3072]{1,0:T(8,128)(2,1)S(1)}, bf16[768,3072]{1,0:T(8,128)(2,1)}, u32[]{:S(2)}) copy-start(bf16[768,3072]{1,0:T(8,128)(2,1)} %w_ref.13) | copy-start | bytes 14155780
  31.9 13.4 %collective-permute-start.13 = (bf16[768,256]{1,0:T(8,128)(2,1)S(1)}, bf16[768,256]{1,0:T(8,128)(2,1)S(1)}, u32[]{:S(2)}, u32[]{:S(2)}) collective-permute-start(bf16[768,256]{1,0:T(8,128)(2,1)S(1)} %get-tuple-element.49), channel_id=1, source_target_pairs={{0,1},{1,0},{2,3},{3,2},{4,5},{5,4},{6,7},{7,6},{8,9},{9,8},{10,11... | collective-permute-start | bytes 1179656 | tf_op jit(solution)/shard_map/ppermute | solution.py:223
  32.1 7.4 %collective-permute-start.5 = (bf16[768,128]{1,0:T(8,128)(2,1)S(1)}, bf16[768,128]{1,0:T(8,128)(2,1)S(1)}, u32[]{:S(2)}, u32[]{:S(2)}) collective-permute-start(bf16[768,128]{1,0:T(8,128)(2,1)S(1)} %get-tuple-element.85), channel_id=1, source_target_pairs={{0,2},{1,3},{2,0},{3,1},{4,6},{5,7},{6,4},{7,5},{8,10},{9,11},{10,... | collective-permute-start | bytes 589832 | tf_op jit(solution)/shard_map/ppermute | solution.py:223
  40.6 18.1 %collective-permute-start.9 = (bf16[128,3072]{1,0:T(8,128)(2,1)S(1)}, bf16[128,3072]{1,0:T(8,128)(2,1)S(1)}, u32[]{:S(2)}, u32[]{:S(2)}) collective-permute-start(bf16[128,3072]{1,0:T(8,128)(2,1)S(1)} %collective-permute-done.1.refs_0_), channel_id=1, source_target_pairs={{0,8},{8,16},{16,24},{24,28},{28,20},{20,12},{12,4},{4,0},{1,9},{9... | collective-permute-start | bytes 2359304 | tf_op jit(solution)/shard_map/ppermute | solution.py:229
  41.3 19.1 %collective-permute-start.11 = (bf16[128,3072]{1,0:T(8,128)(2,1)S(1)}, bf16[128,3072]{1,0:T(8,128)(2,1)S(1)}, u32[]{:S(2)}, u32[]{:S(2)}) collective-permute-start(bf16[128,3072]{1,0:T(8,128)(2,1)S(1)} %collective-permute-done.3.refs_1_), channel_id=1, source_target_pairs={{0,4},{8,0},{16,8},{24,16},{28,24},{20,28},{12,20},{4,12},{1,5},{9... | collective-permute-start | bytes 2359304 | tf_op jit(solution)/shard_map/ppermute | solution.py:229
  45.2 2.9 %collective-permute-start.15 = (bf16[768,256]{1,0:T(8,128)(2,1)S(1)}, bf16[768,256]{1,0:T(8,128)(2,1)S(1)}, u32[]{:S(2)}, u32[]{:S(2)}) collective-permute-start(bf16[768,256]{1,0:T(8,128)(2,1)S(1)} %get-tuple-element.53), channel_id=1, source_target_pairs={{0,1},{1,0},{2,3},{3,2},{4,5},{5,4},{6,7},{7,6},{8,9},{9,8},{10,11... | collective-permute-start | bytes 1179656 | tf_op jit(solution)/shard_map/ppermute | solution.py:223
  45.4 15.6 %collective-permute-start.14 = (bf16[768,256]{1,0:T(8,128)(2,1)S(1)}, bf16[768,256]{1,0:T(8,128)(2,1)S(1)}, u32[]{:S(2)}, u32[]{:S(2)}) collective-permute-start(bf16[768,256]{1,0:T(8,128)(2,1)S(1)} %get-tuple-element.79), channel_id=1, source_target_pairs={{0,2},{1,3},{2,0},{3,1},{4,6},{5,7},{6,4},{7,5},{8,10},{9,11},{10,... | collective-permute-start | bytes 1179656 | tf_op jit(solution)/shard_map/ppermute | solution.py:223
  48.2 17.8 %collective-permute-start.16 = (bf16[768,256]{1,0:T(8,128)(2,1)S(1)}, bf16[768,256]{1,0:T(8,128)(2,1)S(1)}, u32[]{:S(2)}, u32[]{:S(2)}) collective-permute-start(bf16[768,256]{1,0:T(8,128)(2,1)S(1)} %get-tuple-element.77), channel_id=1, source_target_pairs={{0,2},{1,3},{2,0},{3,1},{4,6},{5,7},{6,4},{7,5},{8,10},{9,11},{10,... | collective-permute-start | bytes 1179656 | tf_op jit(solution)/shard_map/ppermute | solution.py:223
  58.7 8.8 %collective-permute-start.10 = (bf16[64,3072]{1,0:T(8,128)(2,1)S(1)}, bf16[64,3072]{1,0:T(8,128)(2,1)S(1)}, u32[]{:S(2)}, u32[]{:S(2)}) collective-permute-start(bf16[64,3072]{1,0:T(8,128)(2,1)S(1)} %slice.93), channel_id=1, source_target_pairs={{0,8},{8,16},{16,24},{24,28},{28,20},{20,12},{12,4},{4,0},{1,9},{9... | collective-permute-start | bytes 1179656 | tf_op jit(solution)/shard_map/ppermute | solution.py:229
  60.3 9.6 %collective-permute-start.12 = (bf16[64,3072]{1,0:T(8,128)(2,1)S(1)}, bf16[64,3072]{1,0:T(8,128)(2,1)S(1)}, u32[]{:S(2)}, u32[]{:S(2)}) collective-permute-start(bf16[64,3072]{1,0:T(8,128)(2,1)S(1)} %slice.94), channel_id=1, source_target_pairs={{0,4},{8,0},{16,8},{24,16},{28,24},{20,28},{12,20},{4,12},{1,5},{9... | collective-permute-start | bytes 1179656 | tf_op jit(solution)/shard_map/ppermute | solution.py:229
  62.5 2.1 %collective-permute-start.20 = (bf16[384,256]{1,0:T(8,128)(2,1)S(1)}, bf16[384,256]{1,0:T(8,128)(2,1)S(1)}, u32[]{:S(2)}, u32[]{:S(2)}) collective-permute-start(bf16[384,256]{1,0:T(8,128)(2,1)S(1)} %get-tuple-element.66), channel_id=1, source_target_pairs={{0,1},{1,0},{2,3},{3,2},{4,5},{5,4},{6,7},{7,6},{8,9},{9,8},{10,11... | collective-permute-start | bytes 589832 | tf_op jit(solution)/shard_map/ppermute | solution.py:223
  62.6 2.1 %collective-permute-start.21 = (bf16[384,256]{1,0:T(8,128)(2,1)S(1)}, bf16[384,256]{1,0:T(8,128)(2,1)S(1)}, u32[]{:S(2)}, u32[]{:S(2)}) collective-permute-start(bf16[384,256]{1,0:T(8,128)(2,1)S(1)} %get-tuple-element.67), channel_id=1, source_target_pairs={{0,1},{1,0},{2,3},{3,2},{4,5},{5,4},{6,7},{7,6},{8,9},{9,8},{10,11... | collective-permute-start | bytes 589832 | tf_op jit(solution)/shard_map/ppermute | solution.py:223
  64.6 9.4 %collective-permute-start.8 = (bf16[384,128]{1,0:T(8,128)(2,1)S(1)}, bf16[384,128]{1,0:T(8,128)(2,1)S(1)}, u32[]{:S(2)}, u32[]{:S(2)}) collective-permute-start(bf16[384,128]{1,0:T(8,128)(2,1)S(1)} %fusion.27.refs_0_), channel_id=1, source_target_pairs={{0,1},{1,0},{2,3},{3,2},{4,5},{5,4},{6,7},{7,6},{8,9},{9,8},{10,11... | collective-permute-start | bytes 294920 | tf_op jit(solution)/shard_map/ppermute | solution.py:223
  64.8 14.0 %collective-permute-start.22 = (bf16[768,256]{1,0:T(8,128)(2,1)S(1)}, bf16[768,256]{1,0:T(8,128)(2,1)S(1)}, u32[]{:S(2)}, u32[]{:S(2)}) collective-permute-start(bf16[768,256]{1,0:T(8,128)(2,1)S(1)} %get-tuple-element.71), channel_id=1, source_target_pairs={{0,2},{1,3},{2,0},{3,1},{4,6},{5,7},{6,4},{7,5},{8,10},{9,11},{10,... | collective-permute-start | bytes 1179656 | tf_op jit(solution)/shard_map/ppermute | solution.py:223
  71.3 2.5 %collective-permute-start.19 = (bf16[768,128]{1,0:T(8,128)(2,1)S(1)}, bf16[768,128]{1,0:T(8,128)(2,1)S(1)}, u32[]{:S(2)}, u32[]{:S(2)}) collective-permute-start(bf16[768,128]{1,0:T(8,128)(2,1)S(1)} %get-tuple-element.64), channel_id=1, source_target_pairs={{0,1},{1,0},{2,3},{3,2},{4,5},{5,4},{6,7},{7,6},{8,9},{9,8},{10,11... | collective-permute-start | bytes 589832 | tf_op jit(solution)/shard_map/ppermute | solution.py:223
  71.8 2.2 %collective-permute-start.18 = (bf16[384,256]{1,0:T(8,128)(2,1)S(1)}, bf16[384,256]{1,0:T(8,128)(2,1)S(1)}, u32[]{:S(2)}, u32[]{:S(2)}) collective-permute-start(bf16[384,256]{1,0:T(8,128)(2,1)S(1)} %get-tuple-element.75.refs_6_), channel_id=1, source_target_pairs={{0,1},{1,0},{2,3},{3,2},{4,5},{5,4},{6,7},{7,6},{8,9},{9,8},{10,11... | collective-permute-start | bytes 589832 | tf_op jit(solution)/shard_map/ppermute | solution.py:223
  72.4 1.6 %collective-permute-start.17 = (bf16[384,256]{1,0:T(8,128)(2,1)S(1)}, bf16[384,256]{1,0:T(8,128)(2,1)S(1)}, u32[]{:S(2)}, u32[]{:S(2)}) collective-permute-start(bf16[384,256]{1,0:T(8,128)(2,1)S(1)} %get-tuple-element.76.refs_3_), channel_id=1, source_target_pairs={{0,1},{1,0},{2,3},{3,2},{4,5},{5,4},{6,7},{7,6},{8,9},{9,8},{10,11... | collective-permute-start | bytes 589832 | tf_op jit(solution)/shard_map/ppermute | solution.py:223
  72.4 2.2 %slice-start = ((s8[4718592]{0:T(1024)(128)(4,1)}), s8[4194304]{0:T(1024)(128)(4,1)S(1)}, s32[]{:S(2)}) async-start(s8[4718592]{0:T(1024)(128)(4,1)} %bitcast.11), calls=%async_computation | async-start | bytes 8388608
  72.4 2.3 %slice-start.1 = ((s8[4718592]{0:T(1024)(128)(4,1)}), s8[524288]{0:T(1024)(128)(4,1)S(1)}, s32[]{:S(2)}) async-start(s8[4718592]{0:T(1024)(128)(4,1)} %bitcast.11), calls=%async_computation.1 | async-start | bytes 1048576
  72.4 2.5 %copy-start.5 = (bf16[128,3072]{1,0:T(8,128)(2,1)S(1)}, bf16[128,3072]{1,0:T(8,128)(2,1)}, u32[]{:S(2)}) copy-start(bf16[128,3072]{1,0:T(8,128)(2,1)} %refs_2_.1) | copy-start | bytes 2359300
  73.9 7.3 %collective-permute-start.24 = (bf16[768,128]{1,0:T(8,128)(2,1)S(1)}, bf16[768,128]{1,0:T(8,128)(2,1)S(1)}, u32[]{:S(2)}, u32[]{:S(2)}) collective-permute-start(bf16[768,128]{1,0:T(8,128)(2,1)S(1)} %get-tuple-element.81), channel_id=1, source_target_pairs={{0,2},{1,3},{2,0},{3,1},{4,6},{5,7},{6,4},{7,5},{8,10},{9,11},{10,... | collective-permute-start | bytes 589832 | tf_op jit(solution)/shard_map/ppermute | solution.py:223
  79.0 4.8 %collective-permute-start.23 = (bf16[384,256]{1,0:T(8,128)(2,1)S(1)}, bf16[384,256]{1,0:T(8,128)(2,1)S(1)}, u32[]{:S(2)}, u32[]{:S(2)}) collective-permute-start(bf16[384,256]{1,0:T(8,128)(2,1)S(1)} %fusion.7.refs_0_), channel_id=1, source_target_pairs={{0,1},{1,0},{2,3},{3,2},{4,5},{5,4},{6,7},{7,6},{8,9},{9,8},{10,11... | collective-permute-start | bytes 589832 | tf_op jit(solution)/shard_map/ppermute | solution.py:223
  81.3 2.6 %collective-permute-start.25 = (bf16[384,128]{1,0:T(8,128)(2,1)S(1)}, bf16[384,128]{1,0:T(8,128)(2,1)S(1)}, u32[]{:S(2)}, u32[]{:S(2)}) collective-permute-start(bf16[384,128]{1,0:T(8,128)(2,1)S(1)} %fusion.22.refs_0_), channel_id=1, source_target_pairs={{0,1},{1,0},{2,3},{3,2},{4,5},{5,4},{6,7},{7,6},{8,9},{9,8},{10,11... | collective-permute-start | bytes 294920 | tf_op jit(solution)/shard_map/ppermute | solution.py:223
